TPU v7x, 512 devices: a whole 4x4x16 slice. The times are simulated.
512 devices in a mesh: section: 32 (over z, core), seq: 16 (over x, y).
Axes of the slice: x: 4, y: 4, z: 16, core: 2. Of those that a mesh axis runs over, the one named last changes fastest.
Arguments:
- slices: bfloat16 [32, 2048, 1024], P('section', 'seq'), may hold values from -6 to 6
- new_slice: bfloat16 [2048, 1024], P('seq'), may hold values from -6 to 6
- w_qkv: bfloat16 [32, 1024, 3072], P('section', None, 'seq'), may hold values from -0.1875 to 0.1875
- w_gate: bfloat16 [32, 1024, 1024], P('section', None, 'seq'), may hold values from -0.1875 to 0.1875
- w_out: bfloat16 [32, 1024, 1024], P('section', 'seq'), may hold values from -0.1875 to 0.1875
- input_gain: float32 [32, 1024], P('section'), may hold values from 0.25 to 1.75
- output_gain: float32 [32, 1024], P('section'), may hold values from 0.25 to 1.75
- bucket_bias: bfloat16 [32, 16, 64], P('section'), may hold values from -6 to 6
- repeat_bias: float32 [32, 16], P('section'), may hold values from -6 to 6
- cache_kv: bfloat16 [32, 768, 16, 128], P('section', None, 'seq'), may hold values from -6 to 6
- slice_positions: int32 [32, 2, 2048], P('section'), may hold values from 0 to 2815
- slice_buckets: int32 [32, 2, 2048], P('section'), may hold values from 0 to 63
- slice_items: int32 [32, 2, 2048], P('section'), may hold values from 0 to 511
- cache_positions: int32 [32, 768], P('section'), may hold values from 0 to 2815
- cache_buckets: int32 [32, 768], P('section'), may hold values from 0 to 63
- cache_items: int32 [32, 768], P('section'), may hold values from 0 to 511
Outputs:
- section_out: bfloat16 [32, 2, 2048, 1024], P('section', None, 'seq')
All inputs are finite; a program needn't handle non-finite values.
Results may differ from a plain program's by a relative error of at most 0.009.
Values may be sent and summed in bfloat16 or wider, within the bound.
No kernel may reach another device: no remote copies, remote signals or barrier semaphores. Data moves between devices by JAX's collectives and lax.ppermute only.
A program may use at most 64 MiB of HBM per device.

v0:
```python
import jax
import jax.numpy as jnp
from jax import lax
from jax.sharding import PartitionSpec as P

D = 1024
H = 16
DH = 64
TICKS = 2


EPSILON = 1e-05


def from_behind(block, axis, distance):
    devices = range(lax.axis_size(axis))
    route = [(i - distance, i) for i in devices if i - distance in devices]
    return lax.ppermute(block, axis, route)


def norm_rows(values, gain):
    row_mean = jnp.mean(values, axis=-1, keepdims=True)
    variance = jnp.mean(values * values, axis=-1, keepdims=True) - row_mean * row_mean
    return (values - row_mean) * lax.rsqrt(variance + EPSILON) * gain


def attend(qkv, cached, table, repeat, positions, buckets, items, cache_pos, cache_bkt, cache_itm):
    slice_rows, heads, triple = qkv.shape
    head_size = triple // 3
    bucket_count = table.shape[1]
    keys = jnp.concatenate([cached[:, :, :head_size], qkv[:, :, head_size : 2 * head_size]], axis=0)
    values = jnp.concatenate([cached[:, :, head_size:], qkv[:, :, 2 * head_size :]], axis=0)
    key_pos = jnp.concatenate([cache_pos, positions])
    key_bkt = jnp.concatenate([cache_bkt, buckets])
    key_itm = jnp.concatenate([cache_itm, items])
    total_keys = keys.shape[0]
    levels = jnp.arange(bucket_count, dtype=jnp.int32)
    distance = jnp.abs(levels[:, None] - levels[None, :])
    lookup = (distance[:, :, None] == levels[None, None, :]).astype(jnp.float32)
    toeplitz = jnp.einsum("abc,hc->hab", lookup, table.astype(jnp.float32)).astype(jnp.bfloat16)
    key_onehot = (key_bkt[:, None] == levels[None, :]).astype(jnp.bfloat16)
    query_onehot = (buckets[:, None] == levels[None, :]).astype(jnp.bfloat16)
    query_bias = jnp.einsum(
        "sa,hab->shb", query_onehot, toeplitz, preferred_element_type=jnp.float32
    ).astype(jnp.bfloat16)
    query_ext = jnp.concatenate([qkv[:, :, :head_size], query_bias], axis=2)
    key_ext = jnp.concatenate([keys, key_onehot[:, None, :]], axis=2)
    block = min(512, slice_rows)
    count = slice_rows // block

    def one_block(inputs):
        query_block, pos_block, item_block = inputs
        scores = jnp.einsum(
            "qhd,khd->hqk", query_block, key_ext, preferred_element_type=jnp.float32
        )
        same_item = item_block[:, None] == key_itm[None, :]
        scores = scores + jnp.where(same_item[None], repeat[:, None, None], 0.0)
        allowed = key_pos[None, :] <= pos_block[:, None]
        weights = jnp.where(allowed[None], jax.nn.silu(scores) / total_keys, 0.0).astype(
            jnp.bfloat16
        )
        return jnp.einsum(
            "hqk,khd->qhd", weights, values, preferred_element_type=jnp.float32
        ).astype(jnp.bfloat16)

    outputs = lax.map(
        one_block,
        (
            query_ext.reshape(count, block, heads, -1),
            positions.reshape(count, block),
            items.reshape(count, block),
        ),
    )
    return outputs.reshape(slice_rows, heads, head_size)


def body(
    slices,
    new_slice,
    w_qkv,
    w_gate,
    w_out,
    input_gain,
    output_gain,
    bucket_bias,
    repeat_bias,
    cache_kv,
    slice_positions,
    slice_buckets,
    slice_items,
    cache_positions,
    cache_buckets,
    cache_items,
):
    seq_count = lax.axis_size("seq")
    heads_here = H // seq_count
    first_head = lax.axis_index("seq") * heads_here
    out_full = lax.all_gather(w_out[0], "seq", axis=0, tiled=True)
    table_here = lax.dynamic_slice_in_dim(bucket_bias[0], first_head, heads_here, 0)
    repeat_here = lax.dynamic_slice_in_dim(repeat_bias[0], first_head, heads_here, 0)
    gain_in = input_gain[0]
    gain_out = output_gain[0]
    cached = cache_kv[0]
    qkv_full, gate_full = (
        lax.all_gather(w_qkv[0], "seq", axis=1, tiled=True),
        lax.all_gather(w_gate[0], "seq", axis=1, tiled=True),
    )
    current = slices[0]
    outputs = []
    for tick_index in range(TICKS):
        resident = current.astype(jnp.float32)
        positions = slice_positions[0, tick_index]
        buckets = slice_buckets[0, tick_index]
        items = slice_items[0, tick_index]
        local_rows = current.shape[0]
        normed = norm_rows(resident, gain_in).astype(jnp.bfloat16)
        qkv = jax.nn.silu(jnp.dot(normed, qkv_full, preferred_element_type=jnp.float32)).astype(
            jnp.bfloat16
        )
        gate = jax.nn.silu(jnp.dot(normed, gate_full, preferred_element_type=jnp.float32))
        by_heads = lax.all_to_all(
            qkv.reshape(local_rows, H, 3 * DH), "seq", split_axis=1, concat_axis=0, tiled=True
        )
        attended = attend(
            by_heads,
            cached,
            table_here,
            repeat_here,
            positions,
            buckets,
            items,
            cache_positions[0],
            cache_buckets[0],
            cache_items[0],
        )
        back = lax.all_to_all(attended, "seq", split_axis=0, concat_axis=1, tiled=True).reshape(
            local_rows, D
        )
        mixed = (norm_rows(back.astype(jnp.float32), gain_out) * gate).astype(jnp.bfloat16)
        produced = (resident + jnp.dot(mixed, out_full, preferred_element_type=jnp.float32)).astype(
            jnp.bfloat16
        )
        outputs.append(produced)
        if tick_index + 1 < TICKS:
            shifted = from_behind(produced, "section", 1)
            current = jnp.where(lax.axis_index("section") == 0, new_slice, shifted)
    return jnp.stack(outputs, axis=0)[None]


def solution(mesh):
    in_specs = (
        P("section", "seq", None),
        P("seq", None),
        P("section", None, "seq"),
        P("section", None, "seq"),
        P("section", "seq", None),
        P("section", None),
        P("section", None),
        P("section", None, None),
        P("section", None),
        P("section", None, "seq", None),
        P("section", None, None),
        P("section", None, None),
        P("section", None, None),
        P("section", None),
        P("section", None),
        P("section", None),
    )
    out_specs = P("section", None, "seq", None)
    return jax.shard_map(body, mesh=mesh, in_specs=in_specs, out_specs=out_specs, check_vma=False)
```

profile of v0, /device:TPU:96, one launch (start us, length us, event | category | flops | bytes accessed | tf_op | source)
XLA Modules:
  0.0 323.7 jit_solution(3667685449797394219)
XLA Ops:
  6.6 0.7 all-gather.7.cloned.1.call-update
  7.3 0.7 all-gather.11.cloned.1.call-update
  8.1 0.7 all-gather.9.cloned.1.call-update
  8.8 1.1 convert_reduce_fusion.1
  9.8 1.1 fusion.74
  10.9 0.8 fusion.123
  11.8 1.1 fusion.122
  12.9 0.7 reduce.21
  13.6 0.7 reduce.19
  14.3 0.7 reduce.23
  15.0 1.2 fusion.44
  16.9 73.6 %all-gather.7.cloned.1.call-done = bf16[1,1024,3072]{1,2,0:T(8,128)(2,1)} async-done(((bf16[1,1024,192]{1,2,0:T(8,128)(2,1)}), bf16[1,1024,3072]{1,2,0:T(8,128)(2,1)}) %all-gather.7.cloned.1.call-update) | async-done | bytes 6291472 | tf_op jit(solution)/shard_map/all_gather | solution.py:105
  90.5 5.0 %multiply_convert_fusion.1 = bf16[128,3072]{1,0:T(8,128)(2,1)S(1)} fusion(bf16[1,1024,3072]{1,2,0:T(8,128)(2,1)} %all-gather.7.cloned.1.call-done, bf16[1,128,1024]{2,1,0:T(8,128)(2,1)S(1)} %copy-done.1, f32[1024]{0:T(1024)S(1)} %bitcast.222, f32[128]{0:T(128)S(1)} %get-tuple-element.253, f32[128]{0:T(128)S(1)} %get-tuple-element.252), kind=kOutput, calls=%fused_computation.47 | convolution fusion | flops 807927808 | bytes 7345152 | tf_op jit(solution)/shard_map/dot_general | solution.py:117
  95.6 1.2 copy.59
  96.7 5.8 %all-to-all-start = ((bf16[128,16,192]{0,2,1:T(8,128)(2,1)}), bf16[128,16,192]{0,2,1:T(8,128)(2,1)S(1)}, u32[]{:S(2)}, u32[]{:S(2)}) async-start(bf16[128,16,192]{0,2,1:T(8,128)(2,1)} %bitcast.24), calls=%async_computation | async-start | bytes 1572864 | tf_op jit(solution)/shard_map/all_to_all | solution.py:121
  102.9 0.6 constant_dynamic-slice_fusion.4
  103.8 13.2 %all-to-all-done = bf16[128,16,192]{0,2,1:T(8,128)(2,1)S(1)} async-done(((bf16[128,16,192]{0,2,1:T(8,128)(2,1)}), bf16[128,16,192]{0,2,1:T(8,128)(2,1)S(1)}, u32[]{:S(2)}, u32[]{:S(2)}) %all-to-all-start) | async-done | bytes 786464 | tf_op jit(solution)/shard_map/all_to_all | solution.py:121
  117.2 1.1 copy.64
  119.5 13.9 %while.20 = (s32[]{:T(128)}, bf16[4,512,1,64]{1,3,2,0:T(8,128)(2,1)S(1)}, s32[2816]{0:T(1024)S(1)}, s32[4,512]{1,0:T(4,128)S(1)}, bf16[4,512,1,128]{3,1,2,0:T(8,...) while((s32[]{:T(128)}, ...), condition=%wide.region_3.4_spmd, body=%wide.region_2.3_spmd.sunk | while | flops 569540608 | bytes 1316465 | solution.py:66
  119.5 3.5 %fusion.137 = bf16[4,512,1,64]{1,3,2,0:T(8,128)(2,1)S(1)} fusion(bf16[4,512,1,64]{1,3,2,0:T(8,128)(2,1)S(1)} %get-tuple-element.402, s32[]{:T(128)} %get-tuple-element.401, f32[]{:T(128)} %bitcast.194, s32[2816]{0:T(1024)S(1)} %get-tuple-element.419, s32[2816]{0:T(1024)S(1)} %get-tuple-element.414, s32[512]{0:T(512)S(1)} %bitcast.210, ...), kind=kOutput, calls=%fused_computation.4.clone.1 | convolution fusion | flops 569540608 | bytes 1308160 | tf_op jit(solution)/shard_map/while/body/eval_jaxpr/hqk,khd->qhd/dot_general | solution.py:62
  123.0 3.5 %fusion.137 = bf16[4,512,1,64]{1,3,2,0:T(8,128)(2,1)S(1)} fusion(bf16[4,512,1,64]{1,3,2,0:T(8,128)(2,1)S(1)} %get-tuple-element.402, s32[]{:T(128)} %get-tuple-element.401, f32[]{:T(128)} %bitcast.194, s32[2816]{0:T(1024)S(1)} %get-tuple-element.419, s32[2816]{0:T(1024)S(1)} %get-tuple-element.414, s32[512]{0:T(512)S(1)} %bitcast.210, ...), kind=kOutput, calls=%fused_computation.4.clone.1 | convolution fusion | flops 569540608 | bytes 1308160 | tf_op jit(solution)/shard_map/while/body/eval_jaxpr/hqk,khd->qhd/dot_general | solution.py:62
  126.5 3.5 %fusion.137 = bf16[4,512,1,64]{1,3,2,0:T(8,128)(2,1)S(1)} fusion(bf16[4,512,1,64]{1,3,2,0:T(8,128)(2,1)S(1)} %get-tuple-element.402, s32[]{:T(128)} %get-tuple-element.401, f32[]{:T(128)} %bitcast.194, s32[2816]{0:T(1024)S(1)} %get-tuple-element.419, s32[2816]{0:T(1024)S(1)} %get-tuple-element.414, s32[512]{0:T(512)S(1)} %bitcast.210, ...), kind=kOutput, calls=%fused_computation.4.clone.1 | convolution fusion | flops 569540608 | bytes 1308160 | tf_op jit(solution)/shard_map/while/body/eval_jaxpr/hqk,khd->qhd/dot_general | solution.py:62
  129.9 3.5 %fusion.137 = bf16[4,512,1,64]{1,3,2,0:T(8,128)(2,1)S(1)} fusion(bf16[4,512,1,64]{1,3,2,0:T(8,128)(2,1)S(1)} %get-tuple-element.402, s32[]{:T(128)} %get-tuple-element.401, f32[]{:T(128)} %bitcast.194, s32[2816]{0:T(1024)S(1)} %get-tuple-element.419, s32[2816]{0:T(1024)S(1)} %get-tuple-element.414, s32[512]{0:T(512)S(1)} %bitcast.210, ...), kind=kOutput, calls=%fused_computation.4.clone.1 | convolution fusion | flops 569540608 | bytes 1308160 | tf_op jit(solution)/shard_map/while/body/eval_jaxpr/hqk,khd->qhd/dot_general | solution.py:62
  134.5 11.6 %reduce.38 = bf16[2048,64]{1,0:T(8,128)(2,1)S(1)} reduce(bf16[2048,1,64]{2,1,0:T(2,128)(2,1)S(1)} %reshape.288, bf16[]{:T(256)} %broadcast.219), dimensions={1}, to_apply=%reshape.288.reduce_sub_computation | reduce | bytes 524290 | tf_op jit(solution)/shard_map/reshape | solution.py:74
  146.5 11.8 %all_to_all.54 = bf16[16,2,4096]{2,1,0:T(2,128)(2,1)S(1)} all-to-all(bf16[16,2,4096]{2,1,0:T(2,128)(2,1)S(1)} %reshape.315), channel_id=1, replica_groups=mesh['section'=32,'seq'=16] {'seq'}, dimensions={0} | all-to-all | bytes 524288 | tf_op jit(solution)/shard_map/all_to_all | solution.py:136
  158.3 0.6 reshape.316
  158.9 0.7 copy.67
  160.0 15.3 %convert_reduce_fusion.3 = (f32[2048]{0:T(1024)S(1)}, f32[2048]{0:T(1024)S(1)}) fusion(bf16[2048,1,64]{2,1,0:T(2,128)(2,1)S(1)} %reshape.316), kind=kLoop, calls=%fused_computation.136 | loop fusion | flops 520192 | bytes 278528 | tf_op jit(solution)/shard_map/reduce_sum | solution.py:22
  175.3 42.1 %all-gather.9.cloned.1.call-done = bf16[1,1024,1024]{1,2,0:T(8,128)(2,1)} async-done(((bf16[1,1024,64]{1,2,0:T(8,128)(2,1)}), bf16[1,1024,1024]{1,2,0:T(8,128)(2,1)}) %all-gather.9.cloned.1.call-update) | async-done | bytes 2097168 | tf_op jit(solution)/shard_map/all_gather | solution.py:106
  217.4 3.5 %fusion.58 = bf16[128,1024]{1,0:T(8,128)(2,1)S(1)} fusion(bf16[1,1024,1024]{2,1,0:T(8,128)(2,1)} %all-gather.11.cloned.1.call-done, bf16[1,128,1024]{2,1,0:T(8,128)(2,1)S(1)} %copy-done.1, bf16[1,1024,1024]{1,2,0:T(8,128)(2,1)} %all-gather.9.cloned.1.call-done, f32[128,1024]{1,0:T(8,128)S(1)} %copy.69, f32[1024]{0:T(1024)S(1)} %bitcast.226, ...), kind=kOutput, calls=%fused_computation.51 | convolution fusion | flops 539099136 | bytes 5253120 | tf_op jit(solution)/shard_map/dot_general | solution.py:140
  220.9 1.9 collective-permute-start
  222.9 5.8 %collective-permute-done = bf16[128,1024]{1,0:T(8,128)(2,1)S(1)} collective-permute-done((bf16[128,1024]{1,0:T(8,128)(2,1)S(1)}, bf16[128,1024]{1,0:T(8,128)(2,1)S(1)}, u32[]{:S(2)}, u32[]{:S(2)}) %collective-permute-start) | collective-permute-done | bytes 262176 | tf_op jit(solution)/shard_map/ppermute | solution.py:18
  228.8 5.0 %multiply_convert_fusion = bf16[128,3072]{1,0:T(8,128)(2,1)S(1)} fusion(bf16[1,1024,3072]{1,2,0:T(8,128)(2,1)} %all-gather.7.cloned.1.call-done, bf16[128,1024]{1,0:T(8,128)(2,1)S(1)} %get-tuple-element.221, f32[128]{0:T(128)S(1)} %get-tuple-element.249, f32[128]{0:T(128)S(1)} %get-tuple-element.248, f32[1024]{0:T(1024)S(1)} %bitcast.224), kind=kOutput, calls=%fused_computation.46 | convolution fusion | flops 807927808 | bytes 7345152 | tf_op jit(solution)/shard_map/dot_general | solution.py:117
  233.9 1.2 copy.70
  235.0 5.2 %all-to-all-start.2 = ((bf16[128,16,192]{0,2,1:T(8,128)(2,1)}), bf16[128,16,192]{0,2,1:T(8,128)(2,1)S(1)}, u32[]{:S(2)}, u32[]{:S(2)}) async-start(bf16[128,16,192]{0,2,1:T(8,128)(2,1)} %bitcast.45), calls=%async_computation.2 | async-start | bytes 1572864 | tf_op jit(solution)/shard_map/all_to_all | solution.py:121
  240.9 14.4 %all-to-all-done.2 = bf16[128,16,192]{0,2,1:T(8,128)(2,1)S(1)} async-done(((bf16[128,16,192]{0,2,1:T(8,128)(2,1)}), bf16[128,16,192]{0,2,1:T(8,128)(2,1)S(1)}, u32[]{:S(2)}, u32[]{:S(2)}) %all-to-all-start.2) | async-done | bytes 786464 | tf_op jit(solution)/shard_map/all_to_all | solution.py:121
  257.0 13.9 %while.21 = (s32[]{:T(128)}, bf16[4,512,1,64]{1,3,2,0:T(8,128)(2,1)S(1)}, s32[2816]{0:T(1024)S(1)}, s32[4,512]{1,0:T(4,128)S(1)}, bf16[4,512,1,128]{3,1,2,0:T(8,...) while((s32[]{:T(128)}, ...), condition=%wide.region_11.12_spmd, body=%wide.region_10.11_spmd.sunk | while | flops 569540608 | bytes 1316465 | solution.py:66
  257.0 3.5 %fusion.141 = bf16[4,512,1,64]{1,3,2,0:T(8,128)(2,1)S(1)} fusion(bf16[4,512,1,64]{1,3,2,0:T(8,128)(2,1)S(1)} %get-tuple-element.435, s32[]{:T(128)} %get-tuple-element.434, f32[]{:T(128)} %bitcast.201, s32[2816]{0:T(1024)S(1)} %get-tuple-element.452, s32[2816]{0:T(1024)S(1)} %get-tuple-element.447, s32[512]{0:T(512)S(1)} %bitcast.212, ...), kind=kOutput, calls=%fused_computation.19.clone.1 | convolution fusion | flops 569540608 | bytes 1308160 | tf_op jit(solution)/shard_map/while/body/eval_jaxpr/hqk,khd->qhd/dot_general | solution.py:62
  260.5 3.4 %fusion.141 = bf16[4,512,1,64]{1,3,2,0:T(8,128)(2,1)S(1)} fusion(bf16[4,512,1,64]{1,3,2,0:T(8,128)(2,1)S(1)} %get-tuple-element.435, s32[]{:T(128)} %get-tuple-element.434, f32[]{:T(128)} %bitcast.201, s32[2816]{0:T(1024)S(1)} %get-tuple-element.452, s32[2816]{0:T(1024)S(1)} %get-tuple-element.447, s32[512]{0:T(512)S(1)} %bitcast.212, ...), kind=kOutput, calls=%fused_computation.19.clone.1 | convolution fusion | flops 569540608 | bytes 1308160 | tf_op jit(solution)/shard_map/while/body/eval_jaxpr/hqk,khd->qhd/dot_general | solution.py:62
  264.0 3.5 %fusion.141 = bf16[4,512,1,64]{1,3,2,0:T(8,128)(2,1)S(1)} fusion(bf16[4,512,1,64]{1,3,2,0:T(8,128)(2,1)S(1)} %get-tuple-element.435, s32[]{:T(128)} %get-tuple-element.434, f32[]{:T(128)} %bitcast.201, s32[2816]{0:T(1024)S(1)} %get-tuple-element.452, s32[2816]{0:T(1024)S(1)} %get-tuple-element.447, s32[512]{0:T(512)S(1)} %bitcast.212, ...), kind=kOutput, calls=%fused_computation.19.clone.1 | convolution fusion | flops 569540608 | bytes 1308160 | tf_op jit(solution)/shard_map/while/body/eval_jaxpr/hqk,khd->qhd/dot_general | solution.py:62
  267.5 3.4 %fusion.141 = bf16[4,512,1,64]{1,3,2,0:T(8,128)(2,1)S(1)} fusion(bf16[4,512,1,64]{1,3,2,0:T(8,128)(2,1)S(1)} %get-tuple-element.435, s32[]{:T(128)} %get-tuple-element.434, f32[]{:T(128)} %bitcast.201, s32[2816]{0:T(1024)S(1)} %get-tuple-element.452, s32[2816]{0:T(1024)S(1)} %get-tuple-element.447, s32[512]{0:T(512)S(1)} %bitcast.212, ...), kind=kOutput, calls=%fused_computation.19.clone.1 | convolution fusion | flops 569540608 | bytes 1308160 | tf_op jit(solution)/shard_map/while/body/eval_jaxpr/hqk,khd->qhd/dot_general | solution.py:62
  271.5 11.6 %reduce.39 = bf16[2048,64]{1,0:T(8,128)(2,1)S(1)} reduce(bf16[2048,1,64]{2,1,0:T(2,128)(2,1)S(1)} %reshape.289, bf16[]{:T(256)} %broadcast.219), dimensions={1}, to_apply=%reshape.289.reduce_sub_computation | reduce | bytes 524290 | tf_op jit(solution)/shard_map/reshape | solution.py:74
  283.5 12.1 %all_to_all.55 = bf16[16,2,4096]{2,1,0:T(2,128)(2,1)S(1)} all-to-all(bf16[16,2,4096]{2,1,0:T(2,128)(2,1)S(1)} %reshape.317), channel_id=1, replica_groups=mesh['section'=32,'seq'=16] {'seq'}, dimensions={0} | all-to-all | bytes 524288 | tf_op jit(solution)/shard_map/all_to_all | solution.py:136
  295.6 0.6 reshape.318
  296.2 15.3 %convert_reduce_fusion.2 = (f32[2048]{0:T(1024)S(1)}, f32[2048]{0:T(1024)S(1)}) fusion(bf16[2048,1,64]{2,1,0:T(2,128)(2,1)S(1)} %reshape.318), kind=kLoop, calls=%fused_computation.135 | loop fusion | flops 520192 | bytes 278528 | tf_op jit(solution)/shard_map/reduce_sum | solution.py:22
  311.4 0.7 copy.76
  312.6 3.5 %fusion.61 = bf16[1,128,1024]{2,1,0:T(8,128)(2,1)S(1)} fusion(bf16[1,1024,1024]{2,1,0:T(8,128)(2,1)} %all-gather.11.cloned.1.call-done, bf16[128,1024]{1,0:T(8,128)(2,1)S(1)} %get-tuple-element.221, bf16[1,1024,1024]{1,2,0:T(8,128)(2,1)} %all-gather.9.cloned.1.call-done, f32[128,1024]{1,0:T(8,128)S(1)} %copy.78, f32[128]{0:T(128)S(1)} %get-tuple-element.247, ...), kind=kOutput, calls=%fused_computation.52 | convolution fusion | flops 539099136 | bytes 5253120 | tf_op jit(solution)/shard_map/dot_general | solution.py:140
  316.0 0.8 maximum_bitcast_fusion
  (83 shorter events, 8.6 us)
Async XLA Ops:
  6.5 8.5 %copy-start = (bf16[1,16,64]{2,1,0:T(8,128)(2,1)S(1)}, bf16[1,16,64]{2,1,0:T(8,128)(2,1)}, u32[]{:S(2)}) copy-start(bf16[1,16,64]{2,1,0:T(8,128)(2,1)} %param.27) | copy-start | bytes 6148
  6.5 84.0 %copy-start.1 = (bf16[1,128,1024]{2,1,0:T(8,128)(2,1)S(1)}, bf16[1,128,1024]{2,1,0:T(8,128)(2,1)}, u32[]{:S(2)}) copy-start(bf16[1,128,1024]{2,1,0:T(8,128)(2,1)} %param.20) | copy-start | bytes 786436
  6.5 10.3 %copy-start.5 = (s32[1,2,2048]{2,1,0:T(2,128)S(1)}, s32[1,2,2048]{2,1,0:T(2,128)}, u32[]{:S(2)}) copy-start(s32[1,2,2048]{2,1,0:T(2,128)} %param.30) | copy-start | bytes 49156
  6.5 10.3 %copy-start.4 = (s32[1,2,2048]{2,1,0:T(2,128)S(1)}, s32[1,2,2048]{2,1,0:T(2,128)}, u32[]{:S(2)}) copy-start(s32[1,2,2048]{2,1,0:T(2,128)} %param.32) | copy-start | bytes 49156
  6.5 84.0 %copy-start.6 = (f32[1,1024]{1,0:T(1,128)S(1)}, f32[1,1024]{1,0:T(1,128)}, u32[]{:S(2)}) copy-start(f32[1,1024]{1,0:T(1,128)} %param.25) | copy-start | bytes 12292
  6.5 84.0 %all-gather.7.cloned.1.call-start = ((), (), s32[]{:S(2)}) async-start(), calls=%async_computation.4 | async-start | bytes 6684672 | tf_op jit(solution)/shard_map/all_gather | solution.py:105
  7.3 168.0 %all-gather.11.cloned.1.call-start = ((), (), s32[]{:S(2)}) async-start(), calls=%async_computation.6 | async-start | bytes 2228224 | tf_op jit(solution)/shard_map/all_gather | solution.py:98
  8.0 209.4 %all-gather.9.cloned.1.call-start = ((), (), s32[]{:S(2)}) async-start(), calls=%async_computation.5 | async-start | bytes 2228224 | tf_op jit(solution)/shard_map/all_gather | solution.py:106
  95.6 7.3 %copy-start.8 = (f32[1,16]{1,0:T(1,128)S(1)}, f32[1,16]{1,0:T(1,128)}, u32[]{:S(2)}) copy-start(f32[1,16]{1,0:T(1,128)} %param.28) | copy-start | bytes 196
  96.7 20.2 %all-to-all-start = ((bf16[128,16,192]{0,2,1:T(8,128)(2,1)}), bf16[128,16,192]{0,2,1:T(8,128)(2,1)S(1)}, u32[]{:S(2)}, u32[]{:S(2)}) async-start(bf16[128,16,192]{0,2,1:T(8,128)(2,1)} %bitcast.24), calls=%async_computation | async-start | bytes 1572864 | tf_op jit(solution)/shard_map/all_to_all | solution.py:121
  118.3 1.1 copy-start.2
  158.3 59.1 %copy-start.7 = (f32[1,1024]{1,0:T(1,128)S(1)}, f32[1,1024]{1,0:T(1,128)}, u32[]{:S(2)}) copy-start(f32[1,1024]{1,0:T(1,128)} %param.26) | copy-start | bytes 12292
  217.4 11.2 %copy-start.3 = (bf16[128,1024]{1,0:T(8,128)(2,1)S(1)}, bf16[128,1024]{1,0:T(8,128)(2,1)}, u32[]{:S(2)}) copy-start(bf16[128,1024]{1,0:T(8,128)(2,1)} %param.21) | copy-start | bytes 786436
  220.9 7.7 %collective-permute-start = (bf16[128,1024]{1,0:T(8,128)(2,1)S(1)}, bf16[128,1024]{1,0:T(8,128)(2,1)S(1)}, u32[]{:S(2)}, u32[]{:S(2)}) collective-permute-start(bf16[128,1024]{1,0:T(8,128)(2,1)S(1)} %fusion.58), channel_id=1, source_target_pairs={{0,16},{16,32},{32,48},{48,64},{64,80},{80,96},{96,112},{112,128},... | collective-permute-start | bytes 786440 | tf_op jit(solution)/shard_map/ppermute | solution.py:18
  235.0 20.4 %all-to-all-start.2 = ((bf16[128,16,192]{0,2,1:T(8,128)(2,1)}), bf16[128,16,192]{0,2,1:T(8,128)(2,1)S(1)}, u32[]{:S(2)}, u32[]{:S(2)}) async-start(bf16[128,16,192]{0,2,1:T(8,128)(2,1)} %bitcast.45), calls=%async_computation.2 | async-start | bytes 1572864 | tf_op jit(solution)/shard_map/all_to_all | solution.py:121
Sparse Core Ops, SparseCore 0:
  10.4 80.0 all-gather.6
  93.5 60.7 all-gather.10
  157.4 59.9 all-gather.8
where the time goes:
time: 328 us; the launch traced here: 324 us
  waiting for transfers between devices  151 us (46%)
  other arithmetic  60 us (18%)
  matrix products  47 us (14%)
  blocking collectives  23.9 us (7%)
  local copies, waits for them, and re-layouts  14.7 us (4%)
  between operations  13.9 us (4%)
  starting transfers between devices  13 us (4%)
    all_gather x1, waiting for transfers between devices, body(): lax.all_gather(w_qkv[0], 'seq', axis=1, tiled=True)  73.6 us
    all_gather x1, waiting for transfers between devices, body(): lax.all_gather(w_gate[0], 'seq', axis=1, tiled=True)  42.1 us
    reduce_sum x6, other arithmetic, norm_rows(): row_mean = jnp.mean(values, axis=-1, keepdims=True)  31.8 us
    all_to_all x2, waiting for transfers between devices, body(): lax.all_to_all(qkv.reshape(local_rows, H, 3 * DH), 'seq', split_axis=1, c...  27.6 us
    dot_general x8, matrix products, one_block(): jnp.einsum('hqk,khd->qhd', weights, values, preferred_element_type=jnp.fl...  27.6 us
    all_to_all x2, blocking collectives, body(): lax.all_to_all(attended, 'seq', split_axis=0, concat_axis=1, tiled=True)  23.9 us
    reshape x2, other arithmetic, attend(): return outputs.reshape(slice_rows, heads, head_size)  23.1 us
    all_to_all x2, starting transfers between devices, body(): lax.all_to_all(qkv.reshape(local_rows, H, 3 * DH), 'seq', split_axis=1, c...  10.9 us
  transfers between devices with their start and end apart: 6, of which 5 were waited for; matrix products, arithmetic and copies ran while one was open for 19% of the time, Pallas kernels for 0%

commit v1 on v0

v1 whole, which is shorter than its diff:
```python
import jax
import jax.numpy as jnp
from jax import lax
from jax.experimental import pallas as pl
from jax.experimental.pallas import tpu as pltpu
from jax.sharding import Mesh, PartitionSpec as P

D = 1024
H = 16
DH = 64
NB = 64
TICKS = 2
CACHE = 768
SLICE = 2048
NK = CACHE + SLICE
EPSILON = 1e-05
NP = 2
NG = 8
ROWS = SLICE // (NP * NG)
BAND = SLICE // NP
KBLOCK = 256
BF16 = jnp.bfloat16
F32 = jnp.float32
VMEM_LIMIT = 60 * 1024 * 1024


def silu(v):
    half = 0.5 * v
    return half + half * jnp.tanh(half)


def vmem():
    return pl.BlockSpec(memory_space=pltpu.VMEM)


def smem():
    return pl.BlockSpec(memory_space=pltpu.SMEM)


def params():
    return pltpu.CompilerParams(vmem_limit_bytes=VMEM_LIMIT)


def low_lanes(rows):
    return lax.broadcasted_iota(jnp.int32, (rows, 2 * DH), 1) < DH


def project_kernel(p_ref, x_ref, own_ref, other_ref, gain_ref, qb_ref, lhs_ref, kv_ref, gate_ref, first):
    p = p_ref[0]
    values = x_ref[...].reshape(BAND, D).astype(F32)
    mean = jnp.mean(values, axis=-1, keepdims=True)
    variance = jnp.mean(values * values, axis=-1, keepdims=True) - mean * mean
    normed = ((values - mean) * lax.rsqrt(variance + EPSILON) * gain_ref[...]).astype(BF16)
    low = low_lanes(BAND)
    for index, w_ref in ((p, own_ref), (1 - p, other_ref)):
        z = silu(jnp.dot(normed, w_ref[...], preferred_element_type=F32))
        kv_ref[index] = z[:, 2 * DH :].astype(BF16)
        first[index] = z[:, : 2 * DH]
    for h in range(NP):
        lhs_ref[h] = jnp.where(low, 0.5 * first[h], qb_ref[h].astype(F32)).astype(BF16)
    gate_ref[...] = jnp.where(low, pltpu.roll(first[0], DH, 1), first[1]).astype(BF16)


def project(p, x, own, other, gain, qb):
    return pl.pallas_call(
        project_kernel,
        out_shape=(
            jax.ShapeDtypeStruct((NP, BAND, 2 * DH), BF16),
            jax.ShapeDtypeStruct((NP, BAND, 2 * DH), BF16),
            jax.ShapeDtypeStruct((BAND, 2 * DH), BF16),
        ),
        in_specs=[smem()] + [vmem()] * 5,
        out_specs=(vmem(), vmem(), vmem()),
        scratch_shapes=[pltpu.VMEM((NP, BAND, 2 * DH), F32)],
        compiler_params=params(),
        name="project",
    )(p, x, own, other, gain, qb)


def add_keys(rep_ref, lhs_ref, qpos_ref, qitm_ref, same, allowed, acc, kv_ref, ko_ref, kpos_ref, kitm_ref, fresh):
    count = kv_ref.shape[1]
    low = low_lanes(KBLOCK)
    for c in range(count // KBLOCK):
        ks = slice(c * KBLOCK, (c + 1) * KBLOCK)
        same[...] = jnp.where(qitm_ref[...] == kitm_ref[:, ks], 1.0, 0.0)
        allowed[...] = jnp.where(kpos_ref[:, ks] <= qpos_ref[...], 1.0, 0.0).astype(BF16)
        for h in range(NP):
            kv = kv_ref[h, ks, :]
            keys = jnp.where(low, kv, ko_ref[ks, :])
            half = lax.dot_general(lhs_ref[h], keys, (((1,), (1,)), ((), ())), preferred_element_type=F32)
            half = half + (0.5 * rep_ref[h]) * same[...]
            weight = (half + half * jnp.tanh(half)).astype(BF16) * allowed[...]
            part = jnp.dot(weight, kv, preferred_element_type=F32)
            if fresh and c == 0:
                acc[h] = part
            else:
                acc[h] += part


def early_kernel(rep_ref, lhs_ref, qpos_ref, qitm_ref, ckv_ref, cko_ref, cpos_ref, citm_ref, kv_ref, ko_ref, kpos_ref, kitm_ref, acc, same, allowed):
    shared = (rep_ref, lhs_ref, qpos_ref, qitm_ref, same, allowed, acc)
    add_keys(*shared, kv_ref, ko_ref, kpos_ref, kitm_ref, True)
    add_keys(*shared, ckv_ref, cko_ref, cpos_ref, citm_ref, False)


def late_kernel(rep_ref, lhs_ref, qpos_ref, qitm_ref, acc_ref, kv_ref, ko_ref, kpos_ref, kitm_ref, out_ref, acc, same, allowed):
    acc[...] = acc_ref[...]
    add_keys(rep_ref, lhs_ref, qpos_ref, qitm_ref, same, allowed, acc, kv_ref, ko_ref, kpos_ref, kitm_ref, False)
    out_ref[...] = (jnp.where(low_lanes(BAND), pltpu.roll(acc[0], DH, 1), acc[1]) * (1.0 / NK)).astype(BF16)


MASKS = [pltpu.VMEM((BAND, KBLOCK), F32), pltpu.VMEM((BAND, KBLOCK), BF16)]


def attend_early(*operands):
    return pl.pallas_call(
        early_kernel,
        out_shape=jax.ShapeDtypeStruct((NP, BAND, 2 * DH), F32),
        in_specs=[smem()] + [vmem()] * 11,
        out_specs=vmem(),
        scratch_shapes=MASKS,
        compiler_params=params(),
        name="attend_early",
    )(*operands)


def attend_late(*operands):
    return pl.pallas_call(
        late_kernel,
        out_shape=jax.ShapeDtypeStruct((BAND, 2 * DH), BF16),
        in_specs=[smem()] + [vmem()] * 8,
        out_specs=vmem(),
        scratch_shapes=[pltpu.VMEM((NP, BAND, 2 * DH), F32)] + MASKS,
        compiler_params=params(),
        name="attend_late",
    )(*operands)


def finish_kernel(r_ref, g_ref, x_ref, w_ref, gain_ref, out_ref, mixed):
    total = jnp.zeros((ROWS, 2 * DH), F32)
    square = jnp.zeros((ROWS, 2 * DH), F32)
    for k in range(NG):
        a = r_ref[k].astype(F32)
        total += a
        square += a * a
    mean = jnp.sum(total, axis=-1, keepdims=True) * (1.0 / D)
    variance = jnp.sum(square, axis=-1, keepdims=True) * (1.0 / D) - mean * mean
    scale = lax.rsqrt(variance + EPSILON)
    for k in range(NG):
        cols = slice(k * 2 * DH, (k + 1) * 2 * DH)
        a = r_ref[k].astype(F32)
        mixed[:, cols] = ((a - mean) * scale * gain_ref[:, cols] * g_ref[k].astype(F32)).astype(BF16)
    y = jnp.dot(mixed[...], w_ref[...], preferred_element_type=F32)
    out_ref[...] = (x_ref[...].astype(F32) + y).astype(BF16)


def finish(*operands):
    return pl.pallas_call(
        finish_kernel,
        out_shape=jax.ShapeDtypeStruct((ROWS, D), BF16),
        in_specs=[vmem()] * 5,
        out_specs=vmem(),
        scratch_shapes=[pltpu.VMEM((ROWS, D), BF16)],
        compiler_params=params(),
        name="finish",
    )(*operands)


def gather_g(x):
    return lax.all_to_all(jnp.broadcast_to(x[None], (NG,) + x.shape), "g", 0, 0)


def swap(x):
    return lax.ppermute(x, "p", [(0, 1), (1, 0)])


def body(
    slices,
    new_slice,
    w_qkv,
    w_gate,
    w_out,
    input_gain,
    output_gain,
    bucket_bias,
    repeat_bias,
    cache_kv,
    slice_positions,
    slice_buckets,
    slice_items,
    cache_positions,
    cache_buckets,
    cache_items,
):
    p = lax.axis_index("p")
    g = lax.axis_index("g")
    section = lax.axis_index("section")

    def both(own):
        other = swap(own)
        return jnp.stack([jnp.where(p == 0, own, other), jnp.where(p == 0, other, own)])

    w_own = jnp.concatenate([w_qkv[0, :, :DH], w_gate[0], w_qkv[0, :, DH:]], axis=1)
    w_other = swap(w_own)
    cached = both(cache_kv[0, :, 0, :])
    w_out_full = gather_g(both(w_out[0])).reshape(D, D)
    gain_out = output_gain[0].reshape(NP, NG, DH).transpose(1, 0, 2).reshape(1, D)
    tables = lax.dynamic_slice_in_dim(bucket_bias[0].reshape(NP, NG, NB), g, 1, 1)[:, 0]
    rep = lax.dynamic_slice_in_dim(repeat_bias[0].reshape(NP, NG), g, 1, 1)[:, 0]
    levels = jnp.arange(NB, dtype=jnp.int32)
    distance = jnp.abs(levels[:, None] - levels[None, :])
    lookup = (distance[:, :, None] == levels[None, None, :]).astype(F32)
    toeplitz = jnp.einsum("abc,hc->hab", lookup, tables.astype(F32)).astype(BF16)
    toeplitz = jnp.pad(0.5 * toeplitz, ((0, 0), (0, 0), (DH, 0)))
    lanes = jnp.arange(2 * DH, dtype=jnp.int32) - DH

    def key_side(bkt, pos, itm):
        return (bkt[:, None] == lanes[None, :]).astype(BF16), pos[None, :], itm[None, :]

    cache_side = key_side(cache_buckets[0], cache_positions[0], cache_items[0])
    p_word = p.astype(jnp.int32).reshape(1)

    current = slices[0]
    outputs = []
    for tick in range(TICKS):
        positions = slice_positions[0, tick].reshape(NP, BAND)
        buckets = slice_buckets[0, tick].reshape(NP, BAND)
        items = slice_items[0, tick].reshape(NP, BAND)

        def take(a, i):
            return lax.dynamic_index_in_dim(a, i, 0, keepdims=False)

        own_side = key_side(take(buckets, p), take(positions, p), take(items, p))
        other_side = key_side(take(buckets, 1 - p), take(positions, 1 - p), take(items, 1 - p))
        qpos = take(positions, p)[:, None]
        qitm = take(items, p)[:, None]
        query_onehot = (take(buckets, p)[:, None] == levels[None, :]).astype(BF16)
        query_bias = jnp.einsum("sa,hab->hsb", query_onehot, toeplitz, preferred_element_type=F32).astype(BF16)
        band = gather_g(current)
        lhs, kv, gate = project(p_word, band, w_own, w_other, input_gain, query_bias)
        kv_other = swap(kv)
        gates = lax.all_to_all(gate.reshape(NG, ROWS, 2 * DH), "g", 0, 0)
        acc = attend_early(rep, lhs, qpos, qitm, cached, *cache_side, kv, *own_side)
        a = attend_late(rep, lhs, qpos, qitm, acc, kv_other, *other_side)
        back = lax.all_to_all(a.reshape(NG, ROWS, 2 * DH), "g", 0, 0)
        produced = finish(back, gates, current, w_out_full, gain_out)
        outputs.append(produced)
        if tick + 1 < TICKS:
            count = lax.axis_size("section")
            shifted = lax.ppermute(produced, "section", [(s, s + 1) for s in range(count - 1)])
            current = jnp.where(section == 0, new_slice, shifted)
    return jnp.stack(outputs, axis=0)[None]


def solution(mesh):
    sections = mesh.shape["section"]
    grid = Mesh(mesh.devices.reshape(sections, NP, NG), ("section", "p", "g"))
    seq = ("p", "g")
    in_specs = (
        P("section", seq, None),
        P(seq, None),
        P("section", None, seq),
        P("section", None, seq),
        P("section", seq, None),
        P("section", None),
        P("section", None),
        P("section", None, None),
        P("section", None),
        P("section", None, seq, None),
        P("section", None, None),
        P("section", None, None),
        P("section", None, None),
        P("section", None),
        P("section", None),
        P("section", None),
    )
    out_specs = P("section", None, seq, None)
    return jax.shard_map(body, mesh=grid, in_specs=in_specs, out_specs=out_specs, check_vma=False)
```

time: 328 us -> 203 us (0.62)
  waiting for transfers between devices: 151 us -> 61.6 us
  other arithmetic: 60 us -> 9.03 us
  matrix products: 47 us -> 3.54 us
  Pallas kernels: 0 us -> 42.8 us
  starting transfers between devices: 13 us -> 50.5 us
  between operations: 13.9 us -> 0.38 us
  blocking collectives: 23.9 us -> 13.1 us
  local copies, waits for them, and re-layouts: 14.7 us -> 20.7 us
    all_gather x3 -> x0, waiting for transfers between devices: 116 us -> none  [the longest x1 73.6 us: body(): lax.all_gather(w_qkv[0], 'seq', axis=1, tiled=True)]
    dot_general x15 -> x3, matrix products: 47 us -> 3.54 us  [the longest x2 2.35 us: body(): jnp.einsum('sa,hab->hsb', query_onehot, toeplitz, preferred_element_type=...]
    pallas_call x0 -> x8, Pallas kernels: none -> 42.8 us  [the longest x2 15.4 us: attend_early(): pl.pallas_call(early_kernel, out_shape=jax.ShapeDtypeStruct((NP, BAND, 2...]
    reduce_sum x9 -> x0, other arithmetic: 32.9 us -> none  [the longest x6 31.8 us: norm_rows(): row_mean = jnp.mean(values, axis=-1, keepdims=True)]
    reshape x2 -> x0, other arithmetic: 23.1 us -> none  [attend(): return outputs.reshape(slice_rows, heads, head_size)]
    ppermute x1 -> x6, starting transfers between devices: 1.92 us -> 22.4 us  [the longest x5 20.5 us: swap(): return lax.ppermute(x, 'p', [(0, 1), (1, 0)])]
    all_to_all x2 -> x6, starting transfers between devices: 10.9 us -> 28.1 us  [the longest x3 14.5 us: gather_g(): return lax.all_to_all(jnp.broadcast_to(x[None], (NG,) + x.shape), 'g', 0, 0)]
    ppermute x1 -> x6, waiting for transfers between devices: 5.76 us -> 21.6 us  [the longest x5 15.7 us: swap(): return lax.ppermute(x, 'p', [(0, 1), (1, 0)])]
  transfers between devices with their start and end apart: 6 -> 12, of which waited for: 5 -> 5; matrix products, arithmetic and copies ran while one was open for 19% -> 12% of each run, Pallas kernels for 0% -> 16%
where the time goes in v1:
time: 203 us; the launch traced here: 202 us
  waiting for transfers between devices  61.6 us (30%)
  starting transfers between devices  50.5 us (25%)
  Pallas kernels  42.8 us (21%)
  local copies, waits for them, and re-layouts  20.7 us (10%)
  blocking collectives  13.1 us (6%)
  other arithmetic  9.03 us (4%)
  matrix products  3.54 us (2%)
    all_to_all x3, waiting for transfers between devices, gather_g(): return lax.all_to_all(jnp.broadcast_to(x[None], (NG,) + x.shape), 'g', 0, 0)  34.2 us
    ppermute x5, starting transfers between devices, swap(): return lax.ppermute(x, 'p', [(0, 1), (1, 0)])  20.5 us
    ppermute x5, waiting for transfers between devices, swap(): return lax.ppermute(x, 'p', [(0, 1), (1, 0)])  15.7 us
    pallas_call x2, Pallas kernels, attend_early(): pl.pallas_call(early_kernel, out_shape=jax.ShapeDtypeStruct((NP, BAND, 2...  15.4 us
    all_to_all x3, starting transfers between devices, gather_g(): return lax.all_to_all(jnp.broadcast_to(x[None], (NG,) + x.shape), 'g', 0, 0)  14.5 us
    all_to_all x1, blocking collectives, body(): back = lax.all_to_all(a.reshape(NG, ROWS, 2 * DH), 'g', 0, 0)  13.1 us
    pallas_call x2, Pallas kernels, attend_late(): pl.pallas_call(late_kernel, out_shape=jax.ShapeDtypeStruct((BAND, 2 * DH)...  11.1 us
    pallas_call x2, Pallas kernels, project(): pl.pallas_call(project_kernel, out_shape=(jax.ShapeDtypeStruct((NP, BAND,...  10.3 us
  transfers between devices with their start and end apart: 12, of which 5 were waited for; matrix products, arithmetic and copies ran while one was open for 12% of the time, Pallas kernels for 16%

profile of v1, /device:TPU:96, one launch (start us, length us, event | category | flops | bytes accessed | tf_op | source)
XLA Modules:
  0.0 201.7 jit_solution(5522906616894915790)
XLA Ops:
  0.0 2.6 %broadcast_in_dim.19 = bf16[8,128,1024]{2,1,0:T(8,128)(2,1)} broadcast(bf16[128,1024]{1,0:T(8,128)(2,1)} %bitcast.57), dimensions={1,2} | broadcast | bytes 2359296 | tf_op jit(solution)/shard_map/broadcast_in_dim | solution.py:170
  2.6 5.5 %all-to-all-start = ((bf16[8,128,1024]{2,1,0:T(8,128)(2,1)}), bf16[8,128,1024]{2,1,0:T(8,128)(2,1)S(1)}, u32[]{:S(2)}, u32[]{:S(2)}) async-start(bf16[8,128,1024]{2,1,0:T(8,128)(2,1)} %broadcast_in_dim.19), calls=%async_computation | async-start | bytes 4194304 | tf_op jit(solution)/shard_map/all_to_all | solution.py:170
  8.1 4.6 %collective-permute-start.3 = (bf16[64,1024]{1,0:T(8,128)(2,1)S(1)}, bf16[64,1024]{1,0:T(8,128)(2,1)}, u32[]{:S(2)}, u32[]{:S(2)}) collective-permute-start(bf16[64,1024]{1,0:T(8,128)(2,1)S(1)} %bitcast.69), channel_id=1, source_target_pairs={{0,8},{8,0},{1,9},{9,1},{2,10},{10,2},{3,11},{11,3},{4,12},{12,4},... | collective-permute-start | bytes 393224 | tf_op jit(solution)/shard_map/ppermute | solution.py:174
  13.6 2.7 %collective-permute-start = (bf16[1024,256]{1,0:T(8,128)(2,1)S(1)}, bf16[1024,256]{1,0:T(8,128)(2,1)S(1)}, u32[]{:S(2)}, u32[]{:S(2)}) collective-permute-start(bf16[1024,256]{1,0:T(8,128)(2,1)S(1)} %pad_maximum_fusion.own_ref), channel_id=1, source_target_pairs={{0,8},{8,0},{1,9},{9,1},{2,10},{10,2},{3,11},{11,3},{4,12},{12,4},... | collective-permute-start | bytes 1572872 | tf_op jit(solution)/shard_map/ppermute | solution.py:174
  16.3 4.6 %collective-permute-start.1 = (bf16[768,128]{1,0:T(8,128)(2,1)}, bf16[768,128]{1,0:T(8,128)(2,1)}, u32[]{:S(2)}, u32[]{:S(2)}) collective-permute-start(bf16[768,128]{1,0:T(8,128)(2,1)} %bitcast.68), channel_id=1, source_target_pairs={{0,8},{8,0},{1,9},{9,1},{2,10},{10,2},{3,11},{11,3},{4,12},{12,4},... | collective-permute-start | bytes 589832 | tf_op jit(solution)/shard_map/ppermute | solution.py:174
  21.0 0.8 slice_reduce_fusion.2
  22.4 15.6 %collective-permute-done.3 = bf16[64,1024]{1,0:T(8,128)(2,1)} collective-permute-done((bf16[64,1024]{1,0:T(8,128)(2,1)S(1)}, bf16[64,1024]{1,0:T(8,128)(2,1)}, u32[]{:S(2)}, u32[]{:S(2)}) %collective-permute-start.3) | collective-permute-done | bytes 131104 | tf_op jit(solution)/shard_map/ppermute | solution.py:174
  38.1 0.9 select_bitcast_fusion.3
  39.1 1.8 broadcast_in_dim.22
  41.1 5.2 %all-to-all-start.3 = ((bf16[8,2,64,1024]{3,2,1,0:T(8,128)(2,1)}), bf16[8,2,64,1024]{3,2,1,0:T(8,128)(2,1)S(1)}, u32[]{:S(2)}, u32[]{:S(2)}) async-start(bf16[8,2,64,1024]{3,2,1,0:T(8,128)(2,1)} %broadcast_in_dim.22), calls=%async_computation.3 | async-start | bytes 4194304 | tf_op jit(solution)/shard_map/all_to_all | solution.py:170
  47.7 1.2 fusion.4
  48.9 1.0 copy.34.qpos_ref
  49.9 1.0 copy.35.qitm_ref
  52.3 0.8 fusion.14.rep_ref
  53.1 1.2 fusion.1.qb_ref
  54.2 2.1 %compare_convert_fusion = (bf16[1024,128]{1,0:T(8,128)(2,1)}, bf16[1024,128]{1,0:T(8,128)(2,1)}, bf16[1024,128]{1,0:T(8,128)(2,1)}, bf16[1024,128]{1,0:T(8,128)(2,1)}) fusion(s32[128]{0:T(128)S(1)} %iota_add_fusion, s32[1024]{0:T(1024)S(1)} %bitcast.79, s32[1024]{0:T(1024)S(1)} %bitcast.80, s32[1024]{0:T(1024)S(1)} %bitcast.70, s32[1024]{0:T(1024)S(1)} %bitcast.75), kind=kLoop, calls=%fused_computation.11 | loop fusion | flops 1048576 | bytes 1065472 | tf_op jit(solution)/shard_map/convert_element_type | solution.py:218
  56.3 0.8 copy-done.6
  57.1 5.2 %project.2 = (bf16[2,1024,128]{2,1,0:T(8,128)(2,1)}, bf16[2,1024,128]{2,1,0:T(8,128)(2,1)}, bf16[1024,128]{1,0:T(8,128)(2,1)}) custom-call(s32[1]{0:T(128)} %bitcast.p_ref, bf16[8,128,1024]{2,1,0:T(8,128)(2,1)} %copy-done.2, bf16[1024,256]{1,0:T(8,128)(2,1)} %copy-done.4, bf16[1024,256]{1,0:T(8,128)(2,1)} %copy-done.6, f32[1,1024]{1,0:T(1,128)} %gain_ref.3, ...), custom_call_target="tpu_custom_call" | custom-call | tf_op jit(solution)/shard_map/project/pallas_call | solution.py:65
  62.3 3.9 %collective-permute-start.2 = (bf16[2,1024,128]{2,1,0:T(8,128)(2,1)}, bf16[2,1024,128]{2,1,0:T(8,128)(2,1)}, u32[]{:S(2)}, u32[]{:S(2)}) collective-permute-start(bf16[2,1024,128]{2,1,0:T(8,128)(2,1)} %get-tuple-element.12.kv_ref), channel_id=1, source_target_pairs={{0,8},{8,0},{1,9},{9,1},{2,10},{10,2},{3,11},{11,3},{4,12},{12,4},... | collective-permute-start | bytes 1572872 | tf_op jit(solution)/shard_map/ppermute | solution.py:174
  66.2 0.9 compare_convert_fusion.4.cko_ref
  67.1 8.3 %all-to-all-done.3 = bf16[8,2,64,1024]{3,2,1,0:T(8,128)(2,1)S(1)} async-done(((bf16[8,2,64,1024]{3,2,1,0:T(8,128)(2,1)}), bf16[8,2,64,1024]{3,2,1,0:T(8,128)(2,1)S(1)}, u32[]{:S(2)}, u32[]{:S(2)}) %all-to-all-start.3) | async-done | bytes 2097184 | tf_op jit(solution)/shard_map/all_to_all | solution.py:170
  75.4 4.3 %all-to-all-start.2 = ((bf16[8,128,128]{2,1,0:T(8,128)(2,1)}), bf16[8,128,128]{2,1,0:T(8,128)(2,1)S(1)}, u32[]{:S(2)}, u32[]{:S(2)}) async-start(bf16[8,128,128]{2,1,0:T(8,128)(2,1)} %bitcast.67), calls=%async_computation.2 | async-start | bytes 524288 | tf_op jit(solution)/shard_map/all_to_all | solution.py:242
  79.8 1.0 select_bitcast_fusion.1
  80.7 0.8 pad_maximum_fusion.1.ckv_ref
  81.5 7.7 %attend_early.2.acc_ref = f32[2,1024,128]{2,1,0:T(8,128)} custom-call(f32[2]{0:T(128)} %fusion.14.rep_ref, bf16[2,1024,128]{2,1,0:T(8,128)(2,1)} %get-tuple-element.11.lhs_ref, s32[1024,1]{1,0:T(8,128)} %copy.34.qpos_ref, s32[1024,1]{1,0:T(8,128)} %copy.35.qitm_ref, bf16[2,768,128]{2,1,0:T(8,128)(2,1)} %pad_maximum_fusion.1.ckv_ref, ...), custom_call_target="tpu_custom_call" | custom-call | tf_op jit(solution)/shard_map/attend_early/pallas_call | solution.py:116
  89.2 5.5 %attend_late.2 = bf16[1024,128]{1,0:T(8,128)(2,1)} custom-call(f32[2]{0:T(128)} %fusion.14.rep_ref, bf16[2,1024,128]{2,1,0:T(8,128)(2,1)} %get-tuple-element.11.lhs_ref, s32[1024,1]{1,0:T(8,128)} %copy.34.qpos_ref, s32[1024,1]{1,0:T(8,128)} %copy.35.qitm_ref, f32[2,1024,128]{2,1,0:T(8,128)} %attend_early.2.acc_ref, ...), custom_call_target="tpu_custom_call" | custom-call | tf_op jit(solution)/shard_map/attend_late/pallas_call | solution.py:128
  94.8 5.8 %all-to-all-start.1 = ((bf16[8,128,128]{2,1,0:T(8,128)(2,1)}), bf16[8,128,128]{2,1,0:T(8,128)(2,1)S(1)}, u32[]{:S(2)}, u32[]{:S(2)}) async-start(bf16[8,128,128]{2,1,0:T(8,128)(2,1)} %bitcast.64), calls=%async_computation.1 | async-start | bytes 524288 | tf_op jit(solution)/shard_map/all_to_all | solution.py:245
  102.0 5.8 %all-to-all-done.1.r_ref = bf16[8,128,128]{2,1,0:T(8,128)(2,1)S(1)} async-done(((bf16[8,128,128]{2,1,0:T(8,128)(2,1)}), bf16[8,128,128]{2,1,0:T(8,128)(2,1)S(1)}, u32[]{:S(2)}, u32[]{:S(2)}) %all-to-all-start.1) | async-done | bytes 262176 | tf_op jit(solution)/shard_map/all_to_all | solution.py:245
  107.8 0.7 copy-done.9
  108.5 3.0 %finish.2 = bf16[128,1024]{1,0:T(8,128)(2,1)} custom-call(bf16[8,128,128]{2,1,0:T(8,128)(2,1)} %copy-done.9, bf16[8,128,128]{2,1,0:T(8,128)(2,1)} %copy-done.7, bf16[128,1024]{1,0:T(8,128)(2,1)} %bitcast.58, bf16[1024,1024]{1,0:T(8,128)(2,1)} %bitcast.55, f32[1,1024]{1,0:T(1,128)} %reshape.57.gain_ref), custom_call_target="tpu_custom_call" | custom-call | tf_op jit(solution)/shard_map/finish/pallas_call | solution.py:158
  111.6 1.9 collective-permute-start.4
  113.5 6.0 %collective-permute-done.4 = bf16[128,1024]{1,0:T(8,128)(2,1)S(1)} collective-permute-done((bf16[128,1024]{1,0:T(8,128)(2,1)}, bf16[128,1024]{1,0:T(8,128)(2,1)S(1)}, u32[]{:S(2)}, u32[]{:S(2)}) %collective-permute-start.4) | collective-permute-done | bytes 262176 | tf_op jit(solution)/shard_map/ppermute | solution.py:250
  119.5 1.6 broadcast_in_dim.23
  121.1 3.8 %all-to-all-start.4 = ((bf16[8,128,1024]{2,1,0:T(8,128)(2,1)}), bf16[8,128,1024]{2,1,0:T(8,128)(2,1)S(1)}, u32[]{:S(2)}, u32[]{:S(2)}) async-start(bf16[8,128,1024]{2,1,0:T(8,128)(2,1)} %broadcast_in_dim.23), calls=%async_computation.4 | async-start | bytes 4194304 | tf_op jit(solution)/shard_map/all_to_all | solution.py:170
  124.9 1.2 fusion.2.qb_ref
  126.1 25.9 %all-to-all-done.4.x_ref = bf16[8,128,1024]{2,1,0:T(8,128)(2,1)S(1)} async-done(((bf16[8,128,1024]{2,1,0:T(8,128)(2,1)}), bf16[8,128,1024]{2,1,0:T(8,128)(2,1)S(1)}, u32[]{:S(2)}, u32[]{:S(2)}) %all-to-all-start.4) | async-done | bytes 2097184 | tf_op jit(solution)/shard_map/all_to_all | solution.py:170
  152.0 1.3 copy-done.3
  153.3 5.1 %project.3 = (bf16[2,1024,128]{2,1,0:T(8,128)(2,1)}, bf16[2,1024,128]{2,1,0:T(8,128)(2,1)}, bf16[1024,128]{1,0:T(8,128)(2,1)}) custom-call(s32[1]{0:T(128)} %bitcast.p_ref, bf16[8,128,1024]{2,1,0:T(8,128)(2,1)} %copy-done.3, bf16[1024,256]{1,0:T(8,128)(2,1)} %copy-done.4, bf16[1024,256]{1,0:T(8,128)(2,1)} %copy-done.6, f32[1,1024]{1,0:T(1,128)} %gain_ref.3, ...), custom_call_target="tpu_custom_call" | custom-call | tf_op jit(solution)/shard_map/project/pallas_call | solution.py:65
  158.4 4.6 %collective-permute-start.5 = (bf16[2,1024,128]{2,1,0:T(8,128)(2,1)}, bf16[2,1024,128]{2,1,0:T(8,128)(2,1)S(1)}, u32[]{:S(2)}, u32[]{:S(2)}) collective-permute-start(bf16[2,1024,128]{2,1,0:T(8,128)(2,1)} %get-tuple-element.15.kv_ref), channel_id=1, source_target_pairs={{0,8},{8,0},{1,9},{9,1},{2,10},{10,2},{3,11},{11,3},{4,12},{12,4},... | collective-permute-start | bytes 1572872 | tf_op jit(solution)/shard_map/ppermute | solution.py:174
  163.0 3.4 %all-to-all-start.6 = ((bf16[8,128,128]{2,1,0:T(8,128)(2,1)}), bf16[8,128,128]{2,1,0:T(8,128)(2,1)S(1)}, u32[]{:S(2)}, u32[]{:S(2)}) async-start(bf16[8,128,128]{2,1,0:T(8,128)(2,1)} %bitcast.66), calls=%async_computation.6 | async-start | bytes 524288 | tf_op jit(solution)/shard_map/all_to_all | solution.py:242
  167.0 1.0 copy.41.qpos_ref
  168.7 1.0 copy.42.qitm_ref
  169.7 7.7 %attend_early.3.acc_ref = f32[2,1024,128]{2,1,0:T(8,128)} custom-call(f32[2]{0:T(128)} %fusion.14.rep_ref, bf16[2,1024,128]{2,1,0:T(8,128)(2,1)} %get-tuple-element.14.lhs_ref, s32[1024,1]{1,0:T(8,128)} %copy.41.qpos_ref, s32[1024,1]{1,0:T(8,128)} %copy.42.qitm_ref, bf16[2,768,128]{2,1,0:T(8,128)(2,1)} %pad_maximum_fusion.1.ckv_ref, ...), custom_call_target="tpu_custom_call" | custom-call | tf_op jit(solution)/shard_map/attend_early/pallas_call | solution.py:116
  177.4 0.8 copy-done.11
  178.2 5.6 %attend_late.3 = bf16[1024,128]{1,0:T(8,128)(2,1)} custom-call(f32[2]{0:T(128)} %fusion.14.rep_ref, bf16[2,1024,128]{2,1,0:T(8,128)(2,1)} %get-tuple-element.14.lhs_ref, s32[1024,1]{1,0:T(8,128)} %copy.41.qpos_ref, s32[1024,1]{1,0:T(8,128)} %copy.42.qitm_ref, f32[2,1024,128]{2,1,0:T(8,128)} %attend_early.3.acc_ref, bf16[2,1024,128]{2,1,0:T(8,128)(2,1)} %copy-done.11, ...), custom_call_target="tpu_custom_call" | custom-call | tf_op jit(solution)/shard_map/attend_late/pallas_call | solution.py:128
  183.8 13.1 %all_to_all.35.r_ref = bf16[8,128,128]{2,1,0:T(8,128)(2,1)} all-to-all(bf16[8,128,128]{2,1,0:T(8,128)(2,1)} %bitcast.65), channel_id=1, replica_groups=mesh['section'=32,'p'=2,'g'=8] {'g'}, dimensions={0} | all-to-all | bytes 524288 | tf_op jit(solution)/shard_map/all_to_all | solution.py:245
  196.9 3.0 %finish.3 = bf16[128,1024]{1,0:T(8,128)(2,1)} custom-call(bf16[8,128,128]{2,1,0:T(8,128)(2,1)} %all_to_all.35.r_ref, bf16[8,128,128]{2,1,0:T(8,128)(2,1)} %copy-done.8, bf16[128,1024]{1,0:T(8,128)(2,1)} %copy-done.5, bf16[1024,1024]{1,0:T(8,128)(2,1)} %bitcast.56, f32[1,1024]{1,0:T(1,128)} %reshape.57.gain_ref), custom_call_target="tpu_custom_call" | custom-call | tf_op jit(solution)/shard_map/finish/pallas_call | solution.py:158
  199.9 1.8 maximum_bitcast_fusion
  (90 shorter events, 7.1 us)
Async XLA Ops:
  0.0 46.4 %copy-start = (bf16[1,16,64]{2,1,0:T(8,128)(2,1)S(1)}, bf16[1,16,64]{2,1,0:T(8,128)(2,1)}, u32[]{:S(2)}) copy-start(bf16[1,16,64]{2,1,0:T(8,128)(2,1)} %param.23) | copy-start | bytes 6148
  2.6 5.6 %copy-start.15 = (bf16[1,64,1024]{2,1,0:T(8,128)(2,1)S(1)}, bf16[1,64,1024]{2,1,0:T(8,128)(2,1)}, u32[]{:S(2)}) copy-start(bf16[1,64,1024]{2,1,0:T(8,128)(2,1)} %param.20) | copy-start | bytes 393220
  2.6 10.2 %slice-start = ((bf16[1,1024,192]{1,2,0:T(8,128)(2,1)}), bf16[1,1024,128]{1,2,0:T(8,128)(2,1)S(1)}, s32[]{:S(2)}) async-start(bf16[1,1024,192]{1,2,0:T(8,128)(2,1)} %param.18), calls=%async_computation.7 | async-start | bytes 524288 | tf_op jit(solution)/shard_map/slice | solution.py:203
  2.6 10.4 %slice-start.1 = ((bf16[1,1024,192]{1,2,0:T(8,128)(2,1)}), bf16[1,1024,64]{1,2,0:T(8,128)(2,1)S(1)}, s32[]{:S(2)}) async-start(bf16[1,1024,192]{1,2,0:T(8,128)(2,1)} %param.18), calls=%async_computation.8 | async-start | bytes 262144 | tf_op jit(solution)/shard_map/slice | solution.py:203
  2.6 10.6 %copy-start.14 = (bf16[1,1024,64]{1,2,0:T(8,128)(2,1)S(1)}, bf16[1,1024,64]{1,2,0:T(8,128)(2,1)}, u32[]{:S(2)}) copy-start(bf16[1,1024,64]{1,2,0:T(8,128)(2,1)} %param.19) | copy-start | bytes 393220
  2.6 36.5 %all-to-all-start = ((bf16[8,128,1024]{2,1,0:T(8,128)(2,1)}), bf16[8,128,1024]{2,1,0:T(8,128)(2,1)S(1)}, u32[]{:S(2)}, u32[]{:S(2)}) async-start(bf16[8,128,1024]{2,1,0:T(8,128)(2,1)} %broadcast_in_dim.19), calls=%async_computation | async-start | bytes 4194304 | tf_op jit(solution)/shard_map/all_to_all | solution.py:170
  8.1 30.0 %collective-permute-start.3 = (bf16[64,1024]{1,0:T(8,128)(2,1)S(1)}, bf16[64,1024]{1,0:T(8,128)(2,1)}, u32[]{:S(2)}, u32[]{:S(2)}) collective-permute-start(bf16[64,1024]{1,0:T(8,128)(2,1)S(1)} %bitcast.69), channel_id=1, source_target_pairs={{0,8},{8,0},{1,9},{9,1},{2,10},{10,2},{3,11},{11,3},{4,12},{12,4},... | collective-permute-start | bytes 393224 | tf_op jit(solution)/shard_map/ppermute | solution.py:174
  13.6 27.5 %copy-start.4 = (bf16[1024,256]{1,0:T(8,128)(2,1)}, bf16[1024,256]{1,0:T(8,128)(2,1)S(1)}, u32[]{:S(2)}) copy-start(bf16[1024,256]{1,0:T(8,128)(2,1)S(1)} %pad_maximum_fusion.own_ref) | copy-start | bytes 1572868
  13.6 42.7 %collective-permute-start = (bf16[1024,256]{1,0:T(8,128)(2,1)S(1)}, bf16[1024,256]{1,0:T(8,128)(2,1)S(1)}, u32[]{:S(2)}, u32[]{:S(2)}) collective-permute-start(bf16[1024,256]{1,0:T(8,128)(2,1)S(1)} %pad_maximum_fusion.own_ref), channel_id=1, source_target_pairs={{0,8},{8,0},{1,9},{9,1},{2,10},{10,2},{3,11},{11,3},{4,12},{12,4},... | collective-permute-start | bytes 1572872 | tf_op jit(solution)/shard_map/ppermute | solution.py:174
  16.3 63.4 %collective-permute-start.1 = (bf16[768,128]{1,0:T(8,128)(2,1)}, bf16[768,128]{1,0:T(8,128)(2,1)}, u32[]{:S(2)}, u32[]{:S(2)}) collective-permute-start(bf16[768,128]{1,0:T(8,128)(2,1)} %bitcast.68), channel_id=1, source_target_pairs={{0,8},{8,0},{1,9},{9,1},{2,10},{10,2},{3,11},{11,3},{4,12},{12,4},... | collective-permute-start | bytes 589832 | tf_op jit(solution)/shard_map/ppermute | solution.py:174
  39.1 2.0 copy-start.2
  40.9 5.4 %copy-start.21 = (s32[1,2,2048]{2,1,0:T(2,128)S(1)}, s32[1,2,2048]{2,1,0:T(2,128)}, u32[]{:S(2)}) copy-start(s32[1,2,2048]{2,1,0:T(2,128)} %param.28) | copy-start | bytes 49156
  40.9 5.4 %copy-start.22 = (s32[1,2,2048]{2,1,0:T(2,128)S(1)}, s32[1,2,2048]{2,1,0:T(2,128)}, u32[]{:S(2)}) copy-start(s32[1,2,2048]{2,1,0:T(2,128)} %param.26) | copy-start | bytes 49156
  40.9 5.5 %copy-start.20 = (s32[2,1024]{1,0:T(2,128)S(1)}, s32[2,1024]{1,0:T(2,128)}, u32[]{:S(2)}) copy-start(s32[2,1024]{1,0:T(2,128)} %reshape_squeeze.33) | copy-start | bytes 24580
  40.9 10.7 %copy-start.25 = (f32[1,16]{1,0:T(1,128)S(1)}, f32[1,16]{1,0:T(1,128)}, u32[]{:S(2)}) copy-start(f32[1,16]{1,0:T(1,128)} %param.24) | copy-start | bytes 196
  40.9 12.2 %copy-start.24 = (s32[1,768]{1,0:T(1,128)S(1)}, s32[1,768]{1,0:T(1,128)}, u32[]{:S(2)}) copy-start(s32[1,768]{1,0:T(1,128)} %param.30) | copy-start | bytes 9220
  41.1 34.4 %all-to-all-start.3 = ((bf16[8,2,64,1024]{3,2,1,0:T(8,128)(2,1)}), bf16[8,2,64,1024]{3,2,1,0:T(8,128)(2,1)S(1)}, u32[]{:S(2)}, u32[]{:S(2)}) async-start(bf16[8,2,64,1024]{3,2,1,0:T(8,128)(2,1)} %broadcast_in_dim.22), calls=%async_computation.3 | async-start | bytes 4194304 | tf_op jit(solution)/shard_map/all_to_all | solution.py:170
  47.1 15.2 %copy-start.16 = (s32[1,1024]{1,0:T(1,128)}, s32[1,1024]{1,0:T(1,128)S(1)}, u32[]{:S(2)}) copy-start(s32[1,1024]{1,0:T(1,128)S(1)} %get-tuple-element.36.kpos_ref) | copy-start | bytes 12292
  47.7 14.6 %copy-start.17 = (s32[1,1024]{1,0:T(1,128)}, s32[1,1024]{1,0:T(1,128)S(1)}, u32[]{:S(2)}) copy-start(s32[1,1024]{1,0:T(1,128)S(1)} %get-tuple-element.34.kitm_ref) | copy-start | bytes 12292
  56.3 0.8 copy-start.6
  57.1 22.6 %copy-start.13 = (bf16[1,768,1,128]{3,1,2,0:T(8,128)(2,1)S(1)}, bf16[1,768,1,128]{3,1,2,0:T(8,128)(2,1)}, u32[]{:S(2)}) copy-start(bf16[1,768,1,128]{3,1,2,0:T(8,128)(2,1)} %param.25) | copy-start | bytes 589828
  62.3 26.9 %collective-permute-start.2 = (bf16[2,1024,128]{2,1,0:T(8,128)(2,1)}, bf16[2,1024,128]{2,1,0:T(8,128)(2,1)}, u32[]{:S(2)}, u32[]{:S(2)}) collective-permute-start(bf16[2,1024,128]{2,1,0:T(8,128)(2,1)} %get-tuple-element.12.kv_ref), channel_id=1, source_target_pairs={{0,8},{8,0},{1,9},{9,1},{2,10},{10,2},{3,11},{11,3},{4,12},{12,4},... | collective-permute-start | bytes 1572872 | tf_op jit(solution)/shard_map/ppermute | solution.py:174
  75.4 13.7 %copy-start.1 = (bf16[8,2,64,1024]{3,2,1,0:T(8,128)(2,1)}, bf16[8,2,64,1024]{3,2,1,0:T(8,128)(2,1)S(1)}, u32[]{:S(2)}) copy-start(bf16[8,2,64,1024]{3,2,1,0:T(8,128)(2,1)S(1)} %all-to-all-done.3) | copy-start | bytes 6291460
  75.4 19.3 %all-to-all-start.2 = ((bf16[8,128,128]{2,1,0:T(8,128)(2,1)}), bf16[8,128,128]{2,1,0:T(8,128)(2,1)S(1)}, u32[]{:S(2)}, u32[]{:S(2)}) async-start(bf16[8,128,128]{2,1,0:T(8,128)(2,1)} %bitcast.67), calls=%async_computation.2 | async-start | bytes 524288 | tf_op jit(solution)/shard_map/all_to_all | solution.py:242
  89.2 11.4 %copy-start.23 = (f32[1,1024]{1,0:T(1,128)S(1)}, f32[1,1024]{1,0:T(1,128)}, u32[]{:S(2)}) copy-start(f32[1,1024]{1,0:T(1,128)} %param.22) | copy-start | bytes 12292
  94.7 24.7 %copy-start.12 = (bf16[128,1024]{1,0:T(8,128)(2,1)S(1)}, bf16[128,1024]{1,0:T(8,128)(2,1)}, u32[]{:S(2)}) copy-start(bf16[128,1024]{1,0:T(8,128)(2,1)} %param.17) | copy-start | bytes 786436
  94.7 13.1 %copy-start.7 = (bf16[8,128,128]{2,1,0:T(8,128)(2,1)}, bf16[8,128,128]{2,1,0:T(8,128)(2,1)S(1)}, u32[]{:S(2)}) copy-start(bf16[8,128,128]{2,1,0:T(8,128)(2,1)S(1)} %all-to-all-done.2.g_ref) | copy-start | bytes 786436
  94.8 13.1 %all-to-all-start.1 = ((bf16[8,128,128]{2,1,0:T(8,128)(2,1)}), bf16[8,128,128]{2,1,0:T(8,128)(2,1)S(1)}, u32[]{:S(2)}, u32[]{:S(2)}) async-start(bf16[8,128,128]{2,1,0:T(8,128)(2,1)} %bitcast.64), calls=%async_computation.1 | async-start | bytes 524288 | tf_op jit(solution)/shard_map/all_to_all | solution.py:245
  107.8 0.7 copy-start.9
  111.6 7.9 %collective-permute-start.4 = (bf16[128,1024]{1,0:T(8,128)(2,1)}, bf16[128,1024]{1,0:T(8,128)(2,1)S(1)}, u32[]{:S(2)}, u32[]{:S(2)}) collective-permute-start(bf16[128,1024]{1,0:T(8,128)(2,1)} %finish.2), channel_id=1, source_target_pairs={{0,16},{16,32},{32,48},{48,64},{64,80},{80,96},{96,112},{112,128},... | collective-permute-start | bytes 786440 | tf_op jit(solution)/shard_map/ppermute | solution.py:250
  119.5 1.6 copy-start.5
  121.1 30.9 %all-to-all-start.4 = ((bf16[8,128,1024]{2,1,0:T(8,128)(2,1)}), bf16[8,128,1024]{2,1,0:T(8,128)(2,1)S(1)}, u32[]{:S(2)}, u32[]{:S(2)}) async-start(bf16[8,128,1024]{2,1,0:T(8,128)(2,1)} %broadcast_in_dim.23), calls=%async_computation.4 | async-start | bytes 4194304 | tf_op jit(solution)/shard_map/all_to_all | solution.py:170
  152.0 1.3 copy-start.3
  158.4 19.0 %collective-permute-start.5 = (bf16[2,1024,128]{2,1,0:T(8,128)(2,1)}, bf16[2,1024,128]{2,1,0:T(8,128)(2,1)S(1)}, u32[]{:S(2)}, u32[]{:S(2)}) collective-permute-start(bf16[2,1024,128]{2,1,0:T(8,128)(2,1)} %get-tuple-element.15.kv_ref), channel_id=1, source_target_pairs={{0,8},{8,0},{1,9},{9,1},{2,10},{10,2},{3,11},{11,3},{4,12},{12,4},... | collective-permute-start | bytes 1572872 | tf_op jit(solution)/shard_map/ppermute | solution.py:174
  163.0 20.8 %all-to-all-start.6 = ((bf16[8,128,128]{2,1,0:T(8,128)(2,1)}), bf16[8,128,128]{2,1,0:T(8,128)(2,1)S(1)}, u32[]{:S(2)}, u32[]{:S(2)}) async-start(bf16[8,128,128]{2,1,0:T(8,128)(2,1)} %bitcast.66), calls=%async_computation.6 | async-start | bytes 524288 | tf_op jit(solution)/shard_map/all_to_all | solution.py:242
  167.0 2.7 %copy-start.18 = (s32[1,1024]{1,0:T(1,128)}, s32[1,1024]{1,0:T(1,128)S(1)}, u32[]{:S(2)}) copy-start(s32[1,1024]{1,0:T(1,128)S(1)} %get-tuple-element.30.kpos_ref) | copy-start | bytes 12292
  168.7 1.1 copy-start.19
  177.4 0.8 copy-start.11
  183.8 16.1 %copy-start.10 = (bf16[128,1024]{1,0:T(8,128)(2,1)S(1)}, bf16[128,1024]{1,0:T(8,128)(2,1)}, u32[]{:S(2)}) copy-start(bf16[128,1024]{1,0:T(8,128)(2,1)} %finish.2) | copy-start | bytes 786436
  183.8 13.1 %copy-start.8 = (bf16[8,128,128]{2,1,0:T(8,128)(2,1)}, bf16[8,128,128]{2,1,0:T(8,128)(2,1)S(1)}, u32[]{:S(2)}) copy-start(bf16[8,128,128]{2,1,0:T(8,128)(2,1)S(1)} %all-to-all-done.6.g_ref) | copy-start | bytes 786436

commit v2 on v1

v2 whole, which is shorter than its diff:
```python
import functools

import jax
import jax.numpy as jnp
from jax import lax
from jax.experimental import pallas as pl
from jax.experimental.pallas import tpu as pltpu
from jax.sharding import Mesh, PartitionSpec as P

D = 1024
H = 16
DH = 64
NB = 64
TICKS = 2
CACHE = 768
SLICE = 2048
NK = CACHE + SLICE
EPSILON = 1e-05
NP = 2
NG = 8
ROWS = SLICE // (NP * NG)
BAND = SLICE // NP
KBLOCK = 256
PART = ROWS // 2
HALF = BAND // 2
BF16 = jnp.bfloat16
F32 = jnp.float32
VMEM_LIMIT = 60 * 1024 * 1024


def silu(v):
    half = 0.5 * v
    return half + half * jnp.tanh(half)


def vmem():
    return pl.BlockSpec(memory_space=pltpu.VMEM)


def smem():
    return pl.BlockSpec(memory_space=pltpu.SMEM)


def params():
    return pltpu.CompilerParams(vmem_limit_bytes=VMEM_LIMIT)


def low_lanes(rows):
    return lax.broadcasted_iota(jnp.int32, (rows, 2 * DH), 1) < DH


def spread_kernel(first_ref, x_ref, new_ref, gain_ref, here_ref, one_ref, two_ref):
    fresh = jnp.full((ROWS, 1), first_ref[0], jnp.int32) > 0
    here = jnp.where(fresh, new_ref[...].astype(F32), x_ref[...].astype(F32))
    here_ref[...] = here.astype(BF16)
    mean = jnp.mean(here, axis=-1, keepdims=True)
    variance = jnp.mean(here * here, axis=-1, keepdims=True) - mean * mean
    normed = ((here - mean) * lax.rsqrt(variance + EPSILON) * gain_ref[...]).astype(BF16)
    for k in range(NG):
        one_ref[k] = normed[:PART]
        two_ref[k] = normed[PART:]


def spread(*operands):
    return pl.pallas_call(
        spread_kernel,
        out_shape=(jax.ShapeDtypeStruct((ROWS, D), BF16),) + (jax.ShapeDtypeStruct((NG, PART, D), BF16),) * 2,
        in_specs=[smem()] + [vmem()] * 3,
        out_specs=(vmem(),) * 3,
        compiler_params=params(),
        name="spread",
    )(*operands)


def column(row):
    return jnp.transpose(jnp.broadcast_to(row, (128, row.shape[1])))


def prep_kernel(tick, p_ref, meta_ref, cbkt_ref, table_ref, qpos_ref, qitm_ref, qb_ref, ko_ref, cko_ref, krow_ref):
    lane = lax.broadcasted_iota(jnp.int32, (BAND, 128), 1)
    flip = jnp.full((1, BAND), p_ref[0], jnp.int32) > 0

    def bands(k):
        row = meta_ref[k * TICKS + tick : k * TICKS + tick + 1, :]
        low, high = row[:, :BAND], row[:, BAND:]
        return jnp.where(flip, high, low), jnp.where(flip, low, high)

    pos, bkt, itm = bands(0), bands(1), bands(2)
    qpos_ref[...] = column(pos[0])
    qitm_ref[...] = column(itm[0])
    for b in range(NP):
        level = column(bkt[b])
        ko_ref[b] = jnp.where(level == lane - DH, 1.0, 0.0).astype(BF16)
        krow_ref[b, 0:1, :] = pos[b]
        krow_ref[b, 1:2, :] = itm[b]
        if b == 0:
            onehot = jnp.where(level == lane, 1.0, 0.0).astype(BF16)
            for h in range(NP):
                qb_ref[h] = jnp.dot(onehot, table_ref[h], preferred_element_type=F32).astype(BF16)
    cko_ref[...] = jnp.where(column(cbkt_ref[...]) == lane[:CACHE] - DH, 1.0, 0.0).astype(BF16)


def prep(tick, *operands):
    return pl.pallas_call(
        functools.partial(prep_kernel, tick),
        out_shape=(
            jax.ShapeDtypeStruct((BAND, 128), jnp.int32),
            jax.ShapeDtypeStruct((BAND, 128), jnp.int32),
            jax.ShapeDtypeStruct((NP, BAND, 128), BF16),
            jax.ShapeDtypeStruct((NP, BAND, 128), BF16),
            jax.ShapeDtypeStruct((CACHE, 128), BF16),
            jax.ShapeDtypeStruct((NP, 2, BAND), jnp.int32),
        ),
        in_specs=[smem()] + [vmem()] * 3,
        out_specs=(vmem(),) * 6,
        compiler_params=params(),
        name="prep",
    )(*operands)


def project_kernel(half, p_ref, x_ref, own_ref, other_ref, qb_ref, lhs_ref, kv_ref, gate_ref):
    normed = x_ref[...].reshape(HALF, D)
    low = low_lanes(HALF)
    rows = slice(half * HALF, (half + 1) * HALF)
    firsts = []
    for h, w_ref in enumerate((own_ref, other_ref)):
        z = silu(jnp.dot(normed, w_ref[...], preferred_element_type=F32))
        kv_ref[h] = z[:, 2 * DH :].astype(BF16)
        first = z[:, : 2 * DH]
        lhs_ref[h] = jnp.where(low, 0.5 * first, qb_ref[h, rows, :].astype(F32)).astype(BF16)
        firsts.append(first)
    flip = jnp.full((HALF, 1), p_ref[0], jnp.int32) > 0
    left = jnp.where(flip, firsts[1], firsts[0])
    right = jnp.where(flip, firsts[0], firsts[1])
    gate_ref[...] = jnp.where(low, pltpu.roll(left, DH, 1), right).astype(BF16)


def project(half, *operands):
    return pl.pallas_call(
        functools.partial(project_kernel, half),
        out_shape=(
            jax.ShapeDtypeStruct((NP, HALF, 2 * DH), BF16),
            jax.ShapeDtypeStruct((NP, HALF, 2 * DH), BF16),
            jax.ShapeDtypeStruct((HALF, 2 * DH), BF16),
        ),
        in_specs=[smem()] + [vmem()] * 4,
        out_specs=(vmem(),) * 3,
        compiler_params=params(),
        name="project",
    )(*operands)


def add_keys(rep_ref, lhs_ref, qpos_ref, qitm_ref, same, allowed, acc, rows, kv_refs, ko, kpos, kitm, fresh):
    count = kv_refs[0].shape[0]
    size = rows.stop - rows.start
    low = low_lanes(KBLOCK)
    for c in range(count // KBLOCK):
        ks = slice(c * KBLOCK, (c + 1) * KBLOCK)
        wide = jnp.concatenate([qitm_ref[rows, :]] * (KBLOCK // 128), axis=1)
        same[:size] = jnp.where(wide == kitm(ks), 1.0, 0.0)
        wide = jnp.concatenate([qpos_ref[rows, :]] * (KBLOCK // 128), axis=1)
        allowed[:size] = jnp.where(kpos(ks) <= wide, 1.0, 0.0).astype(BF16)
        for h in range(NP):
            kv = kv_refs[h][ks, :]
            keys = jnp.where(low, kv, ko(ks))
            half = lax.dot_general(lhs_ref[h, rows, :], keys, (((1,), (1,)), ((), ())), preferred_element_type=F32)
            half = half + (0.5 * rep_ref[h]) * same[:size]
            weight = (half + half * jnp.tanh(half)).astype(BF16) * allowed[:size]
            part = jnp.dot(weight, kv, preferred_element_type=F32)
            if fresh and c == 0:
                acc[h, rows, :] = part
            else:
                acc[h, rows, :] += part


FIRST, SECOND, WHOLE = slice(0, HALF), slice(HALF, BAND), slice(0, BAND)


def sides(ko_ref, krow_ref, band, half):
    base = half * HALF

    def at(ks):
        return slice(base + ks.start, base + ks.stop)

    return (
        lambda ks: ko_ref[band, at(ks), :],
        lambda ks: krow_ref[band, 0:1, at(ks)],
        lambda ks: krow_ref[band, 1:2, at(ks)],
    )


def cache_sides(cko_ref, crow_ref):
    return (lambda ks: cko_ref[ks, :], lambda ks: crow_ref[0:1, ks], lambda ks: crow_ref[1:2, ks])


def one_kernel(rep_ref, qpos_ref, qitm_ref, ko_ref, krow_ref, cko_ref, crow_ref, cown_ref, cother_ref, lhs_ref, kv_ref, acc, same, allowed):
    shared = (rep_ref, lhs_ref, qpos_ref, qitm_ref, same, allowed, acc, FIRST)
    add_keys(*shared, (cown_ref, cother_ref), *cache_sides(cko_ref, crow_ref), True)
    add_keys(*shared, (kv_ref.at[0], kv_ref.at[1]), *sides(ko_ref, krow_ref, 0, 0), False)


def two_kernel(rep_ref, qpos_ref, qitm_ref, ko_ref, krow_ref, cko_ref, crow_ref, cown_ref, cother_ref, lhs1_ref, kv1_ref, acc1_ref, lhs2_ref, kv2_ref, far1_ref, acc, lhs, same, allowed):
    for h in range(NP):
        lhs[h, FIRST, :] = lhs1_ref[h]
        lhs[h, SECOND, :] = lhs2_ref[h]
        acc[h, FIRST, :] = acc1_ref[h]
    shared = (rep_ref, lhs, qpos_ref, qitm_ref, same, allowed, acc)
    add_keys(*shared, SECOND, (cown_ref, cother_ref), *cache_sides(cko_ref, crow_ref), True)
    add_keys(*shared, SECOND, (kv1_ref.at[0], kv1_ref.at[1]), *sides(ko_ref, krow_ref, 0, 0), False)
    add_keys(*shared, WHOLE, (kv2_ref.at[0], kv2_ref.at[1]), *sides(ko_ref, krow_ref, 0, 1), False)
    add_keys(*shared, WHOLE, (far1_ref.at[1], far1_ref.at[0]), *sides(ko_ref, krow_ref, 1, 0), False)


def three_kernel(rep_ref, p_ref, qpos_ref, qitm_ref, ko_ref, krow_ref, lhs1_ref, lhs2_ref, acc_ref, gate1_ref, gate2_ref, far2_ref, out_ref, acc, lhs, same, allowed):
    for h in range(NP):
        lhs[h, FIRST, :] = lhs1_ref[h]
        lhs[h, SECOND, :] = lhs2_ref[h]
    acc[...] = acc_ref[...]
    add_keys(rep_ref, lhs, qpos_ref, qitm_ref, same, allowed, acc, WHOLE, (far2_ref.at[1], far2_ref.at[0]), *sides(ko_ref, krow_ref, 1, 1), False)
    attended = (jnp.where(low_lanes(BAND), pltpu.roll(acc[p_ref[0]], DH, 1), acc[1 - p_ref[0]]) * (1.0 / NK)).astype(BF16)
    for half, gate_ref in enumerate((gate1_ref, gate2_ref)):
        for k in range(NG):
            rows = slice(half * PART, (half + 1) * PART)
            start = half * HALF + k * PART
            out_ref[k, rows, : 2 * DH] = attended[start : start + PART]
            out_ref[k, rows, 2 * DH :] = gate_ref[k * PART : (k + 1) * PART, :]


def masks(rows):
    return [pltpu.VMEM((rows, KBLOCK), F32), pltpu.VMEM((rows, KBLOCK), BF16)]


ACC = pltpu.VMEM((NP, BAND, 2 * DH), F32)
LHS = pltpu.VMEM((NP, BAND, 2 * DH), BF16)


def attend(kernel, shape, dtype, scratch, *operands):
    return pl.pallas_call(
        kernel,
        out_shape=jax.ShapeDtypeStruct(shape, dtype),
        in_specs=[smem() if a.ndim == 1 else vmem() for a in operands],
        out_specs=vmem(),
        scratch_shapes=scratch,
        compiler_params=params(),
        name="attend_" + kernel.__name__,
    )(*operands)


def finish_rows(r_ref, x_ref, w_ref, gain_ref, mixed):
    total = jnp.zeros((ROWS, 2 * DH), F32)
    square = jnp.zeros((ROWS, 2 * DH), F32)
    for k in range(NG):
        a = r_ref[k, :, : 2 * DH].astype(F32)
        total += a
        square += a * a
    mean = jnp.sum(total, axis=-1, keepdims=True) * (1.0 / D)
    variance = jnp.sum(square, axis=-1, keepdims=True) * (1.0 / D) - mean * mean
    scale = lax.rsqrt(variance + EPSILON)
    low = low_lanes(ROWS)
    for k in range(0, NG, 2):
        parts = []
        for r in (r_ref[k], r_ref[k + 1]):
            r = r.astype(F32)
            parts.append((r[:, : 2 * DH] - mean) * scale * r[:, 2 * DH :])
        left = jnp.where(low, parts[0], pltpu.roll(parts[1], DH, 1))
        right = jnp.where(low, pltpu.roll(parts[0], DH, 1), parts[1])
        for start, part in ((k * DH, left), (k * DH + D // 2, right)):
            cols = slice(start, start + 2 * DH)
            mixed[:, cols] = (part * gain_ref[:, cols]).astype(BF16)
    y = jnp.dot(mixed[...], w_ref[...], preferred_element_type=F32)
    return (x_ref[...].astype(F32) + y).astype(BF16)


def finish_kernel(r_ref, x_ref, w_ref, gain_ref, out_ref, mixed):
    out_ref[...] = finish_rows(r_ref, x_ref, w_ref, gain_ref, mixed)


def last_kernel(before_ref, r_ref, x_ref, w_ref, gain_ref, out_ref, mixed):
    out_ref[0] = before_ref[...]
    out_ref[1] = finish_rows(r_ref, x_ref, w_ref, gain_ref, mixed)


def finish(*operands):
    last = len(operands) == 5
    return pl.pallas_call(
        last_kernel if last else finish_kernel,
        out_shape=jax.ShapeDtypeStruct((TICKS, ROWS, D) if last else (ROWS, D), BF16),
        in_specs=[vmem()] * len(operands),
        out_specs=vmem(),
        scratch_shapes=[pltpu.VMEM((ROWS, D), BF16)],
        compiler_params=params(),
        name="finish_last" if last else "finish",
    )(*operands)


def swap(x):
    return lax.ppermute(x, "p", [(0, 1), (1, 0)])


def body(
    slices,
    new_slice,
    w_qkv,
    w_gate,
    w_out,
    input_gain,
    output_gain,
    bucket_bias,
    repeat_bias,
    cache_kv,
    slice_positions,
    slice_buckets,
    slice_items,
    cache_positions,
    cache_buckets,
    cache_items,
):
    p = lax.axis_index("p")
    g = lax.axis_index("g")
    section = lax.axis_index("section")

    w_out_full = lax.all_gather(w_out[0], ("p", "g"), axis=0, tiled=True)
    w_own = jnp.concatenate([w_qkv[0, :, :DH], w_gate[0], w_qkv[0, :, DH:]], axis=1)
    w_other = swap(w_own)
    c_own = cache_kv[0, :, 0, :]
    c_other = swap(c_own)

    def pair(a):
        a = a.reshape((NP, NG) + a.shape[1:])
        a = lax.dynamic_index_in_dim(a, g, 1, keepdims=False)
        return jnp.where(p == 0, a, a[::-1])

    tables = pair(bucket_bias[0])
    rep = pair(repeat_bias[0])
    levels = jnp.arange(NB, dtype=jnp.int32)
    distance = jnp.abs(levels[:, None] - levels[None, :])
    lookup = (distance[:, :, None] == levels[None, None, :]).astype(F32)
    toeplitz = jnp.einsum("abc,hc->hab", lookup, tables.astype(F32)).astype(BF16)
    toeplitz = jnp.pad(0.5 * toeplitz, ((0, 0), (0, DH), (DH, 0)))
    p_word = p.astype(jnp.int32).reshape(1)
    meta = jnp.stack([slice_positions[0], slice_buckets[0], slice_items[0]])
    meta = meta.reshape(3, TICKS, NP, NG, 2, PART).transpose(0, 1, 2, 4, 3, 5).reshape(3 * TICKS, SLICE)
    crow = jnp.concatenate([cache_positions, cache_items])
    preps = [prep(tick, p_word, meta, cache_buckets, toeplitz) for tick in range(TICKS)]

    received = slices[0]
    first = jnp.zeros((1,), jnp.int32)
    produced = ()
    for tick in range(TICKS):
        current, copies1, copies2 = spread(first, received, new_slice, input_gain)
        band1 = lax.all_to_all(copies1, "g", 0, 0)
        if tick == 0:
            band1, preps, crow, rep, w_own, w_other, c_other = lax.optimization_barrier(
                (band1, preps, crow, rep, w_own, w_other, c_other)
            )
        qpos, qitm, qb, ko, cko, krow = preps[tick]
        keyed = (rep, qpos, qitm, ko, krow)
        cache = (cko, crow, c_own, c_other)
        copies2, band1 = lax.optimization_barrier((copies2, band1))
        band2 = lax.all_to_all(copies2, "g", 0, 0)
        lhs1, kv1, gate1 = project(0, p_word, band1, w_own, w_other, qb)
        far1 = swap(kv1)
        acc1 = attend(one_kernel, (NP, HALF, 2 * DH), F32, masks(HALF), *keyed, *cache, lhs1, kv1)
        band2, acc1 = lax.optimization_barrier((band2, acc1))
        lhs2, kv2, gate2 = project(1, p_word, band2, w_own, w_other, qb)
        far2 = swap(kv2)
        acc = attend(two_kernel, (NP, BAND, 2 * DH), F32, [LHS] + masks(BAND), *keyed, *cache, lhs1, kv1, acc1, lhs2, kv2, far1)
        a = attend(three_kernel, (NG, ROWS, 4 * DH), BF16, [ACC, LHS] + masks(BAND), rep, p_word, *keyed[1:], lhs1, lhs2, acc, gate1, gate2, far2)
        back = lax.all_to_all(a, "g", 0, 0)
        if tick + 1 < TICKS:
            one = finish(back, current, w_out_full, output_gain)
            produced = (one,)
            count = lax.axis_size("section")
            received = lax.ppermute(one, "section", [(s, s + 1) for s in range(count - 1)])
            first = (section == 0).astype(jnp.int32).reshape(1)
    return finish(*produced, back, current, w_out_full, output_gain)[None]


def solution(mesh):
    sections = mesh.shape["section"]
    grid = Mesh(mesh.devices.reshape(sections, NP, NG), ("section", "p", "g"))
    seq = ("p", "g")
    in_specs = (
        P("section", seq, None),
        P(seq, None),
        P("section", None, seq),
        P("section", None, seq),
        P("section", seq, None),
        P("section", None),
        P("section", None),
        P("section", None, None),
        P("section", None),
        P("section", None, seq, None),
        P("section", None, None),
        P("section", None, None),
        P("section", None, None),
        P("section", None),
        P("section", None),
        P("section", None),
    )
    out_specs = P("section", None, seq, None)
    return jax.shard_map(body, mesh=grid, in_specs=in_specs, out_specs=out_specs, check_vma=False)
```

time: 203 us -> 209 us (1.030)
  the two profiles are of different devices: /device:TPU:96 before, /device:TPU:224 now
where the time goes in v2:
time: 209 us; the launch traced here: 208 us
  Pallas kernels  63.1 us (30%)
  blocking collectives  48.9 us (23%)
  starting transfers between devices  42.1 us (20%)
  waiting for transfers between devices  28.2 us (13%)
  between operations  13.7 us (7%)
  local copies, waits for them, and re-layouts  8.68 us (4%)
  other arithmetic  2.11 us (1%)
    pallas_call x6, Pallas kernels, attend(): pl.pallas_call(kernel, out_shape=jax.ShapeDtypeStruct(shape, dtype), in_s...  32.4 us
    all_to_all x2, blocking collectives, body(): back = lax.all_to_all(a, 'g', 0, 0)  28.3 us
    ppermute x6, starting transfers between devices, swap(): return lax.ppermute(x, 'p', [(0, 1), (1, 0)])  26.4 us
    all_to_all x1, blocking collectives, body(): band1 = lax.all_to_all(copies1, 'g', 0, 0)  20.5 us
    ppermute x6, waiting for transfers between devices, swap(): return lax.ppermute(x, 'p', [(0, 1), (1, 0)])  13.8 us
    pallas_call x4, Pallas kernels, project(): pl.pallas_call(functools.partial(project_kernel, half), out_shape=(jax.Sh...  13.7 us
    all_to_all x2, starting transfers between devices, body(): band2 = lax.all_to_all(copies2, 'g', 0, 0)  8.34 us
    all_to_all x2, waiting for transfers between devices, body(): band2 = lax.all_to_all(copies2, 'g', 0, 0)  7.76 us
  transfers between devices with their start and end apart: 11, of which 5 were waited for; matrix products, arithmetic and copies ran while one was open for 3% of the time, Pallas kernels for 24%

profile of v2, /device:TPU:224, one launch (start us, length us, event | category | flops | bytes accessed | tf_op | source)
XLA Modules:
  0.0 208.0 jit_solution(11590703549225487930)
XLA Ops:
  6.5 0.7 all-gather.3.cloned.1.call-update
  7.3 2.6 %spread.2 = (bf16[128,1024]{1,0:T(8,128)(2,1)}, bf16[8,64,1024]{2,1,0:T(8,128)(2,1)}, bf16[8,64,1024]{2,1,0:T(8,128)(2,1)}) custom-call(s32[1]{0:T(128)} %constant.12.clone.1.first_ref, bf16[128,1024]{1,0:T(8,128)(2,1)} %bitcast.33, bf16[128,1024]{1,0:T(8,128)(2,1)} %new_ref.3, f32[1,1024]{1,0:T(1,128)} %gain_ref.6), custom_call_target="tpu_custom_call" | custom-call | tf_op jit(solution)/shard_map/spread/pallas_call | solution.py:65
  9.9 5.4 %all-to-all-start = ((bf16[8,64,1024]{2,1,0:T(8,128)(2,1)}), bf16[8,64,1024]{2,1,0:T(8,128)(2,1)S(1)}, u32[]{:S(2)}, u32[]{:S(2)}) async-start(bf16[8,64,1024]{2,1,0:T(8,128)(2,1)} %get-tuple-element.61), calls=%async_computation | async-start | bytes 2097152 | tf_op jit(solution)/shard_map/all_to_all | solution.py:351
  16.2 4.6 %collective-permute-start = (bf16[1024,256]{1,0:T(8,128)(2,1)S(1)}, bf16[1024,256]{1,0:T(8,128)(2,1)S(1)}, u32[]{:S(2)}, u32[]{:S(2)}) collective-permute-start(bf16[1024,256]{1,0:T(8,128)(2,1)S(1)} %pad_maximum_fusion.own_ref), channel_id=1, source_target_pairs={{0,8},{8,0},{1,9},{9,1},{2,10},{10,2},{3,11},{11,3},{4,12},{12,4},... | collective-permute-start | bytes 1572872 | tf_op jit(solution)/shard_map/ppermute | solution.py:297
  20.9 2.7 %collective-permute-start.1 = (bf16[768,128]{1,0:T(8,128)(2,1)S(1)}, bf16[768,128]{1,0:T(8,128)(2,1)S(1)}, u32[]{:S(2)}, u32[]{:S(2)}) collective-permute-start(bf16[768,128]{1,0:T(8,128)(2,1)S(1)} %bitcast.28), channel_id=1, source_target_pairs={{0,8},{8,0},{1,9},{9,1},{2,10},{10,2},{3,11},{11,3},{4,12},{12,4},... | collective-permute-start | bytes 589832 | tf_op jit(solution)/shard_map/ppermute | solution.py:297
  23.8 0.7 reshape.29.meta_ref
  24.6 1.2 fusion
  25.8 0.7 pad.4.table_ref
  26.5 2.6 %prep.2 = (s32[1024,128]{1,0:T(8,128)}, s32[1024,128]{1,0:T(8,128)}, bf16[2,1024,128]{2,1,0:T(8,128)(2,1)}, bf16[2,1024,128]{2,1,0:T(8,128)(2,1)}, bf16[768,128]{1,0:T(8,128)(2,1)}, /*index=5*/s32[2,2,1024]{2,1,0:T(2,128)}) custom-call(s32[1]{0:T(128)} %bitcast.1.p_ref, s32[6,2048]{1,0:T(8,128)} %reshape.29.meta_ref, s32[1,768]{1,0:T(1,128)} %cbkt_ref.3, ...), custom_call_target="tpu_custom_call" | custom-call | tf_op jit(solution)/shard_map/prep/pallas_call | solution.py:104
  29.1 2.6 %prep.3 = (s32[1024,128]{1,0:T(8,128)}, s32[1024,128]{1,0:T(8,128)}, bf16[2,1024,128]{2,1,0:T(8,128)(2,1)}, bf16[2,1024,128]{2,1,0:T(8,128)(2,1)}, bf16[768,128]{1,0:T(8,128)(2,1)}, /*index=5*/s32[2,2,1024]{2,1,0:T(2,128)}) custom-call(s32[1]{0:T(128)} %bitcast.1.p_ref, s32[6,2048]{1,0:T(8,128)} %reshape.29.meta_ref, s32[1,768]{1,0:T(1,128)} %cbkt_ref.3, ...), custom_call_target="tpu_custom_call" | custom-call | tf_op jit(solution)/shard_map/prep/pallas_call | solution.py:104
  31.8 0.6 broadcast.11
  32.4 0.7 reduce.5
  33.4 0.6 pad_add_fusion.1.crow_ref
  34.5 13.0 %collective-permute-done.1.cother_ref = bf16[768,128]{1,0:T(8,128)(2,1)S(1)} collective-permute-done((bf16[768,128]{1,0:T(8,128)(2,1)S(1)}, bf16[768,128]{1,0:T(8,128)(2,1)S(1)}, u32[]{:S(2)}, u32[]{:S(2)}) %collective-permute-start.1) | collective-permute-done | bytes 196640 | tf_op jit(solution)/shard_map/ppermute | solution.py:297
  47.6 4.8 %all-to-all-start.1 = ((bf16[8,64,1024]{2,1,0:T(8,128)(2,1)}), bf16[8,64,1024]{2,1,0:T(8,128)(2,1)S(1)}, u32[]{:S(2)}, u32[]{:S(2)}) async-start(bf16[8,64,1024]{2,1,0:T(8,128)(2,1)} %get-tuple-element.86), calls=%async_computation.1 | async-start | bytes 2097152 | tf_op jit(solution)/shard_map/all_to_all | solution.py:360
  52.4 3.4 %project.4 = (bf16[2,512,128]{2,1,0:T(8,128)(2,1)}, bf16[2,512,128]{2,1,0:T(8,128)(2,1)}, bf16[512,128]{1,0:T(8,128)(2,1)}) custom-call(s32[1]{0:T(128)} %bitcast.1.p_ref, bf16[8,64,1024]{2,1,0:T(8,128)(2,1)} %copy-done.3, bf16[1024,256]{1,0:T(8,128)(2,1)} %copy-done.1, bf16[1024,256]{1,0:T(8,128)(2,1)} %copy-done.2, ...), custom_call_target="tpu_custom_call" | custom-call | tf_op jit(solution)/shard_map/project/pallas_call | solution.py:139
  55.8 3.9 %collective-permute-start.2 = (bf16[2,512,128]{2,1,0:T(8,128)(2,1)}, bf16[2,512,128]{2,1,0:T(8,128)(2,1)S(1)}, u32[]{:S(2)}, u32[]{:S(2)}) collective-permute-start(bf16[2,512,128]{2,1,0:T(8,128)(2,1)} %get-tuple-element.90.kv_ref.kv1_ref), channel_id=1, source_target_pairs={{0,8},{8,0},{1,9},{9,1},{2,10},{10,2},{3,11},{11,3},{4,12},{12,4},... | collective-permute-start | bytes 786440 | tf_op jit(solution)/shard_map/ppermute | solution.py:297
  59.7 4.3 %attend_one_kernel.2.acc1_ref = f32[2,512,128]{2,1,0:T(8,128)} custom-call(f32[2]{0:T(128)} %broadcast_select_fusion.rep_ref, s32[1024,128]{1,0:T(8,128)} %get-tuple-element.75.qpos_ref, s32[1024,128]{1,0:T(8,128)} %get-tuple-element.76.qitm_ref, bf16[2,1024,128]{2,1,0:T(8,128)(2,1)} %get-tuple-element.77.ko_ref, s32[2,2,1024]{2,1,0:T(2,128)} %get-tuple-element.78.krow_ref, ...), custom_call_target="tpu_custom_call" | custom-call | tf_op jit(solution)/shard_map/attend_one_kernel/pallas_call | solution.py:238
  64.0 5.8 %all-to-all-done.1.x_ref = bf16[8,64,1024]{2,1,0:T(8,128)(2,1)S(1)} async-done(((bf16[8,64,1024]{2,1,0:T(8,128)(2,1)}), bf16[8,64,1024]{2,1,0:T(8,128)(2,1)S(1)}, u32[]{:S(2)}, u32[]{:S(2)}) %all-to-all-start.1) | async-done | bytes 1048608 | tf_op jit(solution)/shard_map/all_to_all | solution.py:360
  69.8 1.0 copy-done.5
  70.8 3.5 %project.5 = (bf16[2,512,128]{2,1,0:T(8,128)(2,1)}, bf16[2,512,128]{2,1,0:T(8,128)(2,1)}, bf16[512,128]{1,0:T(8,128)(2,1)}) custom-call(s32[1]{0:T(128)} %bitcast.1.p_ref, bf16[8,64,1024]{2,1,0:T(8,128)(2,1)} %copy-done.5, bf16[1024,256]{1,0:T(8,128)(2,1)} %copy-done.1, bf16[1024,256]{1,0:T(8,128)(2,1)} %copy-done.2, ...), custom_call_target="tpu_custom_call" | custom-call | tf_op jit(solution)/shard_map/project/pallas_call | solution.py:139
  74.2 3.4 %collective-permute-start.3 = (bf16[2,512,128]{2,1,0:T(8,128)(2,1)}, bf16[2,512,128]{2,1,0:T(8,128)(2,1)S(1)}, u32[]{:S(2)}, u32[]{:S(2)}) collective-permute-start(bf16[2,512,128]{2,1,0:T(8,128)(2,1)} %get-tuple-element.94.kv2_ref), channel_id=1, source_target_pairs={{0,8},{8,0},{1,9},{9,1},{2,10},{10,2},{3,11},{11,3},{4,12},{12,4},... | collective-permute-start | bytes 786440 | tf_op jit(solution)/shard_map/ppermute | solution.py:297
  77.7 0.8 collective-permute-done.2.far1_ref
  78.5 0.7 copy-done.11
  79.2 7.4 %attend_two_kernel.2.acc_ref = f32[2,1024,128]{2,1,0:T(8,128)} custom-call(f32[2]{0:T(128)} %broadcast_select_fusion.rep_ref, s32[1024,128]{1,0:T(8,128)} %get-tuple-element.75.qpos_ref, s32[1024,128]{1,0:T(8,128)} %get-tuple-element.76.qitm_ref, bf16[2,1024,128]{2,1,0:T(8,128)(2,1)} %get-tuple-element.77.ko_ref, s32[2,2,1024]{2,1,0:T(2,128)} %get-tuple-element.78.krow_ref, ...), custom_call_target="tpu_custom_call" | custom-call | tf_op jit(solution)/shard_map/attend_two_kernel/pallas_call | solution.py:238
  86.6 0.7 copy-done.10
  87.3 4.5 %attend_three_kernel.2 = bf16[8,128,256]{2,1,0:T(8,128)(2,1)} custom-call(f32[2]{0:T(128)} %broadcast_select_fusion.rep_ref, s32[1]{0:T(128)} %bitcast.1.p_ref, s32[1024,128]{1,0:T(8,128)} %get-tuple-element.75.qpos_ref, s32[1024,128]{1,0:T(8,128)} %get-tuple-element.76.qitm_ref, bf16[2,1024,128]{2,1,0:T(8,128)(2,1)} %get-tuple-element.77.ko_ref, ...), custom_call_target="tpu_custom_call" | custom-call | tf_op jit(solution)/shard_map/attend_three_kernel/pallas_call | solution.py:238
  91.8 14.2 %all_to_all.30.r_ref = bf16[8,128,256]{2,1,0:T(8,128)(2,1)} all-to-all(bf16[8,128,256]{2,1,0:T(8,128)(2,1)} %attend_three_kernel.2), channel_id=1, replica_groups=mesh['section'=32,'p'=2,'g'=8] {'g'}, dimensions={0} | all-to-all | bytes 1048576 | tf_op jit(solution)/shard_map/all_to_all | solution.py:369
  106.0 3.2 %finish.1.before_ref = bf16[128,1024]{1,0:T(8,128)(2,1)} custom-call(bf16[8,128,256]{2,1,0:T(8,128)(2,1)} %all_to_all.30.r_ref, bf16[128,1024]{1,0:T(8,128)(2,1)} %get-tuple-element.97.x_ref, bf16[1024,1024]{1,0:T(8,128)(2,1)} %bitcast.22, f32[1,1024]{1,0:T(1,128)} %gain_ref.7), custom_call_target="tpu_custom_call" | custom-call | tf_op jit(solution)/shard_map/finish/pallas_call | solution.py:285
  109.2 1.9 collective-permute-start.4
  111.2 6.0 %collective-permute-done.4.x_ref = bf16[128,1024]{1,0:T(8,128)(2,1)S(1)} collective-permute-done((bf16[128,1024]{1,0:T(8,128)(2,1)}, bf16[128,1024]{1,0:T(8,128)(2,1)S(1)}, u32[]{:S(2)}, u32[]{:S(2)}) %collective-permute-start.4) | collective-permute-done | bytes 262176 | tf_op jit(solution)/shard_map/ppermute | solution.py:374
  117.1 0.7 copy-done.12
  117.8 2.6 %spread.3 = (bf16[128,1024]{1,0:T(8,128)(2,1)}, bf16[8,64,1024]{2,1,0:T(8,128)(2,1)}, bf16[8,64,1024]{2,1,0:T(8,128)(2,1)}) custom-call(s32[1]{0:T(128)} %bitcast.11.first_ref, bf16[128,1024]{1,0:T(8,128)(2,1)} %copy-done.12, bf16[128,1024]{1,0:T(8,128)(2,1)} %new_ref.3, f32[1,1024]{1,0:T(1,128)} %gain_ref.6), custom_call_target="tpu_custom_call" | custom-call | tf_op jit(solution)/shard_map/spread/pallas_call | solution.py:65
  120.4 20.5 %all_to_all.31.x_ref = bf16[8,64,1024]{2,1,0:T(8,128)(2,1)} all-to-all(bf16[8,64,1024]{2,1,0:T(8,128)(2,1)} %get-tuple-element.103), channel_id=1, replica_groups=mesh['section'=32,'p'=2,'g'=8] {'g'}, dimensions={0} | all-to-all | bytes 2097152 | tf_op jit(solution)/shard_map/all_to_all | solution.py:351
  141.0 3.6 %all-to-all-start.4 = ((bf16[8,64,1024]{2,1,0:T(8,128)(2,1)}), bf16[8,64,1024]{2,1,0:T(8,128)(2,1)S(1)}, u32[]{:S(2)}, u32[]{:S(2)}) async-start(bf16[8,64,1024]{2,1,0:T(8,128)(2,1)} %get-tuple-element.107), calls=%async_computation.4 | async-start | bytes 2097152 | tf_op jit(solution)/shard_map/all_to_all | solution.py:360
  144.5 3.4 %project.6 = (bf16[2,512,128]{2,1,0:T(8,128)(2,1)}, bf16[2,512,128]{2,1,0:T(8,128)(2,1)}, bf16[512,128]{1,0:T(8,128)(2,1)}) custom-call(s32[1]{0:T(128)} %bitcast.1.p_ref, bf16[8,64,1024]{2,1,0:T(8,128)(2,1)} %all_to_all.31.x_ref, bf16[1024,256]{1,0:T(8,128)(2,1)} %copy-done.1, bf16[1024,256]{1,0:T(8,128)(2,1)} %copy-done.2, ...), custom_call_target="tpu_custom_call" | custom-call | tf_op jit(solution)/shard_map/project/pallas_call | solution.py:139
  147.9 5.8 %collective-permute-start.5 = (bf16[2,512,128]{2,1,0:T(8,128)(2,1)}, bf16[2,512,128]{2,1,0:T(8,128)(2,1)S(1)}, u32[]{:S(2)}, u32[]{:S(2)}) collective-permute-start(bf16[2,512,128]{2,1,0:T(8,128)(2,1)} %get-tuple-element.109.kv_ref.kv1_ref), channel_id=1, source_target_pairs={{0,8},{8,0},{1,9},{9,1},{2,10},{10,2},{3,11},{11,3},{4,12},{12,4},... | collective-permute-start | bytes 786440 | tf_op jit(solution)/shard_map/ppermute | solution.py:297
  153.7 4.3 %attend_one_kernel.3.acc1_ref = f32[2,512,128]{2,1,0:T(8,128)} custom-call(f32[2]{0:T(128)} %broadcast_select_fusion.rep_ref, s32[1024,128]{1,0:T(8,128)} %get-tuple-element.98.qpos_ref, s32[1024,128]{1,0:T(8,128)} %get-tuple-element.99.qitm_ref, bf16[2,1024,128]{2,1,0:T(8,128)(2,1)} %get-tuple-element.100.ko_ref, ...), custom_call_target="tpu_custom_call" | custom-call | tf_op jit(solution)/shard_map/attend_one_kernel/pallas_call | solution.py:238
  158.0 2.0 all-to-all-done.4.x_ref
  159.9 1.0 copy-done.4
  160.9 3.4 %project.7 = (bf16[2,512,128]{2,1,0:T(8,128)(2,1)}, bf16[2,512,128]{2,1,0:T(8,128)(2,1)}, bf16[512,128]{1,0:T(8,128)(2,1)}) custom-call(s32[1]{0:T(128)} %bitcast.1.p_ref, bf16[8,64,1024]{2,1,0:T(8,128)(2,1)} %copy-done.4, bf16[1024,256]{1,0:T(8,128)(2,1)} %copy-done.1, bf16[1024,256]{1,0:T(8,128)(2,1)} %copy-done.2, ...), custom_call_target="tpu_custom_call" | custom-call | tf_op jit(solution)/shard_map/project/pallas_call | solution.py:139
  164.3 6.0 %collective-permute-start.6 = (bf16[2,512,128]{2,1,0:T(8,128)(2,1)}, bf16[2,512,128]{2,1,0:T(8,128)(2,1)S(1)}, u32[]{:S(2)}, u32[]{:S(2)}) collective-permute-start(bf16[2,512,128]{2,1,0:T(8,128)(2,1)} %get-tuple-element.113.kv2_ref), channel_id=1, source_target_pairs={{0,8},{8,0},{1,9},{9,1},{2,10},{10,2},{3,11},{11,3},{4,12},{12,4},... | collective-permute-start | bytes 786440 | tf_op jit(solution)/shard_map/ppermute | solution.py:297
  170.4 0.7 copy-done.9
  171.1 7.4 %attend_two_kernel.3.acc_ref = f32[2,1024,128]{2,1,0:T(8,128)} custom-call(f32[2]{0:T(128)} %broadcast_select_fusion.rep_ref, s32[1024,128]{1,0:T(8,128)} %get-tuple-element.98.qpos_ref, s32[1024,128]{1,0:T(8,128)} %get-tuple-element.99.qitm_ref, bf16[2,1024,128]{2,1,0:T(8,128)(2,1)} %get-tuple-element.100.ko_ref, ...), custom_call_target="tpu_custom_call" | custom-call | tf_op jit(solution)/shard_map/attend_two_kernel/pallas_call | solution.py:238
  178.5 0.7 copy-done.8
  179.2 4.5 %attend_three_kernel.3 = bf16[8,128,256]{2,1,0:T(8,128)(2,1)} custom-call(f32[2]{0:T(128)} %broadcast_select_fusion.rep_ref, s32[1]{0:T(128)} %bitcast.1.p_ref, s32[1024,128]{1,0:T(8,128)} %get-tuple-element.98.qpos_ref, s32[1024,128]{1,0:T(8,128)} %get-tuple-element.99.qitm_ref, bf16[2,1024,128]{2,1,0:T(8,128)(2,1)} %get-tuple-element.100.ko_ref, ...), custom_call_target="tpu_custom_call" | custom-call | tf_op jit(solution)/shard_map/attend_three_kernel/pallas_call | solution.py:238
  183.7 14.1 %all_to_all.32.r_ref = bf16[8,128,256]{2,1,0:T(8,128)(2,1)} all-to-all(bf16[8,128,256]{2,1,0:T(8,128)(2,1)} %attend_three_kernel.3), channel_id=1, replica_groups=mesh['section'=32,'p'=2,'g'=8] {'g'}, dimensions={0} | all-to-all | bytes 1048576 | tf_op jit(solution)/shard_map/all_to_all | solution.py:369
  197.8 3.3 %finish_last.1 = bf16[2,128,1024]{2,1,0:T(8,128)(2,1)} custom-call(bf16[128,1024]{1,0:T(8,128)(2,1)} %finish.1.before_ref, bf16[8,128,256]{2,1,0:T(8,128)(2,1)} %all_to_all.32.r_ref, bf16[128,1024]{1,0:T(8,128)(2,1)} %get-tuple-element.116.x_ref, bf16[1024,1024]{1,0:T(8,128)(2,1)} %bitcast.23, f32[1,1024]{1,0:T(1,128)} %gain_ref.7), custom_call_target="tpu_custom_call" | custom-call | tf_op jit(solution)/shard_map/finish_last/pallas_call | solution.py:285
  (60 shorter events, 2.0 us)
Async XLA Ops:
  6.5 17.1 %copy-start = (bf16[1,16,64]{2,1,0:T(8,128)(2,1)S(1)}, bf16[1,16,64]{2,1,0:T(8,128)(2,1)}, u32[]{:S(2)}) copy-start(bf16[1,16,64]{2,1,0:T(8,128)(2,1)} %param.23) | copy-start | bytes 6148
  6.5 8.8 %slice-start = ((bf16[1,1024,192]{1,2,0:T(8,128)(2,1)}), bf16[1,1024,128]{1,2,0:T(8,128)(2,1)S(1)}, s32[]{:S(2)}) async-start(bf16[1,1024,192]{1,2,0:T(8,128)(2,1)} %param.18), calls=%async_computation.7 | async-start | bytes 524288 | tf_op jit(solution)/shard_map/slice | solution.py:323
  6.5 9.0 %copy-start.13 = (bf16[1,1024,64]{1,2,0:T(8,128)(2,1)S(1)}, bf16[1,1024,64]{1,2,0:T(8,128)(2,1)}, u32[]{:S(2)}) copy-start(bf16[1,1024,64]{1,2,0:T(8,128)(2,1)} %param.19) | copy-start | bytes 393220
  6.5 99.5 %all-gather.3.cloned.1.call-start = ((), (), s32[]{:S(2)}) async-start(), calls=%async_computation.6 | async-start | bytes 2228224 | tf_op jit(solution)/shard_map/all_gather | solution.py:322
  7.3 8.5 %slice-start.1 = ((bf16[1,1024,192]{1,2,0:T(8,128)(2,1)}), bf16[1,1024,64]{1,2,0:T(8,128)(2,1)S(1)}, s32[]{:S(2)}) async-start(bf16[1,1024,192]{1,2,0:T(8,128)(2,1)} %param.18), calls=%async_computation.8 | async-start | bytes 262144 | tf_op jit(solution)/shard_map/slice | solution.py:323
  9.9 37.6 %all-to-all-start = ((bf16[8,64,1024]{2,1,0:T(8,128)(2,1)}), bf16[8,64,1024]{2,1,0:T(8,128)(2,1)S(1)}, u32[]{:S(2)}, u32[]{:S(2)}) async-start(bf16[8,64,1024]{2,1,0:T(8,128)(2,1)} %get-tuple-element.61), calls=%async_computation | async-start | bytes 2097152 | tf_op jit(solution)/shard_map/all_to_all | solution.py:351
  15.3 5.6 %copy-start.6 = (bf16[1,768,1,128]{3,1,2,0:T(8,128)(2,1)S(1)}, bf16[1,768,1,128]{3,1,2,0:T(8,128)(2,1)}, u32[]{:S(2)}) copy-start(bf16[1,768,1,128]{3,1,2,0:T(8,128)(2,1)} %param.25) | copy-start | bytes 589828
  15.3 8.3 %copy-start.14 = (s32[1,2,2048]{2,1,0:T(2,128)S(1)}, s32[1,2,2048]{2,1,0:T(2,128)}, u32[]{:S(2)}) copy-start(s32[1,2,2048]{2,1,0:T(2,128)} %param.28) | copy-start | bytes 49156
  15.3 8.3 %copy-start.15 = (s32[1,2,2048]{2,1,0:T(2,128)S(1)}, s32[1,2,2048]{2,1,0:T(2,128)}, u32[]{:S(2)}) copy-start(s32[1,2,2048]{2,1,0:T(2,128)} %param.27) | copy-start | bytes 49156
  15.3 8.3 %copy-start.16 = (s32[1,2,2048]{2,1,0:T(2,128)S(1)}, s32[1,2,2048]{2,1,0:T(2,128)}, u32[]{:S(2)}) copy-start(s32[1,2,2048]{2,1,0:T(2,128)} %param.26) | copy-start | bytes 49156
  15.4 17.0 %copy-start.19 = (f32[1,16]{1,0:T(1,128)S(1)}, f32[1,16]{1,0:T(1,128)}, u32[]{:S(2)}) copy-start(f32[1,16]{1,0:T(1,128)} %param.24) | copy-start | bytes 196
  15.4 18.1 %copy-start.17 = (s32[1,768]{1,0:T(1,128)S(1)}, s32[1,768]{1,0:T(1,128)}, u32[]{:S(2)}) copy-start(s32[1,768]{1,0:T(1,128)} %param.31) | copy-start | bytes 9220
  15.4 18.0 %copy-start.18 = (s32[1,768]{1,0:T(1,128)S(1)}, s32[1,768]{1,0:T(1,128)}, u32[]{:S(2)}) copy-start(s32[1,768]{1,0:T(1,128)} %param.29) | copy-start | bytes 9220
  16.2 36.1 %copy-start.1 = (bf16[1024,256]{1,0:T(8,128)(2,1)}, bf16[1024,256]{1,0:T(8,128)(2,1)S(1)}, u32[]{:S(2)}) copy-start(bf16[1024,256]{1,0:T(8,128)(2,1)S(1)} %pad_maximum_fusion.own_ref) | copy-start | bytes 1572868
  16.2 31.3 %collective-permute-start = (bf16[1024,256]{1,0:T(8,128)(2,1)S(1)}, bf16[1024,256]{1,0:T(8,128)(2,1)S(1)}, u32[]{:S(2)}, u32[]{:S(2)}) collective-permute-start(bf16[1024,256]{1,0:T(8,128)(2,1)S(1)} %pad_maximum_fusion.own_ref), channel_id=1, source_target_pairs={{0,8},{8,0},{1,9},{9,1},{2,10},{10,2},{3,11},{11,3},{4,12},{12,4},... | collective-permute-start | bytes 1572872 | tf_op jit(solution)/shard_map/ppermute | solution.py:297
  20.9 26.7 %collective-permute-start.1 = (bf16[768,128]{1,0:T(8,128)(2,1)S(1)}, bf16[768,128]{1,0:T(8,128)(2,1)S(1)}, u32[]{:S(2)}, u32[]{:S(2)}) collective-permute-start(bf16[768,128]{1,0:T(8,128)(2,1)S(1)} %bitcast.28), channel_id=1, source_target_pairs={{0,8},{8,0},{1,9},{9,1},{2,10},{10,2},{3,11},{11,3},{4,12},{12,4},... | collective-permute-start | bytes 589832 | tf_op jit(solution)/shard_map/ppermute | solution.py:297
  47.5 8.2 %copy-start.7 = (bf16[768,128]{1,0:T(8,128)(2,1)}, bf16[768,128]{1,0:T(8,128)(2,1)S(1)}, u32[]{:S(2)}) copy-start(bf16[768,128]{1,0:T(8,128)(2,1)S(1)} %collective-permute-done.1.cother_ref) | copy-start | bytes 589828
  47.5 4.8 %copy-start.2 = (bf16[1024,256]{1,0:T(8,128)(2,1)}, bf16[1024,256]{1,0:T(8,128)(2,1)S(1)}, u32[]{:S(2)}) copy-start(bf16[1024,256]{1,0:T(8,128)(2,1)S(1)} %collective-permute-done.other_ref) | copy-start | bytes 1572868
  47.5 4.8 %copy-start.3 = (bf16[8,64,1024]{2,1,0:T(8,128)(2,1)}, bf16[8,64,1024]{2,1,0:T(8,128)(2,1)S(1)}, u32[]{:S(2)}) copy-start(bf16[8,64,1024]{2,1,0:T(8,128)(2,1)S(1)} %all-to-all-done.x_ref) | copy-start | bytes 3145732
  47.6 22.2 %all-to-all-start.1 = ((bf16[8,64,1024]{2,1,0:T(8,128)(2,1)}), bf16[8,64,1024]{2,1,0:T(8,128)(2,1)S(1)}, u32[]{:S(2)}, u32[]{:S(2)}) async-start(bf16[8,64,1024]{2,1,0:T(8,128)(2,1)} %get-tuple-element.86), calls=%async_computation.1 | async-start | bytes 2097152 | tf_op jit(solution)/shard_map/all_to_all | solution.py:360
  55.8 22.7 %collective-permute-start.2 = (bf16[2,512,128]{2,1,0:T(8,128)(2,1)}, bf16[2,512,128]{2,1,0:T(8,128)(2,1)S(1)}, u32[]{:S(2)}, u32[]{:S(2)}) collective-permute-start(bf16[2,512,128]{2,1,0:T(8,128)(2,1)} %get-tuple-element.90.kv_ref.kv1_ref), channel_id=1, source_target_pairs={{0,8},{8,0},{1,9},{9,1},{2,10},{10,2},{3,11},{11,3},{4,12},{12,4},... | collective-permute-start | bytes 786440 | tf_op jit(solution)/shard_map/ppermute | solution.py:297
  69.8 1.0 copy-start.5
  74.2 12.4 %collective-permute-start.3 = (bf16[2,512,128]{2,1,0:T(8,128)(2,1)}, bf16[2,512,128]{2,1,0:T(8,128)(2,1)S(1)}, u32[]{:S(2)}, u32[]{:S(2)}) collective-permute-start(bf16[2,512,128]{2,1,0:T(8,128)(2,1)} %get-tuple-element.94.kv2_ref), channel_id=1, source_target_pairs={{0,8},{8,0},{1,9},{9,1},{2,10},{10,2},{3,11},{11,3},{4,12},{12,4},... | collective-permute-start | bytes 786440 | tf_op jit(solution)/shard_map/ppermute | solution.py:297
  78.5 0.7 copy-start.11
  86.6 0.7 copy-start.10
  109.2 7.9 %collective-permute-start.4 = (bf16[128,1024]{1,0:T(8,128)(2,1)}, bf16[128,1024]{1,0:T(8,128)(2,1)S(1)}, u32[]{:S(2)}, u32[]{:S(2)}) collective-permute-start(bf16[128,1024]{1,0:T(8,128)(2,1)} %finish.1.before_ref), channel_id=1, source_target_pairs={{0,16},{16,32},{32,48},{48,64},{64,80},{80,96},{96,112},{112,128},... | collective-permute-start | bytes 786440 | tf_op jit(solution)/shard_map/ppermute | solution.py:374
  117.1 0.7 copy-start.12
  141.0 19.0 %all-to-all-start.4 = ((bf16[8,64,1024]{2,1,0:T(8,128)(2,1)}), bf16[8,64,1024]{2,1,0:T(8,128)(2,1)S(1)}, u32[]{:S(2)}, u32[]{:S(2)}) async-start(bf16[8,64,1024]{2,1,0:T(8,128)(2,1)} %get-tuple-element.107), calls=%async_computation.4 | async-start | bytes 2097152 | tf_op jit(solution)/shard_map/all_to_all | solution.py:360
  147.9 22.4 %collective-permute-start.5 = (bf16[2,512,128]{2,1,0:T(8,128)(2,1)}, bf16[2,512,128]{2,1,0:T(8,128)(2,1)S(1)}, u32[]{:S(2)}, u32[]{:S(2)}) collective-permute-start(bf16[2,512,128]{2,1,0:T(8,128)(2,1)} %get-tuple-element.109.kv_ref.kv1_ref), channel_id=1, source_target_pairs={{0,8},{8,0},{1,9},{9,1},{2,10},{10,2},{3,11},{11,3},{4,12},{12,4},... | collective-permute-start | bytes 786440 | tf_op jit(solution)/shard_map/ppermute | solution.py:297
  159.9 1.0 copy-start.4
  164.3 14.1 %collective-permute-start.6 = (bf16[2,512,128]{2,1,0:T(8,128)(2,1)}, bf16[2,512,128]{2,1,0:T(8,128)(2,1)S(1)}, u32[]{:S(2)}, u32[]{:S(2)}) collective-permute-start(bf16[2,512,128]{2,1,0:T(8,128)(2,1)} %get-tuple-element.113.kv2_ref), channel_id=1, source_target_pairs={{0,8},{8,0},{1,9},{9,1},{2,10},{10,2},{3,11},{11,3},{4,12},{12,4},... | collective-permute-start | bytes 786440 | tf_op jit(solution)/shard_map/ppermute | solution.py:297
  170.4 0.7 copy-start.9
  178.5 0.7 copy-start.8
Sparse Core Ops, SparseCore 0:
  10.4 70.8 all-gather.2

commit v3 on v1

v3 whole, which is shorter than its diff:
```python
import functools

import jax
import jax.numpy as jnp
from jax import lax
from jax.experimental import pallas as pl
from jax.experimental.pallas import tpu as pltpu
from jax.sharding import Mesh, PartitionSpec as P

D = 1024
H = 16
DH = 64
NB = 64
TICKS = 2
CACHE = 768
SLICE = 2048
NK = CACHE + SLICE
EPSILON = 1e-05
NP = 2
NG = 8
ROWS = SLICE // (NP * NG)
BAND = SLICE // NP
KBLOCK = 256
BF16 = jnp.bfloat16
F32 = jnp.float32
VMEM_LIMIT = 24 * 1024 * 1024


def silu(v):
    half = 0.5 * v
    return half + half * jnp.tanh(half)


def vmem():
    return pl.BlockSpec(memory_space=pltpu.VMEM)


def smem():
    return pl.BlockSpec(memory_space=pltpu.SMEM)


def params():
    return pltpu.CompilerParams(vmem_limit_bytes=VMEM_LIMIT)


def low_lanes(rows):
    return lax.broadcasted_iota(jnp.int32, (rows, 2 * DH), 1) < DH


def spread_kernel(first_ref, x_ref, new_ref, gain_ref, here_ref, out_ref):
    fresh = jnp.full((ROWS, 1), first_ref[0], jnp.int32) > 0
    here = jnp.where(fresh, new_ref[...].astype(F32), x_ref[...].astype(F32))
    here_ref[...] = here.astype(BF16)
    mean = jnp.mean(here, axis=-1, keepdims=True)
    variance = jnp.mean(here * here, axis=-1, keepdims=True) - mean * mean
    normed = ((here - mean) * lax.rsqrt(variance + EPSILON) * gain_ref[...]).astype(BF16)
    for k in range(NG):
        out_ref[k] = normed


def spread(*operands):
    return pl.pallas_call(
        spread_kernel,
        out_shape=(jax.ShapeDtypeStruct((ROWS, D), BF16), jax.ShapeDtypeStruct((NG, ROWS, D), BF16)),
        in_specs=[smem()] + [vmem()] * 3,
        out_specs=(vmem(),) * 2,
        compiler_params=params(),
        name="spread",
    )(*operands)


def column(row):
    return jnp.transpose(jnp.broadcast_to(row, (128, row.shape[1])))


def prepare(tick, p_ref, pos_ref, bkt_ref, itm_ref, table_ref, qg_ref, cbkt_ref, far, qpos, qitm, lhs, ko, krow, cko):
    lane = lax.broadcasted_iota(jnp.int32, (BAND, 128), 1)
    flip = jnp.full((1, BAND), p_ref[0], jnp.int32) > 0

    def bands(ref):
        low, high = ref[tick : tick + 1, :BAND], ref[tick : tick + 1, BAND:]
        return jnp.where(flip, high, low), jnp.where(flip, low, high)

    pos, bkt, itm = bands(pos_ref), bands(bkt_ref), bands(itm_ref)
    qpos[...] = column(pos[0])
    qitm[...] = column(itm[0])
    krow[0:1, :] = pos[far]
    krow[1:2, :] = itm[far]
    level = column(bkt[0])
    onehot = jnp.where(level == lane, 1.0, 0.0).astype(BF16)
    for h in range(NP):
        bias = jnp.dot(onehot, table_ref[h], preferred_element_type=F32)
        lhs[h] = jnp.where(lane < DH, qg_ref[h].astype(F32), bias).astype(BF16)
    level = column(bkt[1]) if far else level
    ko[...] = jnp.where(level == lane - DH, 1.0, 0.0).astype(BF16)
    if not far:
        cko[...] = jnp.where(column(cbkt_ref[...]) == lane[:CACHE] - DH, 1.0, 0.0).astype(BF16)


def project_kernel(x_ref, own_ref, other_ref, qg_ref, kv_ref, token_ref):
    token_ref[...] = jnp.zeros((8, 128), F32)
    normed = x_ref[...].reshape(BAND, D)
    scale = jnp.where(low_lanes(BAND), 0.5, 1.0)
    for h, w_ref in enumerate((own_ref, other_ref)):
        z = silu(jnp.dot(normed, w_ref[...], preferred_element_type=F32))
        kv_ref[h] = z[:, 2 * DH :].astype(BF16)
        qg_ref[h] = (z[:, : 2 * DH] * scale).astype(BF16)


def project(*operands):
    return pl.pallas_call(
        project_kernel,
        out_shape=(
            jax.ShapeDtypeStruct((NP, BAND, 2 * DH), BF16),
            jax.ShapeDtypeStruct((NP, BAND, 2 * DH), BF16),
            jax.ShapeDtypeStruct((8, 128), F32),
        ),
        in_specs=[vmem()] * 3,
        out_specs=(vmem(),) * 3,
        compiler_params=params(),
        name="project",
    )(*operands)


def add_keys(rep_ref, lhs_ref, qpos_ref, qitm_ref, same, allowed, acc, kv_refs, ko_ref, kpos_ref, kitm_ref, start):
    low = low_lanes(KBLOCK)
    for c in range(kv_refs[0].shape[0] // KBLOCK):
        ks = slice(c * KBLOCK, (c + 1) * KBLOCK)
        wide = jnp.concatenate([qitm_ref[...]] * (KBLOCK // 128), axis=1)
        same[...] = jnp.where(wide == kitm_ref[:, ks], 1.0, 0.0)
        wide = jnp.concatenate([qpos_ref[...]] * (KBLOCK // 128), axis=1)
        allowed[...] = jnp.where(kpos_ref[:, ks] <= wide, 1.0, 0.0).astype(BF16)
        for h in range(NP):
            kv = kv_refs[h][ks, :]
            keys = jnp.where(low, kv, ko_ref[ks, :])
            half = lax.dot_general(lhs_ref[h], keys, (((1,), (1,)), ((), ())), preferred_element_type=F32)
            half = half + (0.5 * rep_ref[h]) * same[...]
            weight = (half + half * jnp.tanh(half)).astype(BF16) * allowed[...]
            part = jnp.dot(weight, kv, preferred_element_type=F32)
            if c == 0 and start is None:
                acc[h] = part
            else:
                acc[h] = (acc if start is None or c else start)[h] + part


def early_kernel(tick, rep_ref, p_ref, pos_ref, bkt_ref, itm_ref, table_ref, qg_ref, kv_ref, cpos_ref, cbkt_ref, citm_ref, cown_ref, cother_ref, acc, qpos, qitm, lhs, ko, krow, same, allowed, cko):
    prepare(tick, p_ref, pos_ref, bkt_ref, itm_ref, table_ref, qg_ref, cbkt_ref, 0, qpos, qitm, lhs, ko, krow, cko)
    shared = (rep_ref, lhs, qpos, qitm, same, allowed, acc)
    add_keys(*shared, (kv_ref.at[0], kv_ref.at[1]), ko, krow.at[0:1], krow.at[1:2], None)
    add_keys(*shared, (cown_ref, cother_ref), cko, cpos_ref, citm_ref, acc)


def late_kernel(tick, rep_ref, p_ref, pos_ref, bkt_ref, itm_ref, table_ref, qg_ref, acc_ref, far_ref, out_ref, qpos, qitm, lhs, ko, krow, same, allowed, acc):
    prepare(tick, p_ref, pos_ref, bkt_ref, itm_ref, table_ref, qg_ref, None, 1, qpos, qitm, lhs, ko, krow, None)
    shared = (rep_ref, lhs, qpos, qitm, same, allowed, acc)
    add_keys(*shared, (far_ref.at[1], far_ref.at[0]), ko, krow.at[0:1], krow.at[1:2], acc_ref)
    low = low_lanes(BAND)
    out_ref[:, : 2 * DH] = (jnp.where(low, pltpu.roll(acc[0], DH, 1), acc[1]) * (1.0 / NK)).astype(BF16)
    gate = jnp.where(low, pltpu.roll(qg_ref[0].astype(F32), DH, 1), qg_ref[1].astype(F32))
    out_ref[:, 2 * DH :] = gate.astype(BF16)


SCRATCH = [
    pltpu.VMEM((BAND, 128), jnp.int32),
    pltpu.VMEM((BAND, 128), jnp.int32),
    pltpu.VMEM((NP, BAND, 2 * DH), BF16),
    pltpu.VMEM((BAND, 128), BF16),
    pltpu.VMEM((8, BAND), jnp.int32),
    pltpu.VMEM((BAND, KBLOCK), F32),
    pltpu.VMEM((BAND, KBLOCK), BF16),
]
ACC = pltpu.VMEM((NP, BAND, 2 * DH), F32)
CACHE_BUCKETS = pltpu.VMEM((CACHE, 128), BF16)


def attend(kernel, tick, shape, dtype, scratch, *operands):
    return pl.pallas_call(
        functools.partial(kernel, tick),
        out_shape=jax.ShapeDtypeStruct(shape, dtype),
        in_specs=[smem() if a.ndim == 1 else vmem() for a in operands],
        out_specs=vmem(),
        scratch_shapes=scratch,
        compiler_params=params(),
        name="attend_" + kernel.__name__,
    )(*operands)


def finish_rows(r_ref, x_ref, w_ref, gain_ref, mixed):
    total = jnp.zeros((ROWS, 2 * DH), F32)
    square = jnp.zeros((ROWS, 2 * DH), F32)
    for k in range(NG):
        a = r_ref[k, :, : 2 * DH].astype(F32)
        total += a
        square += a * a
    mean = jnp.sum(total, axis=-1, keepdims=True) * (1.0 / D)
    variance = jnp.sum(square, axis=-1, keepdims=True) * (1.0 / D) - mean * mean
    scale = lax.rsqrt(variance + EPSILON)
    for k in range(NG):
        cols = slice(k * 2 * DH, (k + 1) * 2 * DH)
        r = r_ref[k].astype(F32)
        mixed[:, cols] = ((r[:, : 2 * DH] - mean) * scale * gain_ref[:, cols] * r[:, 2 * DH :]).astype(BF16)
    y = jnp.dot(mixed[...], w_ref[...], preferred_element_type=F32)
    return (x_ref[...].astype(F32) + y).astype(BF16)


def finish_kernel(r_ref, x_ref, w_ref, gain_ref, out_ref, mixed):
    out_ref[...] = finish_rows(r_ref, x_ref, w_ref, gain_ref, mixed)


def last_kernel(before_ref, r_ref, x_ref, w_ref, gain_ref, out_ref, mixed):
    out_ref[0] = before_ref[...]
    out_ref[1] = finish_rows(r_ref, x_ref, w_ref, gain_ref, mixed)


def finish(*operands):
    last = len(operands) == 5
    return pl.pallas_call(
        last_kernel if last else finish_kernel,
        out_shape=jax.ShapeDtypeStruct((TICKS, ROWS, D) if last else (ROWS, D), BF16),
        in_specs=[vmem()] * len(operands),
        out_specs=vmem(),
        scratch_shapes=[pltpu.VMEM((ROWS, D), BF16)],
        compiler_params=params(),
        name="finish_last" if last else "finish",
    )(*operands)


def partner(i):
    return (i // NG ^ 1) * NG + (i % NG ^ NG // 2)


def swap(x):
    return lax.ppermute(x, ("p", "g"), [(i, partner(i)) for i in range(H)])


def body(
    slices,
    new_slice,
    w_qkv,
    w_gate,
    w_out,
    input_gain,
    output_gain,
    bucket_bias,
    repeat_bias,
    cache_kv,
    slice_positions,
    slice_buckets,
    slice_items,
    cache_positions,
    cache_buckets,
    cache_items,
):
    p = lax.axis_index("p")
    g = lax.axis_index("g")
    section = lax.axis_index("section")

    def pair(a):
        there = (1 - p) * NG + (g + NG // 2) % NG
        return jnp.concatenate([lax.dynamic_slice_in_dim(a, i, 1) for i in (p * NG + g, there)])

    gain_out = output_gain[0].reshape(NP, NG, DH)
    gain_out = jnp.where(p == 0, gain_out, gain_out[::-1])
    gain_out = jnp.stack([gain_out[0], jnp.roll(gain_out[1], NG // 2, 0)], axis=1).reshape(1, D)
    tables = pair(bucket_bias[0])
    rep = pair(repeat_bias[0])
    levels = jnp.arange(NB, dtype=jnp.int32)
    distance = jnp.abs(levels[:, None] - levels[None, :])
    lookup = (distance[:, :, None] == levels[None, None, :]).astype(F32)
    toeplitz = jnp.einsum("abc,hc->hab", lookup, tables.astype(F32)).astype(BF16)
    toeplitz = jnp.pad(0.5 * toeplitz, ((0, 0), (0, DH), (DH, 0)))
    p_word = p.astype(jnp.int32).reshape(1)
    received = slices[0]
    first = jnp.zeros((1,), jnp.int32)
    produced = ()
    for tick in range(TICKS):
        current, copies = spread(first, received, new_slice, input_gain)
        if tick == 0:
            copies, w_qkv, w_gate, w_out, cache_kv = lax.optimization_barrier((copies, w_qkv, w_gate, w_out, cache_kv))
            w_own = jnp.concatenate([w_qkv[0, :, :DH], w_gate[0], w_qkv[0, :, DH:]], axis=1)
            w_other = swap(w_own)
            c_own = cache_kv[0, :, 0, :]
            c_other = swap(c_own)
            w_pair = jnp.concatenate([w_out[0], swap(w_out[0])])
            w_copies = jnp.broadcast_to(w_pair[None], (NG, 2 * DH, D))
        band = lax.all_to_all(copies, "g", 0, 0)
        if tick == 0:
            band, w_own, w_other, c_other, rep, toeplitz, gain_out, w_copies = lax.optimization_barrier(
                (band, w_own, w_other, c_other, rep, toeplitz, gain_out, w_copies)
            )
        qg, kv, token = project(band, w_own, w_other)
        far = swap(kv)
        if tick == 0:
            w_copies, token = lax.optimization_barrier((w_copies, token))
            w_out_full = lax.all_to_all(w_copies, "g", 0, 0).reshape(D, D)
        keyed = (tick, (NP, BAND, 2 * DH), F32, SCRATCH + [CACHE_BUCKETS])
        given = (rep, p_word, slice_positions[0], slice_buckets[0], slice_items[0], toeplitz, qg)
        acc = attend(early_kernel, *keyed, *given, kv, cache_positions, cache_buckets, cache_items, c_own, c_other)
        a = attend(late_kernel, tick, (BAND, 4 * DH), BF16, SCRATCH + [ACC], *given, acc, far)
        if tick == 0:
            a, w_out_full = lax.optimization_barrier((a, w_out_full))
        back = lax.all_to_all(a.reshape(NG, ROWS, 4 * DH), "g", 0, 0)
        if tick + 1 < TICKS:
            one = finish(back, current, w_out_full, gain_out)
            produced = (one,)
            count = lax.axis_size("section")
            received = lax.ppermute(one, "section", [(s, s + 1) for s in range(count - 1)])
            first = (section == 0).astype(jnp.int32).reshape(1)
    return finish(*produced, back, current, w_out_full, gain_out)[None]


def solution(mesh):
    sections = mesh.shape["section"]
    grid = Mesh(mesh.devices.reshape(sections, NP, NG), ("section", "p", "g"))
    seq = ("p", "g")
    in_specs = (
        P("section", seq, None),
        P(seq, None),
        P("section", None, seq),
        P("section", None, seq),
        P("section", seq, None),
        P("section", None),
        P("section", None),
        P("section", None, None),
        P("section", None),
        P("section", None, seq, None),
        P("section", None, None),
        P("section", None, None),
        P("section", None, None),
        P("section", None),
        P("section", None),
        P("section", None),
    )
    out_specs = P("section", None, seq, None)
    return jax.shard_map(body, mesh=grid, in_specs=in_specs, out_specs=out_specs, check_vma=False)
```

time: 203 us -> 160 us (0.79)
  the two profiles are of different devices: /device:TPU:96 before, /device:TPU:228 now
where the time goes in v3:
time: 160 us; the launch traced here: 159 us
  blocking collectives  58.1 us (36%)
  waiting for transfers between devices  29.3 us (18%)
  starting transfers between devices  26 us (16%)
  Pallas kernels  25.9 us (16%)
  local copies, waits for them, and re-layouts  14.3 us (9%)
  other arithmetic  3.93 us (2%)
    all_to_all x1, blocking collectives, body(): band = lax.all_to_all(copies, 'g', 0, 0)  30.3 us
    all_to_all x2, blocking collectives, body(): back = lax.all_to_all(a.reshape(NG, ROWS, 4 * DH), 'g', 0, 0)  27.8 us
    pallas_call x4, Pallas kernels, attend(): pl.pallas_call(functools.partial(kernel, tick), out_shape=jax.ShapeDtypeS...  19.2 us
    ppermute x5, waiting for transfers between devices, swap(): return lax.ppermute(x, ('p', 'g'), [(i, partner(i)) for i in range(H)])  17.5 us
    ppermute x5, starting transfers between devices, swap(): return lax.ppermute(x, ('p', 'g'), [(i, partner(i)) for i in range(H)])  14.5 us
    unnamed x47, local copies, waits for them, and re-layouts  8.56 us
    ppermute x1, waiting for transfers between devices, body(): lax.ppermute(one, 'section', [(s, s + 1) for s in range(count - 1)])  5.76 us
    all_to_all x1, starting transfers between devices, body(): band = lax.all_to_all(copies, 'g', 0, 0)  5.24 us
  transfers between devices with their start and end apart: 8, of which 6 were waited for; matrix products, arithmetic and copies ran while one was open for 5% of the time, Pallas kernels for 11%

profile of v3, /device:TPU:228, one launch (start us, length us, event | category | flops | bytes accessed | tf_op | source)
XLA Modules:
  0.0 159.0 jit_solution(17051156172971440362)
XLA Ops:
  0.0 0.9 copy-done.5
  1.0 0.9 copy-done.14
  1.9 0.7 copy-done.15
  2.6 0.3 spread.2
  2.9 1.3 copy-done.2
  4.3 0.7 copy-done.12
  5.0 5.2 %all-to-all-start = ((bf16[8,128,1024]{2,1,0:T(8,128)(2,1)}), bf16[8,128,1024]{2,1,0:T(8,128)(2,1)S(1)}, u32[]{:S(2)}, u32[]{:S(2)}) async-start(bf16[8,128,1024]{2,1,0:T(8,128)(2,1)} %copy-done.2), calls=%async_computation | async-start | bytes 4194304 | tf_op jit(solution)/shard_map/all_to_all | solution.py:286
  10.2 3.4 %collective-permute-start.2 = (bf16[64,1024]{1,0:T(8,128)(2,1)}, bf16[64,1024]{1,0:T(8,128)(2,1)}, u32[]{:S(2)}, u32[]{:S(2)}) collective-permute-start(bf16[64,1024]{1,0:T(8,128)(2,1)} %bitcast.15), channel_id=1, source_target_pairs={{0,12},{1,13},{2,14},{3,15},{4,8},{5,9},{6,10},{7,11},{8,4},{9,5},... | collective-permute-start | bytes 393224 | tf_op jit(solution)/shard_map/ppermute | solution.py:233
  13.6 2.5 %collective-permute-start.1 = (bf16[768,128]{1,0:T(8,128)(2,1)S(1)}, bf16[768,128]{1,0:T(8,128)(2,1)}, u32[]{:S(2)}, u32[]{:S(2)}) collective-permute-start(bf16[768,128]{1,0:T(8,128)(2,1)S(1)} %bitcast.38), channel_id=1, source_target_pairs={{0,12},{1,13},{2,14},{3,15},{4,8},{5,9},{6,10},{7,11},{8,4},{9,5},... | collective-permute-start | bytes 589832 | tf_op jit(solution)/shard_map/ppermute | solution.py:233
  16.1 0.2 copy.18
  16.3 1.2 copy.17
  17.5 0.1 slice_bitcast_fusion
  17.7 0.2 pad_maximum_fusion.own_ref
  17.9 3.4 %collective-permute-start = (bf16[1024,256]{1,0:T(8,128)(2,1)S(1)}, bf16[1024,256]{1,0:T(8,128)(2,1)S(1)}, u32[]{:S(2)}, u32[]{:S(2)}) collective-permute-start(bf16[1024,256]{1,0:T(8,128)(2,1)S(1)} %pad_maximum_fusion.own_ref), channel_id=1, source_target_pairs={{0,12},{1,13},{2,14},{3,15},{4,8},{5,9},{6,10},{7,11},{8,4},{9,5},... | collective-permute-start | bytes 1572872 | tf_op jit(solution)/shard_map/ppermute | solution.py:233
  21.3 0.5 broadcast.12
  21.8 0.7 reduce.3
  22.6 0.7 fusion.3
  23.3 1.2 fusion
  24.6 0.1 reshape.40.gain_ref
  24.7 0.6 constant_dynamic-slice_fusion.3
  25.3 1.3 pad_maximum_fusion.4.rep_ref
  26.6 1.7 %pad_maximum_fusion.1 = bf16[128,1024]{1,0:T(8,128)(2,1)} fusion(bf16[64,1024]{1,0:T(8,128)(2,1)} %collective-permute-done.2, bf16[64,1024]{1,0:T(8,128)(2,1)} %bitcast.15), kind=kLoop, calls=%fused_computation.6 | loop fusion | flops 524288 | bytes 524288 | tf_op jit(solution)/shard_map/concatenate | solution.py:284
  28.3 4.4 %collective-permute-done.other_ref = bf16[1024,256]{1,0:T(8,128)(2,1)S(1)} collective-permute-done((bf16[1024,256]{1,0:T(8,128)(2,1)S(1)}, bf16[1024,256]{1,0:T(8,128)(2,1)S(1)}, u32[]{:S(2)}, u32[]{:S(2)}) %collective-permute-start) | collective-permute-done | bytes 524320 | tf_op jit(solution)/shard_map/ppermute | solution.py:233
  32.7 3.5 %all-to-all-done.x_ref = bf16[8,128,1024]{2,1,0:T(8,128)(2,1)S(1)} async-done(((bf16[8,128,1024]{2,1,0:T(8,128)(2,1)}), bf16[8,128,1024]{2,1,0:T(8,128)(2,1)S(1)}, u32[]{:S(2)}, u32[]{:S(2)}) %all-to-all-start) | async-done | bytes 2097184 | tf_op jit(solution)/shard_map/all_to_all | solution.py:286
  36.2 2.7 %broadcast_in_dim.4 = bf16[8,128,1024]{2,1,0:T(8,128)(2,1)} broadcast(bf16[128,1024]{1,0:T(8,128)(2,1)} %pad_maximum_fusion.1), dimensions={1,2} | broadcast | bytes 2359296 | tf_op jit(solution)/shard_map/broadcast_in_dim | solution.py:285
  39.0 4.4 %all-to-all-start.1 = ((bf16[8,128,1024]{2,1,0:T(8,128)(2,1)}), bf16[8,128,1024]{2,1,0:T(8,128)(2,1)S(1)}, u32[]{:S(2)}, u32[]{:S(2)}) async-start(bf16[8,128,1024]{2,1,0:T(8,128)(2,1)} %broadcast_in_dim.4), calls=%async_computation.1 | async-start | bytes 4194304 | tf_op jit(solution)/shard_map/all_to_all | solution.py:295
  43.3 1.6 copy-done.1
  44.9 2.0 %project.2 = (bf16[2,1024,128]{2,1,0:T(8,128)(2,1)S(1)}, bf16[2,1024,128]{2,1,0:T(8,128)(2,1)S(1)}, f32[8,128]{1,0:T(8,128)}) custom-call(bf16[8,128,1024]{2,1,0:T(8,128)(2,1)S(1)} %copy-done.1, bf16[1024,256]{1,0:T(8,128)(2,1)S(1)} %pad_maximum_fusion.own_ref, bf16[1024,256]{1,0:T(8,128)(2,1)S(1)} %collective-permute-done.other_ref), custom_call_target="tpu_custom_call" | custom-call | tf_op jit(solution)/shard_map/project/pallas_call | solution.py:111
  47.0 0.8 copy-done.3
  47.8 2.8 %collective-permute-start.3 = (bf16[2,1024,128]{2,1,0:T(8,128)(2,1)S(1)}, bf16[2,1024,128]{2,1,0:T(8,128)(2,1)S(1)}, u32[]{:S(2)}, u32[]{:S(2)}) collective-permute-start(bf16[2,1024,128]{2,1,0:T(8,128)(2,1)S(1)} %get-tuple-element.40.kv_ref), channel_id=1, source_target_pairs={{0,12},{1,13},{2,14},{3,15},{4,8},{5,9},{6,10},{7,11},{8,4},{9,5},... | collective-permute-start | bytes 1572872 | tf_op jit(solution)/shard_map/ppermute | solution.py:233
  50.6 5.8 %attend_early_kernel.2.acc_ref = f32[2,1024,128]{2,1,0:T(8,128)S(1)} custom-call(f32[2]{0:T(128)S(1)} %pad_maximum_fusion.4.rep_ref, s32[1]{0:T(128)} %bitcast.16.p_ref, s32[2,2048]{1,0:T(2,128)S(1)} %bitcast.41, s32[2,2048]{1,0:T(2,128)S(1)} %bitcast.45, s32[2,2048]{1,0:T(2,128)S(1)} %bitcast.49, bf16[2,128,128]{2,1,0:T(8,128)(2,1)S(1)} %pad.4.table_ref, ...), custom_call_target="tpu_custom_call" | custom-call | tf_op jit(solution)/shard_map/attend_early_kernel/pallas_call | solution.py:177
  56.5 6.0 %collective-permute-done.3.far_ref = bf16[2,1024,128]{2,1,0:T(8,128)(2,1)S(1)} collective-permute-done((bf16[2,1024,128]{2,1,0:T(8,128)(2,1)S(1)}, bf16[2,1024,128]{2,1,0:T(8,128)(2,1)S(1)}, u32[]{:S(2)}, u32[]{:S(2)}) %collective-permute-start.3) | collective-permute-done | bytes 524320 | tf_op jit(solution)/shard_map/ppermute | solution.py:233
  62.5 3.8 %attend_late_kernel.2 = bf16[1024,256]{1,0:T(8,128)(2,1)S(1)} custom-call(f32[2]{0:T(128)S(1)} %pad_maximum_fusion.4.rep_ref, s32[1]{0:T(128)} %bitcast.16.p_ref, s32[2,2048]{1,0:T(2,128)S(1)} %bitcast.42, s32[2,2048]{1,0:T(2,128)S(1)} %bitcast.46, s32[2,2048]{1,0:T(2,128)S(1)} %bitcast.50, bf16[2,128,128]{2,1,0:T(8,128)(2,1)S(1)} %pad.4.table_ref, ...), custom_call_target="tpu_custom_call" | custom-call | tf_op jit(solution)/shard_map/attend_late_kernel/pallas_call | solution.py:177
  66.3 2.5 %all-to-all-done.1 = bf16[8,128,1024]{2,1,0:T(8,128)(2,1)S(1)} async-done(((bf16[8,128,1024]{2,1,0:T(8,128)(2,1)}), bf16[8,128,1024]{2,1,0:T(8,128)(2,1)S(1)}, u32[]{:S(2)}, u32[]{:S(2)}) %all-to-all-start.1) | async-done | bytes 2097184 | tf_op jit(solution)/shard_map/all_to_all | solution.py:295
  68.8 13.8 %all_to_all.25.r_ref = bf16[8,128,256]{2,1,0:T(8,128)(2,1)S(1)} all-to-all(bf16[8,128,256]{2,1,0:T(8,128)(2,1)S(1)} %bitcast.36), channel_id=1, replica_groups=mesh['section'=32,'p'=2,'g'=8] {'g'}, dimensions={0} | all-to-all | bytes 1048576 | tf_op jit(solution)/shard_map/all_to_all | solution.py:302
  82.6 0.9 copy-done.13
  83.5 0.6 finish.1.before_ref
  84.1 1.9 %collective-permute-start.4 = (bf16[128,1024]{1,0:T(8,128)(2,1)S(1)}, bf16[128,1024]{1,0:T(8,128)(2,1)S(1)}, u32[]{:S(2)}, u32[]{:S(2)}) collective-permute-start(bf16[128,1024]{1,0:T(8,128)(2,1)S(1)} %finish.1.before_ref), channel_id=1, source_target_pairs={{0,16},{16,32},{32,48},{48,64},{64,80},{80,96},{96,112},{112,128},... | collective-permute-start | bytes 786440 | tf_op jit(solution)/shard_map/ppermute | solution.py:307
  86.1 5.8 %collective-permute-done.4.x_ref = bf16[128,1024]{1,0:T(8,128)(2,1)S(1)} collective-permute-done((bf16[128,1024]{1,0:T(8,128)(2,1)S(1)}, bf16[128,1024]{1,0:T(8,128)(2,1)S(1)}, u32[]{:S(2)}, u32[]{:S(2)}) %collective-permute-start.4) | collective-permute-done | bytes 262176 | tf_op jit(solution)/shard_map/ppermute | solution.py:307
  91.8 0.3 spread.3
  92.1 30.3 %all_to_all.26.x_ref = bf16[8,128,1024]{2,1,0:T(8,128)(2,1)S(1)} all-to-all(bf16[8,128,1024]{2,1,0:T(8,128)(2,1)S(1)} %get-tuple-element.47), channel_id=1, replica_groups=mesh['section'=32,'p'=2,'g'=8] {'g'}, dimensions={0} | all-to-all | bytes 4194304 | tf_op jit(solution)/shard_map/all_to_all | solution.py:286
  122.5 2.0 %project.3 = (bf16[2,1024,128]{2,1,0:T(8,128)(2,1)S(1)}, bf16[2,1024,128]{2,1,0:T(8,128)(2,1)S(1)}, f32[8,128]{1,0:T(8,128)}) custom-call(bf16[8,128,1024]{2,1,0:T(8,128)(2,1)S(1)} %all_to_all.26.x_ref, bf16[1024,256]{1,0:T(8,128)(2,1)S(1)} %pad_maximum_fusion.own_ref, bf16[1024,256]{1,0:T(8,128)(2,1)S(1)} %copy-done.4), custom_call_target="tpu_custom_call" | custom-call | tf_op jit(solution)/shard_map/project/pallas_call | solution.py:111
  124.5 2.5 %collective-permute-start.5 = (bf16[2,1024,128]{2,1,0:T(8,128)(2,1)S(1)}, bf16[2,1024,128]{2,1,0:T(8,128)(2,1)S(1)}, u32[]{:S(2)}, u32[]{:S(2)}) collective-permute-start(bf16[2,1024,128]{2,1,0:T(8,128)(2,1)S(1)} %get-tuple-element.49.kv_ref), channel_id=1, source_target_pairs={{0,12},{1,13},{2,14},{3,15},{4,8},{5,9},{6,10},{7,11},{8,4},{9,5},... | collective-permute-start | bytes 1572872 | tf_op jit(solution)/shard_map/ppermute | solution.py:233
  127.0 5.8 %attend_early_kernel.3.acc_ref = f32[2,1024,128]{2,1,0:T(8,128)S(1)} custom-call(f32[2]{0:T(128)S(1)} %pad_maximum_fusion.4.rep_ref, s32[1]{0:T(128)} %bitcast.16.p_ref, s32[2,2048]{1,0:T(2,128)S(1)} %bitcast.43, s32[2,2048]{1,0:T(2,128)S(1)} %bitcast.47, s32[2,2048]{1,0:T(2,128)S(1)} %bitcast.51, bf16[2,128,128]{2,1,0:T(8,128)(2,1)S(1)} %pad.4.table_ref, ...), custom_call_target="tpu_custom_call" | custom-call | tf_op jit(solution)/shard_map/attend_early_kernel/pallas_call | solution.py:177
  132.8 7.0 %collective-permute-done.5.far_ref = bf16[2,1024,128]{2,1,0:T(8,128)(2,1)S(1)} collective-permute-done((bf16[2,1024,128]{2,1,0:T(8,128)(2,1)S(1)}, bf16[2,1024,128]{2,1,0:T(8,128)(2,1)S(1)}, u32[]{:S(2)}, u32[]{:S(2)}) %collective-permute-start.5) | collective-permute-done | bytes 524320 | tf_op jit(solution)/shard_map/ppermute | solution.py:233
  139.8 3.7 %attend_late_kernel.3 = bf16[1024,256]{1,0:T(8,128)(2,1)S(1)} custom-call(f32[2]{0:T(128)S(1)} %pad_maximum_fusion.4.rep_ref, s32[1]{0:T(128)} %bitcast.16.p_ref, s32[2,2048]{1,0:T(2,128)S(1)} %bitcast.44, s32[2,2048]{1,0:T(2,128)S(1)} %bitcast.48, s32[2,2048]{1,0:T(2,128)S(1)} %bitcast.52, bf16[2,128,128]{2,1,0:T(8,128)(2,1)S(1)} %pad.4.table_ref, ...), custom_call_target="tpu_custom_call" | custom-call | tf_op jit(solution)/shard_map/attend_late_kernel/pallas_call | solution.py:177
  143.6 14.0 %all_to_all.27.r_ref = bf16[8,128,256]{2,1,0:T(8,128)(2,1)S(1)} all-to-all(bf16[8,128,256]{2,1,0:T(8,128)(2,1)S(1)} %bitcast.37), channel_id=1, replica_groups=mesh['section'=32,'p'=2,'g'=8] {'g'}, dimensions={0} | all-to-all | bytes 1048576 | tf_op jit(solution)/shard_map/all_to_all | solution.py:302
  157.6 1.4 finish_last.1
  (50 shorter events, 0.3 us)
Async XLA Ops:
  0.0 0.9 copy-start.5
  1.0 0.9 copy-start.14
  1.9 0.7 copy-start.15
  2.9 1.4 copy-start.2
  4.3 0.7 copy-start.12
  5.0 8.6 %copy-start.7 = (bf16[1,768,1,128]{3,1,2,0:T(8,128)(2,1)S(1)}, bf16[1,768,1,128]{3,1,2,0:T(8,128)(2,1)}, u32[]{:S(2)}) copy-start(bf16[1,768,1,128]{3,1,2,0:T(8,128)(2,1)} %param.25) | copy-start | bytes 589828
  5.0 11.1 %copy-start.20 = (bf16[1,1024,64]{1,2,0:T(8,128)(2,1)S(1)}, bf16[1,1024,64]{1,2,0:T(8,128)(2,1)}, u32[]{:S(2)}) copy-start(bf16[1,1024,64]{1,2,0:T(8,128)(2,1)} %param.19) | copy-start | bytes 393220
  5.0 31.3 %all-to-all-start = ((bf16[8,128,1024]{2,1,0:T(8,128)(2,1)}), bf16[8,128,1024]{2,1,0:T(8,128)(2,1)S(1)}, u32[]{:S(2)}, u32[]{:S(2)}) async-start(bf16[8,128,1024]{2,1,0:T(8,128)(2,1)} %copy-done.2), calls=%async_computation | async-start | bytes 4194304 | tf_op jit(solution)/shard_map/all_to_all | solution.py:286
  10.2 11.6 %copy-start.21 = (f32[1,1024]{1,0:T(1,128)S(1)}, f32[1,1024]{1,0:T(1,128)}, u32[]{:S(2)}) copy-start(f32[1,1024]{1,0:T(1,128)} %param.22) | copy-start | bytes 12292
  10.2 16.4 %collective-permute-start.2 = (bf16[64,1024]{1,0:T(8,128)(2,1)}, bf16[64,1024]{1,0:T(8,128)(2,1)}, u32[]{:S(2)}, u32[]{:S(2)}) collective-permute-start(bf16[64,1024]{1,0:T(8,128)(2,1)} %bitcast.15), channel_id=1, source_target_pairs={{0,12},{1,13},{2,14},{3,15},{4,8},{5,9},{6,10},{7,11},{8,4},{9,5},... | collective-permute-start | bytes 393224 | tf_op jit(solution)/shard_map/ppermute | solution.py:233
  13.6 14.7 %collective-permute-start.1 = (bf16[768,128]{1,0:T(8,128)(2,1)S(1)}, bf16[768,128]{1,0:T(8,128)(2,1)}, u32[]{:S(2)}, u32[]{:S(2)}) collective-permute-start(bf16[768,128]{1,0:T(8,128)(2,1)S(1)} %bitcast.38), channel_id=1, source_target_pairs={{0,12},{1,13},{2,14},{3,15},{4,8},{5,9},{6,10},{7,11},{8,4},{9,5},... | collective-permute-start | bytes 589832 | tf_op jit(solution)/shard_map/ppermute | solution.py:233
  16.3 8.5 %copy-start.22 = (f32[1,16]{1,0:T(1,128)S(1)}, f32[1,16]{1,0:T(1,128)}, u32[]{:S(2)}) copy-start(f32[1,16]{1,0:T(1,128)} %param.24) | copy-start | bytes 196
  17.9 14.8 %collective-permute-start = (bf16[1024,256]{1,0:T(8,128)(2,1)S(1)}, bf16[1024,256]{1,0:T(8,128)(2,1)S(1)}, u32[]{:S(2)}, u32[]{:S(2)}) collective-permute-start(bf16[1024,256]{1,0:T(8,128)(2,1)S(1)} %pad_maximum_fusion.own_ref), channel_id=1, source_target_pairs={{0,12},{1,13},{2,14},{3,15},{4,8},{5,9},{6,10},{7,11},{8,4},{9,5},... | collective-permute-start | bytes 1572872 | tf_op jit(solution)/shard_map/ppermute | solution.py:233
  36.2 2.7 %copy-start = (bf16[8,128,1024]{2,1,0:T(8,128)(2,1)}, bf16[8,128,1024]{2,1,0:T(8,128)(2,1)S(1)}, u32[]{:S(2)}) copy-start(bf16[8,128,1024]{2,1,0:T(8,128)(2,1)S(1)} %all-to-all-done.x_ref) | copy-start | bytes 6291460
  39.0 29.9 %all-to-all-start.1 = ((bf16[8,128,1024]{2,1,0:T(8,128)(2,1)}), bf16[8,128,1024]{2,1,0:T(8,128)(2,1)S(1)}, u32[]{:S(2)}, u32[]{:S(2)}) async-start(bf16[8,128,1024]{2,1,0:T(8,128)(2,1)} %broadcast_in_dim.4), calls=%async_computation.1 | async-start | bytes 4194304 | tf_op jit(solution)/shard_map/all_to_all | solution.py:295
  43.3 1.6 %copy-start.1 = (bf16[8,128,1024]{2,1,0:T(8,128)(2,1)S(1)}, bf16[8,128,1024]{2,1,0:T(8,128)(2,1)}, u32[]{:S(2)}) copy-start(bf16[8,128,1024]{2,1,0:T(8,128)(2,1)} %copy-done) | copy-start | bytes 6291460
  44.9 5.7 %copy-start.9 = (s32[1,2,2048]{2,1,0:T(2,128)S(1)}, s32[1,2,2048]{2,1,0:T(2,128)}, u32[]{:S(2)}) copy-start(s32[1,2,2048]{2,1,0:T(2,128)} %param.26) | copy-start | bytes 49156
  44.9 5.7 %copy-start.10 = (s32[1,2,2048]{2,1,0:T(2,128)S(1)}, s32[1,2,2048]{2,1,0:T(2,128)}, u32[]{:S(2)}) copy-start(s32[1,2,2048]{2,1,0:T(2,128)} %param.27) | copy-start | bytes 49156
  44.9 5.7 %copy-start.11 = (s32[1,2,2048]{2,1,0:T(2,128)S(1)}, s32[1,2,2048]{2,1,0:T(2,128)}, u32[]{:S(2)}) copy-start(s32[1,2,2048]{2,1,0:T(2,128)} %param.28) | copy-start | bytes 49156
  44.9 5.7 %copy-start.17 = (s32[1,768]{1,0:T(1,128)S(1)}, s32[1,768]{1,0:T(1,128)}, u32[]{:S(2)}) copy-start(s32[1,768]{1,0:T(1,128)} %cpos_ref.3) | copy-start | bytes 9220
  44.9 5.7 %copy-start.18 = (s32[1,768]{1,0:T(1,128)S(1)}, s32[1,768]{1,0:T(1,128)}, u32[]{:S(2)}) copy-start(s32[1,768]{1,0:T(1,128)} %cbkt_ref.3) | copy-start | bytes 9220
  44.9 5.7 %copy-start.19 = (s32[1,768]{1,0:T(1,128)S(1)}, s32[1,768]{1,0:T(1,128)}, u32[]{:S(2)}) copy-start(s32[1,768]{1,0:T(1,128)} %citm_ref.3) | copy-start | bytes 9220
  47.0 0.8 copy-start.3
  47.8 14.7 %collective-permute-start.3 = (bf16[2,1024,128]{2,1,0:T(8,128)(2,1)S(1)}, bf16[2,1024,128]{2,1,0:T(8,128)(2,1)S(1)}, u32[]{:S(2)}, u32[]{:S(2)}) collective-permute-start(bf16[2,1024,128]{2,1,0:T(8,128)(2,1)S(1)} %get-tuple-element.40.kv_ref), channel_id=1, source_target_pairs={{0,12},{1,13},{2,14},{3,15},{4,8},{5,9},{6,10},{7,11},{8,4},{9,5},... | collective-permute-start | bytes 1572872 | tf_op jit(solution)/shard_map/ppermute | solution.py:233
  68.8 23.0 %copy-start.6 = (bf16[128,1024]{1,0:T(8,128)(2,1)S(1)}, bf16[128,1024]{1,0:T(8,128)(2,1)}, u32[]{:S(2)}) copy-start(bf16[128,1024]{1,0:T(8,128)(2,1)} %new_ref.3) | copy-start | bytes 786436
  68.8 23.0 %copy-start.16 = (f32[1,1024]{1,0:T(1,128)S(1)}, f32[1,1024]{1,0:T(1,128)}, u32[]{:S(2)}) copy-start(f32[1,1024]{1,0:T(1,128)} %gain_ref.3) | copy-start | bytes 12292
  82.6 1.0 copy-start.13
  84.1 7.7 %collective-permute-start.4 = (bf16[128,1024]{1,0:T(8,128)(2,1)S(1)}, bf16[128,1024]{1,0:T(8,128)(2,1)S(1)}, u32[]{:S(2)}, u32[]{:S(2)}) collective-permute-start(bf16[128,1024]{1,0:T(8,128)(2,1)S(1)} %finish.1.before_ref), channel_id=1, source_target_pairs={{0,16},{16,32},{32,48},{48,64},{64,80},{80,96},{96,112},{112,128},... | collective-permute-start | bytes 786440 | tf_op jit(solution)/shard_map/ppermute | solution.py:307
  92.1 30.3 %copy-start.4 = (bf16[1024,256]{1,0:T(8,128)(2,1)S(1)}, bf16[1024,256]{1,0:T(8,128)(2,1)}, u32[]{:S(2)}) copy-start(bf16[1024,256]{1,0:T(8,128)(2,1)} %copy-done.3) | copy-start | bytes 1572868
  122.5 4.5 %copy-start.8 = (bf16[1,768,1,128]{3,1,2,0:T(8,128)(2,1)S(1)}, bf16[1,768,1,128]{3,1,2,0:T(8,128)(2,1)}, u32[]{:S(2)}) copy-start(bf16[1,768,1,128]{3,1,2,0:T(8,128)(2,1)} %param.25) | copy-start | bytes 589828
  124.5 15.3 %collective-permute-start.5 = (bf16[2,1024,128]{2,1,0:T(8,128)(2,1)S(1)}, bf16[2,1024,128]{2,1,0:T(8,128)(2,1)S(1)}, u32[]{:S(2)}, u32[]{:S(2)}) collective-permute-start(bf16[2,1024,128]{2,1,0:T(8,128)(2,1)S(1)} %get-tuple-element.49.kv_ref), channel_id=1, source_target_pairs={{0,12},{1,13},{2,14},{3,15},{4,8},{5,9},{6,10},{7,11},{8,4},{9,5},... | collective-permute-start | bytes 1572872 | tf_op jit(solution)/shard_map/ppermute | solution.py:233

commit v4 on v3

--- a/solution.py
+++ b/solution.py
@@ -69,6 +69,32 @@
     )(*operands)
 
 
+def open_kernel(x_ref, gain_ref, out_ref):
+    here = x_ref[...].astype(F32)
+    mean = jnp.mean(here, axis=-1, keepdims=True)
+    variance = jnp.mean(here * here, axis=-1, keepdims=True) - mean * mean
+    normed = ((here - mean) * lax.rsqrt(variance + EPSILON) * gain_ref[...]).astype(BF16)
+    for k in range(NG):
+        out_ref[k] = normed
+
+
+def copies_kernel(own_ref, other_ref, out_ref):
+    for k in range(NG):
+        out_ref[k, :DH, :] = own_ref[...]
+        out_ref[k, DH:, :] = other_ref[...]
+
+
+def copies_of(kernel, *operands):
+    return pl.pallas_call(
+        kernel,
+        out_shape=jax.ShapeDtypeStruct((NG, ROWS, D), BF16),
+        in_specs=[vmem()] * 2,
+        out_specs=vmem(),
+        compiler_params=params(),
+        name=kernel.__name__,
+    )(*operands)
+
+
 def column(row):
     return jnp.transpose(jnp.broadcast_to(row, (128, row.shape[1])))
 
@@ -97,8 +123,8 @@
         cko[...] = jnp.where(column(cbkt_ref[...]) == lane[:CACHE] - DH, 1.0, 0.0).astype(BF16)
 
 
-def project_kernel(x_ref, own_ref, other_ref, qg_ref, kv_ref, token_ref):
-    token_ref[...] = jnp.zeros((8, 128), F32)
+def project_kernel(x_ref, own_ref, other_ref, *refs):
+    qg_ref, kv_ref = refs[-2:]
     normed = x_ref[...].reshape(BAND, D)
     scale = jnp.where(low_lanes(BAND), 0.5, 1.0)
     for h, w_ref in enumerate((own_ref, other_ref)):
@@ -113,10 +139,9 @@
         out_shape=(
             jax.ShapeDtypeStruct((NP, BAND, 2 * DH), BF16),
             jax.ShapeDtypeStruct((NP, BAND, 2 * DH), BF16),
-            jax.ShapeDtypeStruct((8, 128), F32),
         ),
-        in_specs=[vmem()] * 3,
-        out_specs=(vmem(),) * 3,
+        in_specs=[vmem()] * 3 + [pl.BlockSpec(memory_space=pl.ANY)] * (len(operands) - 3),
+        out_specs=(vmem(),) * 2,
         compiler_params=params(),
         name="project",
     )(*operands)
@@ -274,25 +299,28 @@
     first = jnp.zeros((1,), jnp.int32)
     produced = ()
     for tick in range(TICKS):
-        current, copies = spread(first, received, new_slice, input_gain)
+        if tick == 0:
+            current, copies = received, copies_of(open_kernel, received, input_gain)
+        else:
+            current, copies = spread(first, received, new_slice, input_gain)
         if tick == 0:
             copies, w_qkv, w_gate, w_out, cache_kv = lax.optimization_barrier((copies, w_qkv, w_gate, w_out, cache_kv))
             w_own = jnp.concatenate([w_qkv[0, :, :DH], w_gate[0], w_qkv[0, :, DH:]], axis=1)
             w_other = swap(w_own)
             c_own = cache_kv[0, :, 0, :]
             c_other = swap(c_own)
-            w_pair = jnp.concatenate([w_out[0], swap(w_out[0])])
-            w_copies = jnp.broadcast_to(w_pair[None], (NG, 2 * DH, D))
+            w_copies = copies_of(copies_kernel, w_out[0], swap(w_out[0]))
         band = lax.all_to_all(copies, "g", 0, 0)
         if tick == 0:
-            band, w_own, w_other, c_other, rep, toeplitz, gain_out, w_copies = lax.optimization_barrier(
-                (band, w_own, w_other, c_other, rep, toeplitz, gain_out, w_copies)
+            token = band[0, :16, :128]
+            token, w_own, w_other, c_other, rep, toeplitz, gain_out, w_copies = lax.optimization_barrier(
+                (token, w_own, w_other, c_other, rep, toeplitz, gain_out, w_copies)
             )
-        qg, kv, token = project(band, w_own, w_other)
+            w_out_full = lax.all_to_all(w_copies, "g", 0, 0).reshape(D, D)
+            qg, kv = project(band, w_own, w_other, token)
+        else:
+            qg, kv = project(band, w_own, w_other)
         far = swap(kv)
-        if tick == 0:
-            w_copies, token = lax.optimization_barrier((w_copies, token))
-            w_out_full = lax.all_to_all(w_copies, "g", 0, 0).reshape(D, D)
         keyed = (tick, (NP, BAND, 2 * DH), F32, SCRATCH + [CACHE_BUCKETS])
         given = (rep, p_word, slice_positions[0], slice_buckets[0], slice_items[0], toeplitz, qg)
         acc = attend(early_kernel, *keyed, *given, kv, cache_positions, cache_buckets, cache_items, c_own, c_other)

time: 160 us -> 157 us (0.981)
    ppermute x5, waiting for transfers between devices: 17.5 us -> 13.1 us  [swap(): return lax.ppermute(x, ('p', 'g'), [(i, partner(i)) for i in range(H)])]
    broadcast_in_dim x1 -> x0, local copies, waits for them, and re-layouts: 2.72 us -> none  [body(): w_copies = jnp.broadcast_to(w_pair[None], (NG, 2 * DH, D))]
    all_to_all x1, waiting for transfers between devices: 3.51 us -> 5.89 us  [body(): band = lax.all_to_all(copies, 'g', 0, 0)]
    concatenate x1 -> x0, other arithmetic: 1.69 us -> none  [body(): w_pair = jnp.concatenate([w_out[0], swap(w_out[0])])]
    unnamed x47 -> x51, local copies, waits for them, and re-layouts: 8.56 us -> 9.52 us
  transfers between devices with their start and end apart: 8 -> 8, of which waited for: 6 -> 5; matrix products, arithmetic and copies ran while one was open for 5% -> 5% of each run, Pallas kernels for 11% -> 11%
where the time goes in v4:
time: 157 us; the launch traced here: 156 us
  blocking collectives  58.3 us (37%)
  waiting for transfers between devices  28.7 us (18%)
  starting transfers between devices  25.9 us (16%)
  Pallas kernels  25.6 us (16%)
  local copies, waits for them, and re-layouts  13.3 us (8%)
  other arithmetic  2.93 us (2%)
    all_to_all x1, blocking collectives, body(): band = lax.all_to_all(copies, 'g', 0, 0)  30.4 us
    all_to_all x2, blocking collectives, body(): back = lax.all_to_all(a.reshape(NG, ROWS, 4 * DH), 'g', 0, 0)  27.9 us
    pallas_call x4, Pallas kernels, attend(): pl.pallas_call(functools.partial(kernel, tick), out_shape=jax.ShapeDtypeS...  19.1 us
    ppermute x5, starting transfers between devices, swap(): return lax.ppermute(x, ('p', 'g'), [(i, partner(i)) for i in range(H)])  15.1 us
    ppermute x5, waiting for transfers between devices, swap(): return lax.ppermute(x, ('p', 'g'), [(i, partner(i)) for i in range(H)])  13.1 us
    unnamed x51, local copies, waits for them, and re-layouts  9.52 us
    all_to_all x1, waiting for transfers between devices, body(): band = lax.all_to_all(copies, 'g', 0, 0)  5.89 us
    ppermute x1, waiting for transfers between devices, body(): lax.ppermute(one, 'section', [(s, s + 1) for s in range(count - 1)])  5.76 us
  transfers between devices with their start and end apart: 8, of which 5 were waited for; matrix products, arithmetic and copies ran while one was open for 5% of the time, Pallas kernels for 11%

profile of v4, /device:TPU:228, one launch (start us, length us, event | category | flops | bytes accessed | tf_op | source)
XLA Modules:
  0.0 156.2 jit_solution(13181330828597866832)
XLA Ops:
  0.0 0.9 copy-done.6
  1.0 0.7 copy-done.17
  1.6 0.3 open_kernel.1
  1.9 1.4 copy-done.2
  3.3 5.2 %all-to-all-start = ((bf16[8,128,1024]{2,1,0:T(8,128)(2,1)}), bf16[8,128,1024]{2,1,0:T(8,128)(2,1)S(1)}, u32[]{:S(2)}, u32[]{:S(2)}) async-start(bf16[8,128,1024]{2,1,0:T(8,128)(2,1)} %copy-done.2), calls=%async_computation | async-start | bytes 4194304 | tf_op jit(solution)/shard_map/all_to_all | solution.py:313
  8.5 3.4 %collective-permute-start.2 = (bf16[64,1024]{1,0:T(8,128)(2,1)S(1)}, bf16[64,1024]{1,0:T(8,128)(2,1)}, u32[]{:S(2)}, u32[]{:S(2)}) collective-permute-start(bf16[64,1024]{1,0:T(8,128)(2,1)S(1)} %bitcast.57), channel_id=1, source_target_pairs={{0,12},{1,13},{2,14},{3,15},{4,8},{5,9},{6,10},{7,11},{8,4},{9,5},... | collective-permute-start | bytes 393224 | tf_op jit(solution)/shard_map/ppermute | solution.py:258
  11.9 2.5 %collective-permute-start.1 = (bf16[768,128]{1,0:T(8,128)(2,1)S(1)}, bf16[768,128]{1,0:T(8,128)(2,1)}, u32[]{:S(2)}, u32[]{:S(2)}) collective-permute-start(bf16[768,128]{1,0:T(8,128)(2,1)S(1)} %bitcast.42), channel_id=1, source_target_pairs={{0,12},{1,13},{2,14},{3,15},{4,8},{5,9},{6,10},{7,11},{8,4},{9,5},... | collective-permute-start | bytes 589832 | tf_op jit(solution)/shard_map/ppermute | solution.py:258
  14.4 0.2 copy.17
  14.6 0.1 slice_bitcast_fusion
  14.8 1.1 copy.18
  15.9 0.2 pad_maximum_fusion.own_ref
  16.1 3.4 %collective-permute-start = (bf16[1024,256]{1,0:T(8,128)(2,1)S(1)}, bf16[1024,256]{1,0:T(8,128)(2,1)S(1)}, u32[]{:S(2)}, u32[]{:S(2)}) collective-permute-start(bf16[1024,256]{1,0:T(8,128)(2,1)S(1)} %pad_maximum_fusion.own_ref), channel_id=1, source_target_pairs={{0,12},{1,13},{2,14},{3,15},{4,8},{5,9},{6,10},{7,11},{8,4},{9,5},... | collective-permute-start | bytes 1572872 | tf_op jit(solution)/shard_map/ppermute | solution.py:258
  19.5 0.5 broadcast.11
  20.1 0.7 reduce.3
  20.8 0.7 fusion.3
  21.5 1.2 fusion
  22.7 0.7 fusion.2
  23.4 0.1 reshape.39.gain_ref
  23.5 0.8 pad.4.table_ref
  24.3 0.6 constant_dynamic-slice_fusion.3
  24.9 1.3 pad_maximum_fusion.3.rep_ref
  26.3 1.0 copies_kernel.1
  27.3 1.3 copy-done.3
  28.7 5.9 %all-to-all-done.x_ref = bf16[8,128,1024]{2,1,0:T(8,128)(2,1)S(1)} async-done(((bf16[8,128,1024]{2,1,0:T(8,128)(2,1)}), bf16[8,128,1024]{2,1,0:T(8,128)(2,1)S(1)}, u32[]{:S(2)}, u32[]{:S(2)}) %all-to-all-start) | async-done | bytes 2097184 | tf_op jit(solution)/shard_map/all_to_all | solution.py:313
  34.6 1.4 copy-done
  35.9 3.6 %all-to-all-start.1 = ((bf16[8,128,1024]{2,1,0:T(8,128)(2,1)}), bf16[8,128,1024]{2,1,0:T(8,128)(2,1)S(1)}, u32[]{:S(2)}, u32[]{:S(2)}) async-start(bf16[8,128,1024]{2,1,0:T(8,128)(2,1)} %copy-done.3), calls=%async_computation.1 | async-start | bytes 4194304 | tf_op jit(solution)/shard_map/all_to_all | solution.py:319
  39.6 1.6 %copy-done.1 = bf16[8,128,1024]{2,1,0:T(8,128)(2,1)S(1)} copy-done((bf16[8,128,1024]{2,1,0:T(8,128)(2,1)S(1)}, bf16[8,128,1024]{2,1,0:T(8,128)(2,1)}, u32[]{:S(2)}) %copy-start.1) | copy-done | bytes 2097176
  41.2 1.5 project.2
  42.7 3.4 %collective-permute-start.3 = (bf16[2,1024,128]{2,1,0:T(8,128)(2,1)S(1)}, bf16[2,1024,128]{2,1,0:T(8,128)(2,1)S(1)}, u32[]{:S(2)}, u32[]{:S(2)}) collective-permute-start(bf16[2,1024,128]{2,1,0:T(8,128)(2,1)S(1)} %get-tuple-element.37.kv_ref), channel_id=1, source_target_pairs={{0,12},{1,13},{2,14},{3,15},{4,8},{5,9},{6,10},{7,11},{8,4},{9,5},... | collective-permute-start | bytes 1572872 | tf_op jit(solution)/shard_map/ppermute | solution.py:258
  46.2 5.8 %attend_early_kernel.2.acc_ref = f32[2,1024,128]{2,1,0:T(8,128)S(1)} custom-call(f32[2]{0:T(128)S(1)} %pad_maximum_fusion.3.rep_ref, s32[1]{0:T(128)} %bitcast.17.p_ref, s32[2,2048]{1,0:T(2,128)S(1)} %bitcast.45, s32[2,2048]{1,0:T(2,128)S(1)} %bitcast.49, s32[2,2048]{1,0:T(2,128)S(1)} %bitcast.53, bf16[2,128,128]{2,1,0:T(8,128)(2,1)S(1)} %pad.4.table_ref, ...), custom_call_target="tpu_custom_call" | custom-call | tf_op jit(solution)/shard_map/attend_early_kernel/pallas_call | solution.py:202
  52.0 6.1 %collective-permute-done.3.far_ref = bf16[2,1024,128]{2,1,0:T(8,128)(2,1)S(1)} collective-permute-done((bf16[2,1024,128]{2,1,0:T(8,128)(2,1)S(1)}, bf16[2,1024,128]{2,1,0:T(8,128)(2,1)S(1)}, u32[]{:S(2)}, u32[]{:S(2)}) %collective-permute-start.3) | collective-permute-done | bytes 524320 | tf_op jit(solution)/shard_map/ppermute | solution.py:258
  58.1 3.7 %attend_late_kernel.2 = bf16[1024,256]{1,0:T(8,128)(2,1)S(1)} custom-call(f32[2]{0:T(128)S(1)} %pad_maximum_fusion.3.rep_ref, s32[1]{0:T(128)} %bitcast.17.p_ref, s32[2,2048]{1,0:T(2,128)S(1)} %bitcast.46, s32[2,2048]{1,0:T(2,128)S(1)} %bitcast.50, s32[2,2048]{1,0:T(2,128)S(1)} %bitcast.54, bf16[2,128,128]{2,1,0:T(8,128)(2,1)S(1)} %pad.4.table_ref, ...), custom_call_target="tpu_custom_call" | custom-call | tf_op jit(solution)/shard_map/attend_late_kernel/pallas_call | solution.py:202
  61.9 3.9 %all-to-all-done.1 = bf16[8,128,1024]{2,1,0:T(8,128)(2,1)S(1)} async-done(((bf16[8,128,1024]{2,1,0:T(8,128)(2,1)}), bf16[8,128,1024]{2,1,0:T(8,128)(2,1)S(1)}, u32[]{:S(2)}, u32[]{:S(2)}) %all-to-all-start.1) | async-done | bytes 2097184 | tf_op jit(solution)/shard_map/all_to_all | solution.py:319
  65.8 13.8 %all_to_all.25.r_ref = bf16[8,128,256]{2,1,0:T(8,128)(2,1)S(1)} all-to-all(bf16[8,128,256]{2,1,0:T(8,128)(2,1)S(1)} %bitcast.38), channel_id=1, replica_groups=mesh['section'=32,'p'=2,'g'=8] {'g'}, dimensions={0} | all-to-all | bytes 1048576 | tf_op jit(solution)/shard_map/all_to_all | solution.py:330
  79.6 0.6 finish.1.before_ref
  80.2 1.9 %collective-permute-start.4 = (bf16[128,1024]{1,0:T(8,128)(2,1)S(1)}, bf16[128,1024]{1,0:T(8,128)(2,1)S(1)}, u32[]{:S(2)}, u32[]{:S(2)}) collective-permute-start(bf16[128,1024]{1,0:T(8,128)(2,1)S(1)} %finish.1.before_ref), channel_id=1, source_target_pairs={{0,16},{16,32},{32,48},{48,64},{64,80},{80,96},{96,112},{112,128},... | collective-permute-start | bytes 786440 | tf_op jit(solution)/shard_map/ppermute | solution.py:335
  82.1 5.8 %collective-permute-done.4.x_ref = bf16[128,1024]{1,0:T(8,128)(2,1)S(1)} collective-permute-done((bf16[128,1024]{1,0:T(8,128)(2,1)S(1)}, bf16[128,1024]{1,0:T(8,128)(2,1)S(1)}, u32[]{:S(2)}, u32[]{:S(2)}) %collective-permute-start.4) | collective-permute-done | bytes 262176 | tf_op jit(solution)/shard_map/ppermute | solution.py:335
  87.9 0.7 copy-done.14
  88.6 0.9 copy-done.15
  89.5 0.3 spread.1
  89.9 30.4 %all_to_all.26.x_ref = bf16[8,128,1024]{2,1,0:T(8,128)(2,1)S(1)} all-to-all(bf16[8,128,1024]{2,1,0:T(8,128)(2,1)S(1)} %get-tuple-element.43), channel_id=1, replica_groups=mesh['section'=32,'p'=2,'g'=8] {'g'}, dimensions={0} | all-to-all | bytes 4194304 | tf_op jit(solution)/shard_map/all_to_all | solution.py:313
  120.2 1.5 project.3
  121.7 2.4 %collective-permute-start.5 = (bf16[2,1024,128]{2,1,0:T(8,128)(2,1)S(1)}, bf16[2,1024,128]{2,1,0:T(8,128)(2,1)S(1)}, u32[]{:S(2)}, u32[]{:S(2)}) collective-permute-start(bf16[2,1024,128]{2,1,0:T(8,128)(2,1)S(1)} %get-tuple-element.45.kv_ref), channel_id=1, source_target_pairs={{0,12},{1,13},{2,14},{3,15},{4,8},{5,9},{6,10},{7,11},{8,4},{9,5},... | collective-permute-start | bytes 1572872 | tf_op jit(solution)/shard_map/ppermute | solution.py:258
  124.1 5.8 %attend_early_kernel.3.acc_ref = f32[2,1024,128]{2,1,0:T(8,128)S(1)} custom-call(f32[2]{0:T(128)S(1)} %pad_maximum_fusion.3.rep_ref, s32[1]{0:T(128)} %bitcast.17.p_ref, s32[2,2048]{1,0:T(2,128)S(1)} %bitcast.47, s32[2,2048]{1,0:T(2,128)S(1)} %bitcast.51, s32[2,2048]{1,0:T(2,128)S(1)} %bitcast.55, bf16[2,128,128]{2,1,0:T(8,128)(2,1)S(1)} %pad.4.table_ref, ...), custom_call_target="tpu_custom_call" | custom-call | tf_op jit(solution)/shard_map/attend_early_kernel/pallas_call | solution.py:202
  129.9 7.0 %collective-permute-done.5.far_ref = bf16[2,1024,128]{2,1,0:T(8,128)(2,1)S(1)} collective-permute-done((bf16[2,1024,128]{2,1,0:T(8,128)(2,1)S(1)}, bf16[2,1024,128]{2,1,0:T(8,128)(2,1)S(1)}, u32[]{:S(2)}, u32[]{:S(2)}) %collective-permute-start.5) | collective-permute-done | bytes 524320 | tf_op jit(solution)/shard_map/ppermute | solution.py:258
  136.9 3.7 %attend_late_kernel.3 = bf16[1024,256]{1,0:T(8,128)(2,1)S(1)} custom-call(f32[2]{0:T(128)S(1)} %pad_maximum_fusion.3.rep_ref, s32[1]{0:T(128)} %bitcast.17.p_ref, s32[2,2048]{1,0:T(2,128)S(1)} %bitcast.48, s32[2,2048]{1,0:T(2,128)S(1)} %bitcast.52, s32[2,2048]{1,0:T(2,128)S(1)} %bitcast.56, bf16[2,128,128]{2,1,0:T(8,128)(2,1)S(1)} %pad.4.table_ref, ...), custom_call_target="tpu_custom_call" | custom-call | tf_op jit(solution)/shard_map/attend_late_kernel/pallas_call | solution.py:202
  140.7 14.1 %all_to_all.27.r_ref = bf16[8,128,256]{2,1,0:T(8,128)(2,1)S(1)} all-to-all(bf16[8,128,256]{2,1,0:T(8,128)(2,1)S(1)} %bitcast.39), channel_id=1, replica_groups=mesh['section'=32,'p'=2,'g'=8] {'g'}, dimensions={0} | all-to-all | bytes 1048576 | tf_op jit(solution)/shard_map/all_to_all | solution.py:330
  154.8 1.4 finish_last.1
  (54 shorter events, 0.2 us)
Async XLA Ops:
  0.0 0.9 copy-start.6
  1.0 0.7 copy-start.17
  1.9 1.4 copy-start.2
  3.3 5.2 %copy-start.16 = (bf16[1,64,1024]{2,1,0:T(8,128)(2,1)S(1)}, bf16[1,64,1024]{2,1,0:T(8,128)(2,1)}, u32[]{:S(2)}) copy-start(bf16[1,64,1024]{2,1,0:T(8,128)(2,1)} %param.20) | copy-start | bytes 393220
  3.3 8.7 %copy-start.8 = (bf16[1,768,1,128]{3,1,2,0:T(8,128)(2,1)S(1)}, bf16[1,768,1,128]{3,1,2,0:T(8,128)(2,1)}, u32[]{:S(2)}) copy-start(bf16[1,768,1,128]{3,1,2,0:T(8,128)(2,1)} %param.25) | copy-start | bytes 589828
  3.3 11.1 %copy-start.22 = (bf16[1,1024,192]{1,2,0:T(8,128)(2,1)S(1)}, bf16[1,1024,192]{1,2,0:T(8,128)(2,1)}, u32[]{:S(2)}) copy-start(bf16[1,1024,192]{1,2,0:T(8,128)(2,1)} %param.18) | copy-start | bytes 1179652
  3.3 31.3 %all-to-all-start = ((bf16[8,128,1024]{2,1,0:T(8,128)(2,1)}), bf16[8,128,1024]{2,1,0:T(8,128)(2,1)S(1)}, u32[]{:S(2)}, u32[]{:S(2)}) async-start(bf16[8,128,1024]{2,1,0:T(8,128)(2,1)} %copy-done.2), calls=%async_computation | async-start | bytes 4194304 | tf_op jit(solution)/shard_map/all_to_all | solution.py:313
  8.5 11.5 %copy-start.23 = (f32[1,1024]{1,0:T(1,128)S(1)}, f32[1,1024]{1,0:T(1,128)}, u32[]{:S(2)}) copy-start(f32[1,1024]{1,0:T(1,128)} %param.22) | copy-start | bytes 12292
  8.5 17.8 %collective-permute-start.2 = (bf16[64,1024]{1,0:T(8,128)(2,1)S(1)}, bf16[64,1024]{1,0:T(8,128)(2,1)}, u32[]{:S(2)}, u32[]{:S(2)}) collective-permute-start(bf16[64,1024]{1,0:T(8,128)(2,1)S(1)} %bitcast.57), channel_id=1, source_target_pairs={{0,12},{1,13},{2,14},{3,15},{4,8},{5,9},{6,10},{7,11},{8,4},{9,5},... | collective-permute-start | bytes 393224 | tf_op jit(solution)/shard_map/ppermute | solution.py:258
  11.9 24.0 %collective-permute-start.1 = (bf16[768,128]{1,0:T(8,128)(2,1)S(1)}, bf16[768,128]{1,0:T(8,128)(2,1)}, u32[]{:S(2)}, u32[]{:S(2)}) collective-permute-start(bf16[768,128]{1,0:T(8,128)(2,1)S(1)} %bitcast.42), channel_id=1, source_target_pairs={{0,12},{1,13},{2,14},{3,15},{4,8},{5,9},{6,10},{7,11},{8,4},{9,5},... | collective-permute-start | bytes 589832 | tf_op jit(solution)/shard_map/ppermute | solution.py:258
  14.6 9.7 %copy-start.24 = (f32[1,16]{1,0:T(1,128)S(1)}, f32[1,16]{1,0:T(1,128)}, u32[]{:S(2)}) copy-start(f32[1,16]{1,0:T(1,128)} %param.24) | copy-start | bytes 196
  16.1 19.8 %collective-permute-start = (bf16[1024,256]{1,0:T(8,128)(2,1)S(1)}, bf16[1024,256]{1,0:T(8,128)(2,1)S(1)}, u32[]{:S(2)}, u32[]{:S(2)}) collective-permute-start(bf16[1024,256]{1,0:T(8,128)(2,1)S(1)} %pad_maximum_fusion.own_ref), channel_id=1, source_target_pairs={{0,12},{1,13},{2,14},{3,15},{4,8},{5,9},{6,10},{7,11},{8,4},{9,5},... | collective-permute-start | bytes 1572872 | tf_op jit(solution)/shard_map/ppermute | solution.py:258
  27.3 1.3 copy-start.3
  34.6 1.4 copy-start
  35.9 6.7 %copy-start.4 = (bf16[1024,256]{1,0:T(8,128)(2,1)}, bf16[1024,256]{1,0:T(8,128)(2,1)S(1)}, u32[]{:S(2)}) copy-start(bf16[1024,256]{1,0:T(8,128)(2,1)S(1)} %collective-permute-done.other_ref) | copy-start | bytes 1572868
  35.9 29.9 %all-to-all-start.1 = ((bf16[8,128,1024]{2,1,0:T(8,128)(2,1)}), bf16[8,128,1024]{2,1,0:T(8,128)(2,1)S(1)}, u32[]{:S(2)}, u32[]{:S(2)}) async-start(bf16[8,128,1024]{2,1,0:T(8,128)(2,1)} %copy-done.3), calls=%async_computation.1 | async-start | bytes 4194304 | tf_op jit(solution)/shard_map/all_to_all | solution.py:319
  39.6 1.6 %copy-start.1 = (bf16[8,128,1024]{2,1,0:T(8,128)(2,1)S(1)}, bf16[8,128,1024]{2,1,0:T(8,128)(2,1)}, u32[]{:S(2)}) copy-start(bf16[8,128,1024]{2,1,0:T(8,128)(2,1)} %copy-done) | copy-start | bytes 6291460
  41.2 5.0 %copy-start.10 = (s32[1,2,2048]{2,1,0:T(2,128)S(1)}, s32[1,2,2048]{2,1,0:T(2,128)}, u32[]{:S(2)}) copy-start(s32[1,2,2048]{2,1,0:T(2,128)} %param.26) | copy-start | bytes 49156
  41.2 5.0 %copy-start.11 = (s32[1,2,2048]{2,1,0:T(2,128)S(1)}, s32[1,2,2048]{2,1,0:T(2,128)}, u32[]{:S(2)}) copy-start(s32[1,2,2048]{2,1,0:T(2,128)} %param.27) | copy-start | bytes 49156
  41.2 5.0 %copy-start.12 = (s32[1,2,2048]{2,1,0:T(2,128)S(1)}, s32[1,2,2048]{2,1,0:T(2,128)}, u32[]{:S(2)}) copy-start(s32[1,2,2048]{2,1,0:T(2,128)} %param.28) | copy-start | bytes 49156
  41.2 5.0 %copy-start.19 = (s32[1,768]{1,0:T(1,128)S(1)}, s32[1,768]{1,0:T(1,128)}, u32[]{:S(2)}) copy-start(s32[1,768]{1,0:T(1,128)} %cpos_ref.3) | copy-start | bytes 9220
  41.2 5.0 %copy-start.20 = (s32[1,768]{1,0:T(1,128)S(1)}, s32[1,768]{1,0:T(1,128)}, u32[]{:S(2)}) copy-start(s32[1,768]{1,0:T(1,128)} %cbkt_ref.3) | copy-start | bytes 9220
  41.2 5.0 %copy-start.21 = (s32[1,768]{1,0:T(1,128)S(1)}, s32[1,768]{1,0:T(1,128)}, u32[]{:S(2)}) copy-start(s32[1,768]{1,0:T(1,128)} %citm_ref.3) | copy-start | bytes 9220
  42.7 15.5 %collective-permute-start.3 = (bf16[2,1024,128]{2,1,0:T(8,128)(2,1)S(1)}, bf16[2,1024,128]{2,1,0:T(8,128)(2,1)S(1)}, u32[]{:S(2)}, u32[]{:S(2)}) collective-permute-start(bf16[2,1024,128]{2,1,0:T(8,128)(2,1)S(1)} %get-tuple-element.37.kv_ref), channel_id=1, source_target_pairs={{0,12},{1,13},{2,14},{3,15},{4,8},{5,9},{6,10},{7,11},{8,4},{9,5},... | collective-permute-start | bytes 1572872 | tf_op jit(solution)/shard_map/ppermute | solution.py:258
  52.0 27.6 %copy-start.7 = (bf16[1,128,1024]{2,1,0:T(8,128)(2,1)S(1)}, bf16[1,128,1024]{2,1,0:T(8,128)(2,1)}, u32[]{:S(2)}) copy-start(bf16[1,128,1024]{2,1,0:T(8,128)(2,1)} %param.16) | copy-start | bytes 786436
  65.8 22.8 %copy-start.18 = (f32[1,1024]{1,0:T(1,128)S(1)}, f32[1,1024]{1,0:T(1,128)}, u32[]{:S(2)}) copy-start(f32[1,1024]{1,0:T(1,128)} %gain_ref.3) | copy-start | bytes 12292
  79.6 9.0 %copy-start.13 = (bf16[128,1024]{1,0:T(8,128)(2,1)S(1)}, bf16[128,1024]{1,0:T(8,128)(2,1)}, u32[]{:S(2)}) copy-start(bf16[128,1024]{1,0:T(8,128)(2,1)} %new_ref.1) | copy-start | bytes 786436
  80.2 7.7 %collective-permute-start.4 = (bf16[128,1024]{1,0:T(8,128)(2,1)S(1)}, bf16[128,1024]{1,0:T(8,128)(2,1)S(1)}, u32[]{:S(2)}, u32[]{:S(2)}) collective-permute-start(bf16[128,1024]{1,0:T(8,128)(2,1)S(1)} %finish.1.before_ref), channel_id=1, source_target_pairs={{0,16},{16,32},{32,48},{48,64},{64,80},{80,96},{96,112},{112,128},... | collective-permute-start | bytes 786440 | tf_op jit(solution)/shard_map/ppermute | solution.py:335
  87.9 0.7 copy-start.14
  88.6 1.0 copy-start.15
  89.9 30.4 %copy-start.5 = (bf16[1024,256]{1,0:T(8,128)(2,1)S(1)}, bf16[1024,256]{1,0:T(8,128)(2,1)}, u32[]{:S(2)}) copy-start(bf16[1024,256]{1,0:T(8,128)(2,1)} %copy-done.4) | copy-start | bytes 1572868
  120.2 3.9 %copy-start.9 = (bf16[1,768,1,128]{3,1,2,0:T(8,128)(2,1)S(1)}, bf16[1,768,1,128]{3,1,2,0:T(8,128)(2,1)}, u32[]{:S(2)}) copy-start(bf16[1,768,1,128]{3,1,2,0:T(8,128)(2,1)} %param.25) | copy-start | bytes 589828
  121.7 15.2 %collective-permute-start.5 = (bf16[2,1024,128]{2,1,0:T(8,128)(2,1)S(1)}, bf16[2,1024,128]{2,1,0:T(8,128)(2,1)S(1)}, u32[]{:S(2)}, u32[]{:S(2)}) collective-permute-start(bf16[2,1024,128]{2,1,0:T(8,128)(2,1)S(1)} %get-tuple-element.45.kv_ref), channel_id=1, source_target_pairs={{0,12},{1,13},{2,14},{3,15},{4,8},{5,9},{6,10},{7,11},{8,4},{9,5},... | collective-permute-start | bytes 1572872 | tf_op jit(solution)/shard_map/ppermute | solution.py:258
